TPU v7x, 32 devices: a whole 2x2x4 slice. The times are simulated.
32 devices in a mesh: rep: 8 (over z, core), seq: 4 (over y, x).
Axes of the slice: x: 2, y: 2, z: 4, core: 2. Of those that a mesh axis runs over, the one named last changes fastest.
Arguments:
- tokens: bfloat16 [8, 2048, 1024], P('rep', 'seq'), may hold values from -6 to 6
- mixer_gain: bfloat16 [1024], P('seq'), may hold values from 0.5 to 1.5
- query_weight: bfloat16 [1024, 512], P('seq'), may hold values from -0.1875 to 0.1875
- key_weight: bfloat16 [1024, 512], P('seq'), may hold values from -0.1875 to 0.1875
- value_weight: bfloat16 [1024, 1024], P('seq'), may hold values from -0.1875 to 0.1875
- decay_down: bfloat16 [1024, 16], P('seq'), may hold values from -0.1875 to 0.1875
- decay_up: bfloat16 [16, 512], P(None, 'seq'), may hold values from -1.5 to 1.5
- decay_bias: bfloat16 [512], P('seq'), may hold values from 0 to 6
- outgate_weight: bfloat16 [1024, 1024], P('seq'), may hold values from -0.1875 to 0.1875
- head_gain: bfloat16 [256], P('seq'), may hold values from 0.5 to 1.5
- output_weight: bfloat16 [1024, 1024], P('seq'), may hold values from -0.25 to 0.25
- channel_gain: bfloat16 [1024], P('seq'), may hold values from 0.5 to 1.5
- gate_weight: bfloat16 [1024, 2816], P('seq'), may hold values from -0.1875 to 0.1875
- up_weight: bfloat16 [1024, 2816], P('seq'), may hold values from -0.1875 to 0.1875
- down_weight: bfloat16 [2816, 1024], P('seq'), may hold values from -0.21875 to 0.21875
- cotangent: bfloat16 [8, 2048, 1024], P('rep', 'seq'), may hold values from -6 to 6
Outputs:
- block_out: bfloat16 [8, 2048, 1024], P('rep', 'seq')
- tokens_grad: float32 [8, 2048, 1024], P('rep', 'seq')
- mixer_gain_grad: float32 [1024], P('seq')
- query_weight_grad: float32 [1024, 512], P('seq')
- key_weight_grad: float32 [1024, 512], P('seq')
- value_weight_grad: float32 [1024, 1024], P('seq')
- decay_down_grad: float32 [1024, 16], P('seq')
- decay_up_grad: float32 [16, 512], P(None, 'seq')
- decay_bias_grad: float32 [512], P('seq')
- outgate_weight_grad: float32 [1024, 1024], P('seq')
- head_gain_grad: float32 [256], P('seq')
- output_weight_grad: float32 [1024, 1024], P('seq')
- channel_gain_grad: float32 [1024], P('seq')
- gate_weight_grad: float32 [1024, 2816], P('seq')
- up_weight_grad: float32 [1024, 2816], P('seq')
- down_weight_grad: float32 [2816, 1024], P('seq')
All inputs are finite; a program needn't handle non-finite values.
Results may differ from a plain program's by a relative error of at most 0.018.
Values may be sent and summed in bfloat16 or wider, within the bound.
No kernel may reach another device: no remote copies, remote signals or barrier semaphores. Data moves between devices by JAX's collectives and lax.ppermute only.
A program may use at most 320 MiB of HBM per device.

v0:
```python
import jax
import jax.numpy as jnp
from jax import lax
from jax.sharding import PartitionSpec as P

HEADS = 4
DK = 128
DV = 256
SPAN = 64


epsilon = 1e-06
normalizer = 16.0
highest_precision = lax.Precision.HIGHEST


def prefix(value, axis, join, neutral):
    count, mine = (lax.axis_size(axis), lax.axis_index(axis))
    pieces = jax.tree.map(lambda part: lax.all_gather(part, axis), value)
    running = jax.tree.map(
        lambda part, zero: jnp.full_like(part, 0) + jnp.asarray(zero, part.dtype), value, neutral
    )

    def lap(position, running):
        longer = join(running, jax.tree.map(lambda part: part[position], pieces))
        return jax.tree.map(lambda new, old: jnp.where(position < mine, new, old), longer, running)

    return lax.fori_loop(0, count - 1, lap, running)


def carried_in(array, axis, join, neutral):
    count = lax.axis_size(axis)
    place = lax.axis_index(axis)
    ahead = count - 1 - place
    gathered = jax.tree.map(
        lambda a, kind: lax.all_gather(a.astype(kind), axis),
        array,
        jax.tree.map(lambda a: jnp.bfloat16 if a.dtype == jnp.float32 else a.dtype, array),
    )
    state = jax.tree.map(lambda a, e: jnp.zeros_like(a) + jnp.asarray(e, a.dtype), array, neutral)

    def one(lap, state):
        source = count - 1 - lap
        return join(
            state,
            jax.tree.map(
                lambda a, own: lax.dynamic_index_in_dim(a, source, 0, False).astype(own.dtype),
                gathered,
                array,
            ),
        )

    return lax.fori_loop(0, ahead, one, state)


def normalize(values_in):
    return values_in * lax.rsqrt(jnp.mean(values_in * values_in, axis=-1, keepdims=True) + epsilon)


def combine(earlier, later):
    return (earlier[0] * later[0], later[0][..., None] * earlier[1] + later[1])


def span_item(carried, pieces):
    stored, decayed = carried
    queries, keys_in, values_in, gates = pieces
    length = queries.shape[0]
    lower = jnp.arange(length)[:, None] >= jnp.arange(length)[None, :]
    cumul = jnp.dot(lower.astype(jnp.float32), gates, precision=highest_precision)
    finish = cumul[-1]
    inter = jnp.dot(queries * jnp.exp(cumul), stored, precision=highest_precision)
    differ = cumul[:, None, :] - cumul[None, :, :]
    pairwise = jnp.exp(jnp.where(lower[:, :, None], differ, -1e30))
    scores = jnp.einsum("ik,jk,ijk->ij", queries, keys_in, pairwise, precision=highest_precision)
    intra = jnp.dot(scores, values_in, precision=highest_precision)
    update = stored * jnp.exp(finish)[:, None] + jnp.dot(
        (keys_in * jnp.exp(finish[None, :] - cumul)).T, values_in, precision=highest_precision
    )
    return (
        (update, decayed + finish),
        (inter + intra, queries * jnp.exp(cumul + decayed[None, :])),
    )


def segment_item(pieces):
    queries, keys_in, values_in, gates = pieces
    seg_len = queries.shape[0]
    blocks = seg_len // SPAN

    def split(array):
        return array.reshape(blocks, SPAN, array.shape[-1])

    start = (jnp.zeros((DK, DV), jnp.float32), jnp.zeros((DK,), jnp.float32))
    (summary, decayed), (outputs, query_forget_factor) = lax.scan(
        jax.checkpoint(span_item),
        start,
        (split(queries), split(keys_in), split(values_in), split(gates)),
    )
    return (
        outputs.reshape(seg_len, DV),
        query_forget_factor.reshape(seg_len, DK),
        summary,
        jnp.exp(decayed),
    )


def whole_segment(queries, keys_in, values_in, gates, incoming_state):
    segment_output, query_forget_factor, summary, retain = lax.map(
        segment_item, (queries, keys_in, values_in, gates)
    )
    attention_result = segment_output + jnp.einsum(
        "ywm,ymb->ywb", query_forget_factor, incoming_state, precision=highest_precision
    )
    return (attention_result, retain[..., None] * incoming_state + summary)


def product(left, right):
    return jnp.dot(left, right, preferred_element_type=jnp.float32)


def product_left(left, right):
    return lax.dot_general(
        left, right, (((0,), (0,)), ((), ())), preferred_element_type=jnp.float32
    )


def product_right(left, right):
    return lax.dot_general(
        left, right, (((1,), (1,)), ((), ())), preferred_element_type=jnp.float32
    )


def local(
    tokens,
    mixer_gain,
    query_weight,
    key_weight,
    value_weight,
    decay_down,
    decay_up,
    decay_bias,
    outgate_weight,
    head_gain,
    output_weight,
    channel_gain,
    gate_weight,
    up_weight,
    down_weight,
    cotangent,
):
    seqs_here, seg_len, width = tokens.shape
    rows_here = seqs_here * seg_len

    def to_items(array, size):
        shaped = array.reshape(seqs_here, seg_len, HEADS, size).transpose(0, 2, 1, 3)
        return shaped.reshape(seqs_here * HEADS, seg_len, size)

    def from_items(array, size):
        shaped = array.reshape(seqs_here, HEADS, seg_len, size).transpose(0, 2, 1, 3)
        return shaped.reshape(rows_here, HEADS * size)

    mixer_full = (
        lax.all_gather(mixer_gain, "seq", axis=0, tiled=True),
        lax.all_gather(query_weight, "seq", axis=0, tiled=True),
        lax.all_gather(key_weight, "seq", axis=0, tiled=True),
        lax.all_gather(value_weight, "seq", axis=0, tiled=True),
        lax.all_gather(decay_down, "seq", axis=0, tiled=True),
        lax.all_gather(decay_up, "seq", axis=1, tiled=True),
        lax.all_gather(decay_bias, "seq", axis=0, tiled=True),
        lax.all_gather(outgate_weight, "seq", axis=0, tiled=True),
        lax.all_gather(head_gain, "seq", axis=0, tiled=True),
        lax.all_gather(output_weight, "seq", axis=0, tiled=True),
    )
    gain_one = mixer_full[0].astype(jnp.float32)
    decay_up_f = mixer_full[5].astype(jnp.float32)
    decay_bias_f = mixer_full[6].astype(jnp.float32)
    head_gain_f = mixer_full[8].astype(jnp.float32)
    inputs = tokens.reshape(rows_here, width).astype(jnp.float32)

    def first_norm(inputs_in, gain_in):
        return normalize(inputs_in) * gain_in

    normed_one = first_norm(inputs, gain_one).astype(jnp.bfloat16)
    queries = product(normed_one, mixer_full[1])
    keys_all = product(normed_one, mixer_full[2])
    values_all = product(normed_one, mixer_full[3])
    low_rank = product(normed_one, mixer_full[4])
    outgate = product(normed_one, mixer_full[7])

    def gate_fn(rank_in, up_in, bias_in):
        return (
            jax.nn.log_sigmoid(jnp.dot(rank_in, up_in, precision=highest_precision) + bias_in)
            / normalizer
        )

    gates = gate_fn(low_rank, decay_up_f, decay_bias_f)
    item_query = to_items(queries * DK ** (-0.5), DK)
    item_key = to_items(keys_all, DK)
    item_value = to_items(values_all, DV)
    item_gate = to_items(gates, DK)
    segment_output, query_forget_factor, summary, retain = lax.map(
        segment_item, (item_query, item_key, item_value, item_gate)
    )
    identity = (jnp.ones_like(retain), jnp.zeros_like(summary))
    incoming_state = prefix((retain, summary), "seq", combine, identity)[1]
    attention_result = segment_output + jnp.einsum(
        "ywm,ymb->ywb", query_forget_factor, incoming_state, precision=highest_precision
    )
    attended_rows = from_items(attention_result, DV).reshape(rows_here, HEADS, DV)

    def mix_fn(attended_in, gain_in, outgate_in):
        return (normalize(attended_in) * gain_in).reshape(rows_here, HEADS * DV) * jax.nn.silu(
            outgate_in
        )

    mixed = mix_fn(attended_rows, head_gain_f, outgate).astype(jnp.bfloat16)
    resid = inputs + product(mixed, mixer_full[9])
    ffn_full = (
        lax.all_gather(channel_gain, "seq", axis=0, tiled=True),
        lax.all_gather(gate_weight, "seq", axis=0, tiled=True),
        lax.all_gather(up_weight, "seq", axis=0, tiled=True),
        lax.all_gather(down_weight, "seq", axis=0, tiled=True),
    )
    gain_two = ffn_full[0].astype(jnp.float32)
    normed_two = first_norm(resid, gain_two).astype(jnp.bfloat16)
    gate_pre = product(normed_two, ffn_full[1])
    up_pre = product(normed_two, ffn_full[2])

    def swiglu(gate_in, up_in):
        return jax.nn.silu(gate_in) * up_in

    hidden = swiglu(gate_pre, up_pre).astype(jnp.bfloat16)
    result = resid + product(hidden, ffn_full[3])
    block_out = result.astype(jnp.bfloat16).reshape(tokens.shape)
    mixer_back = (
        lax.all_gather(mixer_gain, "seq", axis=0, tiled=True),
        lax.all_gather(query_weight, "seq", axis=0, tiled=True),
        lax.all_gather(key_weight, "seq", axis=0, tiled=True),
        lax.all_gather(value_weight, "seq", axis=0, tiled=True),
        lax.all_gather(decay_down, "seq", axis=0, tiled=True),
        lax.all_gather(decay_up, "seq", axis=1, tiled=True),
        lax.all_gather(decay_bias, "seq", axis=0, tiled=True),
        lax.all_gather(outgate_weight, "seq", axis=0, tiled=True),
        lax.all_gather(head_gain, "seq", axis=0, tiled=True),
        lax.all_gather(output_weight, "seq", axis=0, tiled=True),
    )
    ffn_back = (
        lax.all_gather(channel_gain, "seq", axis=0, tiled=True),
        lax.all_gather(gate_weight, "seq", axis=0, tiled=True),
        lax.all_gather(up_weight, "seq", axis=0, tiled=True),
        lax.all_gather(down_weight, "seq", axis=0, tiled=True),
    )
    grad_out = cotangent.reshape(rows_here, width).astype(jnp.float32)
    grad_low = grad_out.astype(jnp.bfloat16)
    down_weight_grad = product_left(hidden, grad_low)
    hidden_grad = product_right(grad_low, ffn_back[3])
    swiglu_pulled = jax.vjp(swiglu, gate_pre, up_pre)[1](hidden_grad)
    gate_grad = swiglu_pulled[0].astype(jnp.bfloat16)
    up_grad = swiglu_pulled[1].astype(jnp.bfloat16)
    gate_weight_grad = product_left(normed_two, gate_grad)
    up_weight_grad = product_left(normed_two, up_grad)
    normed_two_grad = product_right(gate_grad, ffn_back[1]) + product_right(up_grad, ffn_back[2])
    norm_pulled = jax.vjp(first_norm, resid, gain_two)[1](normed_two_grad)
    resid_grad = grad_out + norm_pulled[0]
    channel_gain_grad = norm_pulled[1]
    branch_grad = resid_grad.astype(jnp.bfloat16)
    output_weight_grad = product_left(mixed, branch_grad)
    mixed_grad = product_right(branch_grad, mixer_back[9])
    mix_pulled = jax.vjp(mix_fn, attended_rows, head_gain_f, outgate)[1](mixed_grad)
    head_gain_grad = mix_pulled[1]
    outgate_grad = mix_pulled[2].astype(jnp.bfloat16)
    attention_result_grad = to_items(mix_pulled[0].reshape(rows_here, HEADS * DV), DV)
    segment_state_grad = jnp.einsum(
        "azr,azq->arq", query_forget_factor, attention_result_grad, precision=highest_precision
    )
    later_grad = carried_in((retain, segment_state_grad), "seq", combine, identity)[1]
    segment_pulled = jax.vjp(
        whole_segment, item_query, item_key, item_value, item_gate, incoming_state
    )[1]((attention_result_grad, later_grad))
    query_grad = (from_items(segment_pulled[0], DK) * DK ** (-0.5)).astype(jnp.bfloat16)
    key_grad = from_items(segment_pulled[1], DK).astype(jnp.bfloat16)
    value_grad = from_items(segment_pulled[2], DV).astype(jnp.bfloat16)
    gates_grad = from_items(segment_pulled[3], DK)
    gate_pulled = jax.vjp(gate_fn, low_rank, decay_up_f, decay_bias_f)[1](gates_grad)
    low_rank_grad = gate_pulled[0].astype(jnp.bfloat16)
    decay_up_grad = gate_pulled[1]
    decay_bias_grad = gate_pulled[2]
    query_weight_grad = product_left(normed_one, query_grad)
    key_weight_grad = product_left(normed_one, key_grad)
    value_weight_grad = product_left(normed_one, value_grad)
    decay_down_grad = product_left(normed_one, low_rank_grad)
    outgate_weight_grad = product_left(normed_one, outgate_grad)
    normed_one_grad = (
        product_right(query_grad, mixer_back[1])
        + product_right(key_grad, mixer_back[2])
        + product_right(value_grad, mixer_back[3])
        + product_right(low_rank_grad, mixer_back[4])
        + product_right(outgate_grad, mixer_back[7])
    )
    first_pulled = jax.vjp(first_norm, inputs, gain_one)[1](normed_one_grad)
    tokens_grad = (resid_grad + first_pulled[0]).reshape(tokens.shape)
    mixer_gain_grad = first_pulled[1]
    shares = (
        lax.psum_scatter(
            mixer_gain_grad.astype(jnp.bfloat16), "seq", scatter_dimension=0, tiled=True
        ).astype(jnp.float32),
        lax.psum_scatter(
            query_weight_grad.astype(jnp.bfloat16), "seq", scatter_dimension=0, tiled=True
        ).astype(jnp.float32),
        lax.psum_scatter(
            key_weight_grad.astype(jnp.bfloat16), "seq", scatter_dimension=0, tiled=True
        ).astype(jnp.float32),
        lax.psum_scatter(
            value_weight_grad.astype(jnp.bfloat16), "seq", scatter_dimension=0, tiled=True
        ).astype(jnp.float32),
        lax.psum_scatter(
            decay_down_grad.astype(jnp.bfloat16), "seq", scatter_dimension=0, tiled=True
        ).astype(jnp.float32),
        lax.psum_scatter(
            decay_up_grad.astype(jnp.bfloat16), "seq", scatter_dimension=1, tiled=True
        ).astype(jnp.float32),
        lax.psum_scatter(
            decay_bias_grad.astype(jnp.bfloat16), "seq", scatter_dimension=0, tiled=True
        ).astype(jnp.float32),
        lax.psum_scatter(
            outgate_weight_grad.astype(jnp.bfloat16), "seq", scatter_dimension=0, tiled=True
        ).astype(jnp.float32),
        lax.psum_scatter(
            head_gain_grad.astype(jnp.bfloat16), "seq", scatter_dimension=0, tiled=True
        ).astype(jnp.float32),
        lax.psum_scatter(
            output_weight_grad.astype(jnp.bfloat16), "seq", scatter_dimension=0, tiled=True
        ).astype(jnp.float32),
        lax.psum_scatter(
            channel_gain_grad.astype(jnp.bfloat16), "seq", scatter_dimension=0, tiled=True
        ).astype(jnp.float32),
        lax.psum_scatter(
            gate_weight_grad.astype(jnp.bfloat16), "seq", scatter_dimension=0, tiled=True
        ).astype(jnp.float32),
        lax.psum_scatter(
            up_weight_grad.astype(jnp.bfloat16), "seq", scatter_dimension=0, tiled=True
        ).astype(jnp.float32),
        lax.psum_scatter(
            down_weight_grad.astype(jnp.bfloat16), "seq", scatter_dimension=0, tiled=True
        ).astype(jnp.float32),
    )
    totals = (
        lax.psum(shares[0].astype(jnp.bfloat16), "rep").astype(jnp.float32),
        lax.psum(shares[1].astype(jnp.bfloat16), "rep").astype(jnp.float32),
        lax.psum(shares[2].astype(jnp.bfloat16), "rep").astype(jnp.float32),
        lax.psum(shares[3].astype(jnp.bfloat16), "rep").astype(jnp.float32),
        lax.psum(shares[4].astype(jnp.bfloat16), "rep").astype(jnp.float32),
        lax.psum(shares[5].astype(jnp.bfloat16), "rep").astype(jnp.float32),
        lax.psum(shares[6].astype(jnp.bfloat16), "rep").astype(jnp.float32),
        lax.psum(shares[7].astype(jnp.bfloat16), "rep").astype(jnp.float32),
        lax.psum(shares[8].astype(jnp.bfloat16), "rep").astype(jnp.float32),
        lax.psum(shares[9].astype(jnp.bfloat16), "rep").astype(jnp.float32),
        lax.psum(shares[10].astype(jnp.bfloat16), "rep").astype(jnp.float32),
        lax.psum(shares[11].astype(jnp.bfloat16), "rep").astype(jnp.float32),
        lax.psum(shares[12].astype(jnp.bfloat16), "rep").astype(jnp.float32),
        lax.psum(shares[13].astype(jnp.bfloat16), "rep").astype(jnp.float32),
    )
    return (
        block_out,
        tokens_grad,
        totals[0],
        totals[1],
        totals[2],
        totals[3],
        totals[4],
        totals[5],
        totals[6],
        totals[7],
        totals[8],
        totals[9],
        totals[10],
        totals[11],
        totals[12],
        totals[13],
    )


def solution(mesh):
    in_specs = (
        P("rep", "seq", None),
        P("seq"),
        P("seq", None),
        P("seq", None),
        P("seq", None),
        P("seq", None),
        P(None, "seq"),
        P("seq"),
        P("seq", None),
        P("seq"),
        P("seq", None),
        P("seq"),
        P("seq", None),
        P("seq", None),
        P("seq", None),
        P("rep", "seq", None),
    )
    out_specs = (
        P("rep", "seq", None),
        P("rep", "seq", None),
        P("seq"),
        P("seq", None),
        P("seq", None),
        P("seq", None),
        P("seq", None),
        P(None, "seq"),
        P("seq"),
        P("seq", None),
        P("seq"),
        P("seq", None),
        P("seq"),
        P("seq", None),
        P("seq", None),
        P("seq", None),
    )
    return jax.shard_map(local, mesh=mesh, in_specs=in_specs, out_specs=out_specs, check_vma=False)
```

profile of v0, /device:TPU:0, one launch (start us, length us, event | category | flops | bytes accessed | tf_op | source)
XLA Modules:
  0.0 1744.6 jit_solution(8467272681562996415)
XLA Ops:
  73.2 32.0 %all-gather.24.cloned.1.call-done = bf16[1024,1024]{1,0:T(8,128)(2,1)} async-done(((bf16[256,1024]{1,0:T(8,128)(2,1)}), bf16[1024,1024]{1,0:T(8,128)(2,1)}) %all-gather.24.cloned.1.call-update) | async-done | bytes 2097168 | tf_op jit(solution)/shard_map/all_gather | solution.py:166
  115.2 129.6 %while.193 = (s32[]{:T(128)}, f32[4,512,256]{1,2,0:T(8,128)}, f32[4,512,128]{2,1,0:T(8,128)}, f32[4,128,256]{2,1,0:T(8,128)}, f32[4,128]{1,0:T(4,128)S(1)}, /*in...) while((s32[]{:T(128)}, f32[4,512,256]{1,2,0:T(8,128)}, ...), condition=%wide.region_4.5_spmd.clone, body=%wide.region_1.4_spmd.sunk.clone | while | flops 72020224 | bytes 10980198 | solution.py:201
  117.4 27.7 %while.192 = (s32[]{:T(128)}, f32[128,256]{1,0:T(8,128)S(1)}, f32[128]{0:T(128)S(1)}, f32[8,64,256]{2,1,0:T(8,128)S(1)}, f32[8,64,128]{2,1,0:T(8,128)S(1)}, /*in...) while((s32[]{:T(128)}, f32[128,256]{1,0:T(8,128)S(1)}, ...), condition=%wide.region_3.3_spmd.clone, body=%wide.region_2.2_spmd.clone.sunk | while | flops 72020224 | bytes 5471369 | solution.py:94
  149.8 27.7 %while.192 = (s32[]{:T(128)}, f32[128,256]{1,0:T(8,128)S(1)}, f32[128]{0:T(128)S(1)}, f32[8,64,256]{2,1,0:T(8,128)S(1)}, f32[8,64,128]{2,1,0:T(8,128)S(1)}, /*in...) while((s32[]{:T(128)}, f32[128,256]{1,0:T(8,128)S(1)}, ...), condition=%wide.region_3.3_spmd.clone, body=%wide.region_2.2_spmd.clone.sunk | while | flops 72020224 | bytes 5471369 | solution.py:94
  182.2 27.7 %while.192 = (s32[]{:T(128)}, f32[128,256]{1,0:T(8,128)S(1)}, f32[128]{0:T(128)S(1)}, f32[8,64,256]{2,1,0:T(8,128)S(1)}, f32[8,64,128]{2,1,0:T(8,128)S(1)}, /*in...) while((s32[]{:T(128)}, f32[128,256]{1,0:T(8,128)S(1)}, ...), condition=%wide.region_3.3_spmd.clone, body=%wide.region_2.2_spmd.clone.sunk | while | flops 72020224 | bytes 5471369 | solution.py:94
  214.6 27.7 %while.192 = (s32[]{:T(128)}, f32[128,256]{1,0:T(8,128)S(1)}, f32[128]{0:T(128)S(1)}, f32[8,64,256]{2,1,0:T(8,128)S(1)}, f32[8,64,128]{2,1,0:T(8,128)S(1)}, /*in...) while((s32[]{:T(128)}, f32[128,256]{1,0:T(8,128)S(1)}, ...), condition=%wide.region_3.3_spmd.clone, body=%wide.region_2.2_spmd.clone.sunk | while | flops 72020224 | bytes 5471369 | solution.py:94
  324.3 30.2 %all-gather.28.cloned.1.call-done = bf16[1024,1024]{1,0:T(8,128)(2,1)} async-done(((bf16[256,1024]{1,0:T(8,128)(2,1)}), bf16[1024,1024]{1,0:T(8,128)(2,1)}) %all-gather.28.cloned.1.call-update) | async-done | bytes 2097168 | tf_op jit(solution)/shard_map/all_gather | solution.py:172
  359.3 62.8 %all-gather.30.cloned.1.call-done = bf16[1024,2816]{1,0:T(8,128)(2,1)} async-done(((bf16[256,2816]{1,0:T(8,128)(2,1)}), bf16[1024,2816]{1,0:T(8,128)(2,1)}) %all-gather.30.cloned.1.call-update) | async-done | bytes 5767184 | tf_op jit(solution)/shard_map/all_gather | solution.py:220
  429.7 60.1 %all-gather.32.cloned.1.call-done = bf16[1024,2816]{1,0:T(8,128)(2,1)} async-done(((bf16[256,2816]{1,0:T(8,128)(2,1)}), bf16[1024,2816]{1,0:T(8,128)(2,1)}) %all-gather.32.cloned.1.call-update) | async-done | bytes 5767184 | tf_op jit(solution)/shard_map/all_gather | solution.py:221
  497.4 60.1 %all-gather.34.cloned.1.call-done = bf16[2816,1024]{1,0:T(8,128)(2,1)} async-done(((bf16[704,1024]{1,0:T(8,128)(2,1)}), bf16[2816,1024]{1,0:T(8,128)(2,1)}) %all-gather.34.cloned.1.call-update) | async-done | bytes 5767184 | tf_op jit(solution)/shard_map/all_gather | solution.py:222
  599.8 84.0 %while.198 = (s32[]{:T(128)}, f32[4,128]{1,0:T(4,128)}, f32[4,8,128,256]{3,2,1,0:T(8,128)}, f32[4,8,128]{2,1,0:T(8,128)}, f32[4,8,64,128]{3,2,1,0:T(8,128)}, /*i...) while((s32[]{:T(128)}, f32[4,128]{1,0:T(4,128)}, ...), condition=%wide.region_17.18_spmd.clone.clone, body=%wide.region_14.17_spmd.clone.sunk.clone | while | flops 31613188 | bytes 8130426 | solution.py:108
  703.4 439.7 %while.196 = (s32[]{:T(128)}, f32[4,512,128]{1,2,0:T(8,128)}, bf16[4,512,128]{1,2,0:T(8,128)(2,1)}, bf16[4,512,256]{1,2,0:T(8,128)(2,1)}, f32[4,512,128]{2,1,0:T...) while((s32[]{:T(128)}, f32[4,512,128]{1,2,0:T(8,128)}, ...), condition=%wide.region_26.27_spmd.clone, body=%wide.region_18.26_spmd.sunk.clone | while | flops 149364992 | bytes 21190920 | solution.py:108
  717.4 91.6 %while.195 = (s32[]{:T(128)}, f32[128,256]{1,0:T(8,128)S(1)}, f32[128]{0:T(128)S(1)}, f32[8,64,128]{2,1,0:T(8,128)S(1)}, bf16[8,64,128]{2,1,0:T(8,128)(2,1)}, /*...) while((s32[]{:T(128)}, f32[128,256]{1,0:T(8,128)S(1)}, ...), condition=%wide.region_25.25_spmd, body=%wide.region_19.24_spmd.sunk | while | flops 149299328 | bytes 3731657 | solution.py:94
  827.3 91.6 %while.195 = (s32[]{:T(128)}, f32[128,256]{1,0:T(8,128)S(1)}, f32[128]{0:T(128)S(1)}, f32[8,64,128]{2,1,0:T(8,128)S(1)}, bf16[8,64,128]{2,1,0:T(8,128)(2,1)}, /*...) while((s32[]{:T(128)}, f32[128,256]{1,0:T(8,128)S(1)}, ...), condition=%wide.region_25.25_spmd, body=%wide.region_19.24_spmd.sunk | while | flops 149299328 | bytes 3731657 | solution.py:94
  937.3 91.6 %while.195 = (s32[]{:T(128)}, f32[128,256]{1,0:T(8,128)S(1)}, f32[128]{0:T(128)S(1)}, f32[8,64,128]{2,1,0:T(8,128)S(1)}, bf16[8,64,128]{2,1,0:T(8,128)(2,1)}, /*...) while((s32[]{:T(128)}, f32[128,256]{1,0:T(8,128)S(1)}, ...), condition=%wide.region_25.25_spmd, body=%wide.region_19.24_spmd.sunk | while | flops 149299328 | bytes 3731657 | solution.py:94
  1047.2 91.6 %while.195 = (s32[]{:T(128)}, f32[128,256]{1,0:T(8,128)S(1)}, f32[128]{0:T(128)S(1)}, f32[8,64,128]{2,1,0:T(8,128)S(1)}, bf16[8,64,128]{2,1,0:T(8,128)(2,1)}, /*...) while((s32[]{:T(128)}, f32[128,256]{1,0:T(8,128)S(1)}, ...), condition=%wide.region_25.25_spmd, body=%wide.region_19.24_spmd.sunk | while | flops 149299328 | bytes 3731657 | solution.py:94
  1206.3 38.2 %reduce-scatter.23.cloned.1.call-done = bf16[256,1024]{1,0:T(8,128)(2,1)} async-done(((bf16[1024,1024]{1,0:T(8,128)(2,1)}), bf16[256,1024]{1,0:T(8,128)(2,1)}) %reduce-scatter.23.cloned.1.call-update) | async-done | bytes 524304 | tf_op jit(solution)/shard_map/reduce_scatter | solution.py:331
  1244.5 38.3 %reduce-scatter.21.cloned.1.call-done = bf16[256,1024]{1,0:T(8,128)(2,1)} async-done(((bf16[1024,1024]{1,0:T(8,128)(2,1)}), bf16[256,1024]{1,0:T(8,128)(2,1)}) %reduce-scatter.21.cloned.1.call-update) | async-done | bytes 524304 | tf_op jit(solution)/shard_map/reduce_scatter | solution.py:325
  1282.8 38.0 %reduce-scatter.17.cloned.1.call-done = bf16[256,1024]{1,0:T(8,128)(2,1)} async-done(((bf16[1024,1024]{1,0:T(8,128)(2,1)}), bf16[256,1024]{1,0:T(8,128)(2,1)}) %reduce-scatter.17.cloned.1.call-update) | async-done | bytes 524304 | tf_op jit(solution)/shard_map/reduce_scatter | solution.py:313
  1320.8 68.9 %reduce-scatter.25.cloned.1.call-done = bf16[256,2816]{1,0:T(8,128)(2,1)} async-done(((bf16[1024,2816]{1,0:T(8,128)(2,1)}), bf16[256,2816]{1,0:T(8,128)(2,1)}) %reduce-scatter.25.cloned.1.call-update) | async-done | bytes 1441808 | tf_op jit(solution)/shard_map/reduce_scatter | solution.py:337
  1389.8 68.9 %reduce-scatter.27.cloned.1.call-done = bf16[256,2816]{1,0:T(8,128)(2,1)} async-done(((bf16[1024,2816]{1,0:T(8,128)(2,1)}), bf16[256,2816]{1,0:T(8,128)(2,1)}) %reduce-scatter.27.cloned.1.call-update) | async-done | bytes 1441808 | tf_op jit(solution)/shard_map/reduce_scatter | solution.py:340
  1458.7 68.9 %reduce-scatter.29.cloned.1.call-done = bf16[704,1024]{1,0:T(8,128)(2,1)} async-done(((bf16[2816,1024]{1,0:T(8,128)(2,1)}), bf16[704,1024]{1,0:T(8,128)(2,1)}) %reduce-scatter.29.cloned.1.call-update) | async-done | bytes 1441808 | tf_op jit(solution)/shard_map/reduce_scatter | solution.py:343
  1580.7 29.1 %all-reduce.6 = (bf16[256]{0:T(256)(128)(2,1)S(1)}, bf16[256,16]{0,1:T(8,128)(2,1)S(1)}, bf16[16,128]{1,0:T(8,128)(2,1)S(1)}, bf16[128]{0:T(256)(128)(2,1)S(1)},...) all-reduce(bf16[256]{0:T(256)(128)(2,1)S(1)} %dynamic-slice.2, ...), channel_id=1, replica_groups=mesh['rep'=8,'seq'=4] {'rep'}, use_global_device_ids=true, to_apply=%region_30.31 | all-reduce | flops 6848 | bytes 27392 | tf_op jit(solution)/shard_map/psum | solution.py:348
  1613.2 112.0 %all-reduce.11.cloned.1.call-done = (bf16[256,512]{1,0:T(8,128)(2,1)}, bf16[256,512]{1,0:T(8,128)(2,1)}, bf16[256,1024]{1,0:T(8,128)(2,1)}, bf16[256,1024]{1,0:T...) async-done(((bf16[256,512]{1,0:T(8,128)(2,1)}, bf16[256,512]{1,0:T(8,128)(2,1)}, ...) | async-done | bytes 6422544 | tf_op jit(solution)/shard_map/psum | solution.py:349
  (1765 shorter events, 1059.3 us)
Async XLA Ops:
  7.2 37.2 %copy-start.10 = (bf16[1,512,1024]{2,1,0:T(8,128)(2,1)S(1)}, bf16[1,512,1024]{2,1,0:T(8,128)(2,1)}, u32[]{:S(2)}) copy-start(bf16[1,512,1024]{2,1,0:T(8,128)(2,1)} %param.32) | copy-start | bytes 3145732
  7.2 41.8 %all-gather.20.cloned.1.call-start = ((), (), s32[]{:S(2)}) async-start(), calls=%async_computation.10 | async-start | bytes 1310720 | tf_op jit(solution)/shard_map/all_gather | solution.py:164
  7.9 60.0 %all-gather.22.cloned.1.call-start = ((), (), s32[]{:S(2)}) async-start(), calls=%async_computation.11 | async-start | bytes 1310720 | tf_op jit(solution)/shard_map/all_gather | solution.py:165
  8.7 96.5 %all-gather.24.cloned.1.call-start = ((), (), s32[]{:S(2)}) async-start(), calls=%async_computation.12 | async-start | bytes 2621440 | tf_op jit(solution)/shard_map/all_gather | solution.py:166
  9.4 271.0 %all-gather.36.cloned.1.call-start = ((), (), s32[]{:S(2)}) async-start(), calls=%async_computation.27 | async-start | bytes 2621440 | tf_op jit(solution)/shard_map/all_gather | solution.py:19
  244.8 72.6 %all-gather.26.cloned.1.call-start = ((), (), s32[]{:S(2)}) async-start(), calls=%async_computation.13 | async-start | bytes 2621440 | tf_op jit(solution)/shard_map/all_gather | solution.py:170
  245.4 109.1 %all-gather.28.cloned.1.call-start = ((), (), s32[]{:S(2)}) async-start(), calls=%async_computation.14 | async-start | bytes 2621440 | tf_op jit(solution)/shard_map/all_gather | solution.py:172
  246.0 176.1 %all-gather.30.cloned.1.call-start = ((), (), s32[]{:S(2)}) async-start(), calls=%async_computation.15 | async-start | bytes 7208960 | tf_op jit(solution)/shard_map/all_gather | solution.py:220
  246.8 243.1 %all-gather.32.cloned.1.call-start = ((), (), s32[]{:S(2)}) async-start(), calls=%async_computation.16 | async-start | bytes 7208960 | tf_op jit(solution)/shard_map/all_gather | solution.py:221
  247.5 310.0 %all-gather.34.cloned.1.call-start = ((), (), s32[]{:S(2)}) async-start(), calls=%async_computation.17 | async-start | bytes 7208960 | tf_op jit(solution)/shard_map/all_gather | solution.py:222
  248.3 449.2 %all-gather.38.cloned.1.call-start = ((), (), s32[]{:S(2)}) async-start(), calls=%async_computation.28 | async-start | bytes 1310720 | tf_op jit(solution)/shard_map/all_gather | solution.py:36
  288.3 303.3 %copy-start.2 = (f32[4,512,256]{1,2,0:T(8,128)}, f32[4,512,256]{1,2,0:T(8,128)S(1)}, u32[]{:S(2)}) copy-start(f32[4,512,256]{1,2,0:T(8,128)S(1)} %get-tuple-element.1503) | copy-start | bytes 6291460
  359.3 130.5 %copy-start.27 = (bf16[512,1024]{1,0:T(8,128)(2,1)}, bf16[512,1024]{1,0:T(8,128)(2,1)S(1)}, u32[]{:S(2)}) copy-start(bf16[512,1024]{1,0:T(8,128)(2,1)S(1)} %multiply_convert_fusion.2) | copy-start | bytes 3145732
  599.3 600.6 %reduce-scatter.13.cloned.1.call-start = ((), (), s32[]{:S(2)}) async-start(), calls=%async_computation.18 | async-start | bytes 1310720 | tf_op jit(solution)/shard_map/reduce_scatter | solution.py:307
  1148.5 57.7 %reduce-scatter.15.cloned.1.call-start = ((), (), s32[]{:S(2)}) async-start(), calls=%async_computation.19 | async-start | bytes 1310720 | tf_op jit(solution)/shard_map/reduce_scatter | solution.py:310
  1150.6 93.9 %reduce-scatter.23.cloned.1.call-start = ((), (), s32[]{:S(2)}) async-start(), calls=%async_computation.23 | async-start | bytes 2621440 | tf_op jit(solution)/shard_map/reduce_scatter | solution.py:331
  1154.8 128.0 %reduce-scatter.21.cloned.1.call-start = ((), (), s32[]{:S(2)}) async-start(), calls=%async_computation.22 | async-start | bytes 2621440 | tf_op jit(solution)/shard_map/reduce_scatter | solution.py:325
  1158.9 162.0 %reduce-scatter.17.cloned.1.call-start = ((), (), s32[]{:S(2)}) async-start(), calls=%async_computation.20 | async-start | bytes 2621440 | tf_op jit(solution)/shard_map/reduce_scatter | solution.py:313
  1162.9 226.9 %reduce-scatter.25.cloned.1.call-start = ((), (), s32[]{:S(2)}) async-start(), calls=%async_computation.24 | async-start | bytes 7208960 | tf_op jit(solution)/shard_map/reduce_scatter | solution.py:337
  1170.9 287.8 %reduce-scatter.27.cloned.1.call-start = ((), (), s32[]{:S(2)}) async-start(), calls=%async_computation.25 | async-start | bytes 7208960 | tf_op jit(solution)/shard_map/reduce_scatter | solution.py:340
  1177.8 349.9 %reduce-scatter.29.cloned.1.call-start = ((), (), s32[]{:S(2)}) async-start(), calls=%async_computation.26 | async-start | bytes 7208960 | tf_op jit(solution)/shard_map/reduce_scatter | solution.py:343
  1185.9 370.9 %reduce-scatter.31.cloned.1.call-start = ((), (), s32[]{:S(2)}) async-start(), calls=%async_computation.29 | async-start | bytes 163840
  1194.2 386.5 %reduce-scatter.19.cloned.1.call-start = ((), (), s32[]{:S(2)}) async-start(), calls=%async_computation.21 | async-start | bytes 40960 | tf_op jit(solution)/shard_map/reduce_scatter | solution.py:316
  1195.3 529.9 %all-reduce.11.cloned.1.call-start = ((), (), s32[]{:S(2)}) async-start(), calls=%async_computation.30 | async-start | bytes 12845056 | tf_op jit(solution)/shard_map/psum | solution.py:349
  (77 other events, 317.3 us)
Sparse Core Ops, SparseCore 0:
  9.9 29.5 all-gather.19
  41.3 26.6 all-gather.21
  69.8 35.2 all-gather.23
  244.9 35.4 all-gather.35
  282.1 35.2 all-gather.25
  319.1 35.3 all-gather.27
  356.3 65.7 all-gather.29
  424.0 65.7 all-gather.31
  491.7 65.7 all-gather.33
  599.4 26.6 all-gather.37
  1148.6 26.8 reduce-scatter.12
  1178.5 27.7 reduce-scatter.14
  1209.2 35.1 reduce-scatter.22
  1247.6 35.1 reduce-scatter.20
  1285.6 35.1 reduce-scatter.16
  1324.0 65.7 reduce-scatter.24
  1392.9 65.7 reduce-scatter.26
  1461.8 65.7 reduce-scatter.28
  1531.2 23.8 reduce-scatter.30
  1558.2 22.4 reduce-scatter.18
  1583.7 141.4 all-reduce.10
where the time goes:
time: 1760 us; the launch traced here: 1740 us
  waiting for transfers between devices  756 us (43%)
  other arithmetic  325 us (18%)
  matrix products  285 us (16%)
  local copies, waits for them, and re-layouts  248 us (14%)
  blocking collectives  104 us (6%)
  between operations  18.2 us (1%)
    dot_general x96, other arithmetic, span_item(): jnp.einsum('ik,jk,ijk->ij', queries, keys_in, pairwise, precision=highest...  144 us
    psum x1, waiting for transfers between devices, local(): lax.psum(shares[1].astype(jnp.bfloat16), 'rep').astype(jnp.float32)  112 us
    squeeze x192, local copies, waits for them, and re-layouts, segment_item(): lax.scan(jax.checkpoint(span_item), start, (split(queries), split(keys_in...  79.4 us
    reduce_scatter x1, waiting for transfers between devices, local(): lax.psum_scatter(down_weight_grad.astype(jnp.bfloat16), 'seq', scatter_di...  68.9 us
    reduce_scatter x1, waiting for transfers between devices, local(): lax.psum_scatter(gate_weight_grad.astype(jnp.bfloat16), 'seq', scatter_di...  68.9 us
    reduce_scatter x1, waiting for transfers between devices, local(): lax.psum_scatter(up_weight_grad.astype(jnp.bfloat16), 'seq', scatter_dime...  68.9 us
    reduce_sum x32, other arithmetic, span_item(): differ = cumul[:, None, :] - cumul[None, :, :]  68.4 us
    all_gather x1, waiting for transfers between devices, local(): lax.all_gather(gate_weight, 'seq', axis=0, tiled=True)  62.8 us
  transfers between devices with their start and end apart: 21, of which 17 were waited for; matrix products, arithmetic and copies ran while one was open for 12% of the time, Pallas kernels for 0%

commit v1 on v0

--- a/solution.py
+++ b/solution.py
@@ -1,12 +1,17 @@
+import functools
+
 import jax
 import jax.numpy as jnp
 from jax import lax
+from jax.experimental import pallas as pl
+from jax.experimental.pallas import tpu as pltpu
 from jax.sharding import PartitionSpec as P
 
 HEADS = 4
 DK = 128
 DV = 256
-SPAN = 64
+CHUNK = 128
+SAFE = 60.0
 
 
 epsilon = 1e-06
@@ -14,104 +19,392 @@
 highest_precision = lax.Precision.HIGHEST
 
 
-def prefix(value, axis, join, neutral):
-    count, mine = (lax.axis_size(axis), lax.axis_index(axis))
-    pieces = jax.tree.map(lambda part: lax.all_gather(part, axis), value)
-    running = jax.tree.map(
-        lambda part, zero: jnp.full_like(part, 0) + jnp.asarray(zero, part.dtype), value, neutral
-    )
-
-    def lap(position, running):
-        longer = join(running, jax.tree.map(lambda part: part[position], pieces))
-        return jax.tree.map(lambda new, old: jnp.where(position < mine, new, old), longer, running)
-
-    return lax.fori_loop(0, count - 1, lap, running)
-
-
-def carried_in(array, axis, join, neutral):
-    count = lax.axis_size(axis)
-    place = lax.axis_index(axis)
-    ahead = count - 1 - place
-    gathered = jax.tree.map(
-        lambda a, kind: lax.all_gather(a.astype(kind), axis),
-        array,
-        jax.tree.map(lambda a: jnp.bfloat16 if a.dtype == jnp.float32 else a.dtype, array),
-    )
-    state = jax.tree.map(lambda a, e: jnp.zeros_like(a) + jnp.asarray(e, a.dtype), array, neutral)
-
-    def one(lap, state):
-        source = count - 1 - lap
-        return join(
-            state,
-            jax.tree.map(
-                lambda a, own: lax.dynamic_index_in_dim(a, source, 0, False).astype(own.dtype),
-                gathered,
-                array,
-            ),
-        )
-
-    return lax.fori_loop(0, ahead, one, state)
-
-
 def normalize(values_in):
     return values_in * lax.rsqrt(jnp.mean(values_in * values_in, axis=-1, keepdims=True) + epsilon)
 
 
-def combine(earlier, later):
-    return (earlier[0] * later[0], later[0][..., None] * earlier[1] + later[1])
-
-
-def span_item(carried, pieces):
-    stored, decayed = carried
-    queries, keys_in, values_in, gates = pieces
-    length = queries.shape[0]
-    lower = jnp.arange(length)[:, None] >= jnp.arange(length)[None, :]
-    cumul = jnp.dot(lower.astype(jnp.float32), gates, precision=highest_precision)
-    finish = cumul[-1]
-    inter = jnp.dot(queries * jnp.exp(cumul), stored, precision=highest_precision)
-    differ = cumul[:, None, :] - cumul[None, :, :]
-    pairwise = jnp.exp(jnp.where(lower[:, :, None], differ, -1e30))
-    scores = jnp.einsum("ik,jk,ijk->ij", queries, keys_in, pairwise, precision=highest_precision)
-    intra = jnp.dot(scores, values_in, precision=highest_precision)
-    update = stored * jnp.exp(finish)[:, None] + jnp.dot(
-        (keys_in * jnp.exp(finish[None, :] - cumul)).T, values_in, precision=highest_precision
-    )
-    return (
-        (update, decayed + finish),
-        (inter + intra, queries * jnp.exp(cumul + decayed[None, :])),
-    )
-
-
-def segment_item(pieces):
-    queries, keys_in, values_in, gates = pieces
-    seg_len = queries.shape[0]
-    blocks = seg_len // SPAN
-
-    def split(array):
-        return array.reshape(blocks, SPAN, array.shape[-1])
-
-    start = (jnp.zeros((DK, DV), jnp.float32), jnp.zeros((DK,), jnp.float32))
-    (summary, decayed), (outputs, query_forget_factor) = lax.scan(
-        jax.checkpoint(span_item),
-        start,
-        (split(queries), split(keys_in), split(values_in), split(gates)),
-    )
-    return (
-        outputs.reshape(seg_len, DV),
-        query_forget_factor.reshape(seg_len, DK),
-        summary,
-        jnp.exp(decayed),
-    )
-
-
-def whole_segment(queries, keys_in, values_in, gates, incoming_state):
-    segment_output, query_forget_factor, summary, retain = lax.map(
-        segment_item, (queries, keys_in, values_in, gates)
-    )
-    attention_result = segment_output + jnp.einsum(
-        "ywm,ymb->ywb", query_forget_factor, incoming_state, precision=highest_precision
-    )
-    return (attention_result, retain[..., None] * incoming_state + summary)
+def dot_nn(left, right):
+    return lax.dot_general(left, right, (((1,), (0,)), ((), ())), preferred_element_type=jnp.float32)
+
+
+def dot_nt(left, right):
+    return lax.dot_general(left, right, (((1,), (1,)), ((), ())), preferred_element_type=jnp.float32)
+
+
+def dot_tn(left, right):
+    return lax.dot_general(left, right, (((0,), (0,)), ((), ())), preferred_element_type=jnp.float32)
+
+
+def low(array):
+    return array.astype(jnp.bfloat16)
+
+
+def exact_sum(selector, array):
+    high = low(array)
+    rest = low(array - high.astype(jnp.float32))
+    return dot_nn(selector, high) + dot_nn(selector, rest)
+
+
+def halves(array):
+    high = low(array)
+    return high, low(array - high.astype(jnp.float32))
+
+
+def close_dot(dot, left, right):
+    (left_high, left_rest), (right_high, right_rest) = halves(left), halves(right)
+    return dot(left_high, right_high) + (dot(left_high, right_rest) + dot(left_rest, right_high))
+
+
+def positions(chunk):
+    row = lax.broadcasted_iota(jnp.int32, (chunk, chunk), 0)
+    column = lax.broadcasted_iota(jnp.int32, (chunk, chunk), 1)
+    return row, column
+
+
+def as_selector(mask):
+    return low(jnp.where(mask, 1.0, 0.0))
+
+
+def halvings(chunk):
+    sizes, half = [], chunk // 2
+    while half >= 1:
+        sizes.append(half)
+        half //= 2
+    return sizes
+
+
+def halving_parts(chunk, half):
+    row, column = positions(chunk)
+    row_late = (row & half) != 0
+    pairs = ((row & -(2 * half)) == (column & -(2 * half))) & row_late & ((column & half) == 0)
+    middle = (row & -(2 * half)) + (half - 1)
+    late = row_late & (column > middle) & (column <= row)
+    early = jnp.logical_not(row_late) & (column > row) & (column <= middle)
+    return pairs, as_selector(late | early)
+
+
+def scan_forward_kernel(chunk, q_ref, k_ref, v_ref, g_ref, o_ref, qf_ref, a_ref, st_ref, cs_ref, sum_ref, state, start, table):
+    step, steps = pl.program_id(1), pl.num_programs(1)
+
+    @pl.when(step == 0)
+    def _():
+        state[...] = jnp.zeros_like(state)
+        start[...] = jnp.zeros_like(start)
+
+    row, column = positions(chunk)
+    gates = g_ref[...]
+    cumul = exact_sum(as_selector(row >= column), gates)
+    left = exact_sum(as_selector(row < column), gates)
+    finish = cumul[chunk - 1 : chunk, :]
+    mild = jnp.min(finish) > -SAFE
+    begin = start[...]
+    cs_ref[0] = begin
+    grown = jnp.exp(cumul)
+    faded = jnp.exp(left)
+    begun = jnp.exp(begin)
+    kept = jnp.exp(finish)
+    scale = DK ** (-0.5)
+
+    @pl.when(mild)
+    def _():
+        for h in range(HEADS):
+            ks = slice(h * DK, (h + 1) * DK)
+            far = q_ref[:, ks] * scale * grown[:, ks]
+            near = k_ref[:, ks] * jnp.exp(-cumul[:, ks])
+            table[h] = jnp.where(row >= column, close_dot(dot_nt, far, near), 0.0)
+
+    @pl.when(jnp.logical_not(mild))
+    def _():
+        def one_head(h, carry):
+            ks = pl.ds(pl.multiple_of(h * DK, DK), DK)
+            queries, keys, decay = q_ref[:, ks] * scale, k_ref[:, ks], g_ref[:, ks]
+            total = jnp.where(row == column, close_dot(dot_nt, queries, keys), 0.0)
+            for half in halvings(chunk):
+                pairs, selector = halving_parts(chunk, half)
+                factor = jnp.exp(exact_sum(selector, decay))
+                total = jnp.where(pairs, close_dot(dot_nt, queries * factor, keys * factor), total)
+            table[h] = total
+            return carry
+
+        lax.fori_loop(0, HEADS, one_head, 0)
+
+    for h in range(HEADS):
+        ks, vs = slice(h * DK, (h + 1) * DK), slice(h * DV, (h + 1) * DV)
+        queries = q_ref[:, ks] * scale * grown[:, ks]
+        values = low(v_ref[:, vs])
+        held = state[h]
+        st_ref[0, h] = held
+        scores = table[h]
+        a_ref[0, h] = low(scores)
+        o_ref[:, vs] = close_dot(dot_nn, scores, v_ref[:, vs]) + dot_nt(low(queries), low(held))
+        qf_ref[:, ks] = low(queries * begun[:, ks])
+        state[h] = held * kept[:, ks] + dot_tn(values, low(k_ref[:, ks] * faded[:, ks]))
+    start[...] = begin + finish
+
+    @pl.when(step == steps - 1)
+    def _():
+        for h in range(HEADS):
+            ks = slice(h * DK, (h + 1) * DK)
+            sum_ref[0, h, :DV] = state[h]
+            sum_ref[0, h, DV:] = jnp.broadcast_to(jnp.exp(begin[:, ks] + finish[:, ks]), (8, DK))
+
+
+def scan_backward_kernel(
+    chunk, q_ref, k_ref, v_ref, g_ref, a_ref, st_ref, cs_ref, in_ref, do_ref, later_ref,
+    dq_ref, dk_ref, dv_ref, dg_ref, later, dqi, dki, dci,
+):
+    @pl.when(pl.program_id(1) == 0)
+    def _():
+        later[...] = later_ref[0]
+
+    row, column = positions(chunk)
+    lower = row >= column
+    gates = g_ref[...]
+    cumul = exact_sum(as_selector(lower), gates)
+    left = exact_sum(as_selector(row < column), gates)
+    finish = cumul[chunk - 1 : chunk, :]
+    mild = jnp.min(finish) > -SAFE
+    grown = jnp.exp(cumul)
+    faded = jnp.exp(left)
+    kept = jnp.exp(finish)
+    begun = jnp.exp(cs_ref[0])
+    scale = DK ** (-0.5)
+
+    def overlap(h, vs):
+        return close_dot(dot_nt, do_ref[:, vs], v_ref[:, vs])
+
+    @pl.when(mild)
+    def _():
+        for h in range(HEADS):
+            ks, vs = slice(h * DK, (h + 1) * DK), slice(h * DV, (h + 1) * DV)
+            shrunk = jnp.exp(-cumul[:, ks])
+            far = low(q_ref[:, ks] * scale * grown[:, ks])
+            near = low(k_ref[:, ks] * shrunk)
+            pairs = low(jnp.where(lower, overlap(h, vs), 0.0))
+            for_q, for_k = dot_nn(pairs, near), dot_tn(pairs, far)
+            dqi[:, ks] = grown[:, ks] * for_q
+            dki[:, ks] = shrunk * for_k
+            dci[:, ks] = far.astype(jnp.float32) * for_q - near.astype(jnp.float32) * for_k
+
+    @pl.when(jnp.logical_not(mild))
+    def _():
+        def one_head(h, carry):
+            ks = pl.ds(pl.multiple_of(h * DK, DK), DK)
+            vs = pl.ds(pl.multiple_of(h * DV, DV), DV)
+            queries, keys, decay = q_ref[:, ks] * scale, k_ref[:, ks], g_ref[:, ks]
+            both = overlap(h, vs)
+            pairs = low(jnp.where(row == column, both, 0.0))
+            grad_q, grad_k = dot_nn(pairs, low(keys)), dot_tn(pairs, low(queries))
+            grad_c = jnp.zeros_like(grad_q)
+            for half in halvings(chunk):
+                here, selector = halving_parts(chunk, half)
+                factor = jnp.exp(exact_sum(selector, decay))
+                far, near = low(queries * factor), low(keys * factor)
+                pairs = low(jnp.where(here, both, 0.0))
+                for_q, for_k = dot_nn(pairs, near), dot_tn(pairs, far)
+                grad_q += factor * for_q
+                grad_k += factor * for_k
+                grad_c += far.astype(jnp.float32) * for_q - near.astype(jnp.float32) * for_k
+            dqi[:, ks] = grad_q
+            dki[:, ks] = grad_k
+            dci[:, ks] = grad_c
+            return carry
+
+        lax.fori_loop(0, HEADS, one_head, 0)
+
+    before = as_selector(row > column)
+    after = as_selector(row <= column)
+    for h in range(HEADS):
+        ks, vs = slice(h * DK, (h + 1) * DK), slice(h * DV, (h + 1) * DV)
+        values, grad_out = low(v_ref[:, vs]), low(do_ref[:, vs])
+        held = st_ref[0, h] + in_ref[0, h] * begun[:, ks]
+        ahead = later[h]
+        ahead_low = low(ahead)
+        queries = q_ref[:, ks] * scale * grown[:, ks]
+        keys = k_ref[:, ks] * faded[:, ks]
+        from_state = dot_nn(grad_out, low(held))
+        from_later = dot_nn(values, ahead_low)
+        dq_ref[:, ks] = low((dqi[:, ks] + grown[:, ks] * from_state) * scale)
+        dk_ref[:, ks] = low(dki[:, ks] + faded[:, ks] * from_later)
+        dv_ref[:, vs] = low(dot_tn(a_ref[0, h], grad_out) + dot_nt(low(keys), ahead_low))
+        through = kept[:, ks] * jnp.sum(held * ahead, axis=0, keepdims=True)
+        dg_ref[:, ks] = (
+            exact_sum(after, dci[:, ks] + queries * from_state)
+            + exact_sum(before, keys * from_later)
+            + through
+        )
+        later[h] = ahead * kept[:, ks] + dot_tn(grad_out, low(queries))
+
+
+def mix_forward_kernel(o_ref, qf_ref, in_ref, og_ref, gain_ref, att_ref, mixed_ref):
+    gain = gain_ref[...]
+    for h in range(HEADS):
+        ks, vs = slice(h * DK, (h + 1) * DK), slice(h * DV, (h + 1) * DV)
+        attended = o_ref[:, vs] + dot_nt(qf_ref[:, ks], low(in_ref[0, h]))
+        att_ref[:, vs] = attended
+        outgate = og_ref[:, vs]
+        mixed_ref[:, vs] = low(normalize(attended) * gain * (outgate * jax.nn.sigmoid(outgate)))
+
+
+def mix_backward_kernel(dm_ref, att_ref, og_ref, gain_ref, qf_ref, do_ref, dog_ref, grad_ref, dgain_ref):
+    @pl.when(pl.program_id(1) == 0)
+    def _():
+        grad_ref[...] = jnp.zeros_like(grad_ref)
+        dgain_ref[...] = jnp.zeros_like(dgain_ref)
+
+    gain = gain_ref[...]
+    for h in range(HEADS):
+        ks, vs = slice(h * DK, (h + 1) * DK), slice(h * DV, (h + 1) * DV)
+        attended, outgate, grad = att_ref[:, vs], og_ref[:, vs], dm_ref[:, vs]
+        inverse = lax.rsqrt(jnp.mean(attended * attended, axis=-1, keepdims=True) + epsilon)
+        normed = attended * inverse
+        sigma = jax.nn.sigmoid(outgate)
+        gated = grad * (outgate * sigma)
+        dog_ref[:, vs] = low(grad * normed * gain * (sigma + outgate * sigma * (1.0 - sigma)))
+        dgain_ref[0] += jnp.sum(gated * normed, axis=0, keepdims=True)
+        inner = gated * gain
+        result = inverse * (inner - normed * jnp.mean(inner * normed, axis=-1, keepdims=True))
+        do_ref[:, vs] = result
+        grad_ref[0, h] += dot_tn(low(result), qf_ref[:, ks])
+
+
+def rows_spec(chunk, chunks, width, backward=False):
+    if backward:
+        return pl.BlockSpec((chunk, width), lambda s, c: (s * chunks + chunks - 1 - c, 0))
+    return pl.BlockSpec((chunk, width), lambda s, c: (s * chunks + c, 0))
+
+
+def item_spec(shape):
+    return pl.BlockSpec((1,) + shape, lambda s, c: (s,) + (0,) * len(shape))
+
+
+def chunk_spec(chunks, shape, backward=False):
+    if backward:
+        return pl.BlockSpec((1,) + shape, lambda s, c: (s * chunks + chunks - 1 - c,) + (0,) * len(shape))
+    return pl.BlockSpec((1,) + shape, lambda s, c: (s * chunks + c,) + (0,) * len(shape))
+
+
+def shaped(shape, kind=jnp.float32):
+    return jax.ShapeDtypeStruct(shape, kind)
+
+
+KEYS, VALUES = HEADS * DK, HEADS * DV
+ROOM = pltpu.CompilerParams(vmem_limit_bytes=40 * 1024 * 1024)
+
+
+def scan_forward(queries, keys, values, gates, seqs, chunk):
+    rows = queries.shape[0]
+    chunks = rows // seqs // chunk
+    keyed, valued = rows_spec(chunk, chunks, KEYS), rows_spec(chunk, chunks, VALUES)
+    return pl.pallas_call(
+        functools.partial(scan_forward_kernel, chunk),
+        grid=(seqs, chunks),
+        in_specs=[keyed, keyed, valued, keyed],
+        out_specs=[
+            valued,
+            keyed,
+            chunk_spec(chunks, (HEADS, chunk, chunk)),
+            chunk_spec(chunks, (HEADS, DV, DK)),
+            chunk_spec(chunks, (1, KEYS)),
+            item_spec((HEADS, DV + 8, DK)),
+        ],
+        out_shape=[
+            shaped((rows, VALUES)),
+            shaped((rows, KEYS), jnp.bfloat16),
+            shaped((seqs * chunks, HEADS, chunk, chunk), jnp.bfloat16),
+            shaped((seqs * chunks, HEADS, DV, DK)),
+            shaped((seqs * chunks, 1, KEYS)),
+            shaped((seqs, HEADS, DV + 8, DK)),
+        ],
+        scratch_shapes=[
+            pltpu.VMEM((HEADS, DV, DK), jnp.float32),
+            pltpu.VMEM((1, KEYS), jnp.float32),
+            pltpu.VMEM((HEADS, chunk, chunk), jnp.float32),
+        ],
+        compiler_params=ROOM,
+        name="scan_forward",
+    )(queries, keys, values, gates)
+
+
+def scan_backward(queries, keys, values, gates, scores, states, starts, incoming, grad_out, later, seqs, chunk):
+    rows = queries.shape[0]
+    chunks = rows // seqs // chunk
+    keyed, valued = rows_spec(chunk, chunks, KEYS, True), rows_spec(chunk, chunks, VALUES, True)
+    return pl.pallas_call(
+        functools.partial(scan_backward_kernel, chunk),
+        grid=(seqs, chunks),
+        in_specs=[
+            keyed, keyed, valued, keyed,
+            chunk_spec(chunks, (HEADS, chunk, chunk), True),
+            chunk_spec(chunks, (HEADS, DV, DK), True),
+            chunk_spec(chunks, (1, KEYS), True),
+            item_spec((HEADS, DV, DK)),
+            valued,
+            item_spec((HEADS, DV, DK)),
+        ],
+        out_specs=[keyed, keyed, valued, keyed],
+        out_shape=[
+            shaped((rows, KEYS), jnp.bfloat16),
+            shaped((rows, KEYS), jnp.bfloat16),
+            shaped((rows, VALUES), jnp.bfloat16),
+            shaped((rows, KEYS)),
+        ],
+        scratch_shapes=[pltpu.VMEM((HEADS, DV, DK), jnp.float32)] + [pltpu.VMEM((chunk, KEYS), jnp.float32)] * 3,
+        compiler_params=ROOM,
+        name="scan_backward",
+    )(queries, keys, values, gates, scores, states, starts, incoming, grad_out, later)
+
+
+def mix_forward(local_out, forget, incoming, outgate, gain, seqs, chunk):
+    rows = local_out.shape[0]
+    chunks = rows // seqs // chunk
+    keyed, valued = rows_spec(chunk, chunks, KEYS), rows_spec(chunk, chunks, VALUES)
+    whole_gain = pl.BlockSpec((1, DV), lambda s, c: (0, 0))
+    return pl.pallas_call(
+        mix_forward_kernel,
+        grid=(seqs, chunks),
+        in_specs=[valued, keyed, item_spec((HEADS, DV, DK)), valued, whole_gain],
+        out_specs=[valued, valued],
+        out_shape=[shaped((rows, VALUES)), shaped((rows, VALUES), jnp.bfloat16)],
+        compiler_params=ROOM,
+        name="mix_forward",
+    )(local_out, forget, incoming, outgate, gain)
+
+
+def mix_backward(mixed_grad, attended, outgate, gain, forget, seqs, chunk):
+    rows = attended.shape[0]
+    chunks = rows // seqs // chunk
+    keyed, valued = rows_spec(chunk, chunks, KEYS), rows_spec(chunk, chunks, VALUES)
+    whole_gain = pl.BlockSpec((1, DV), lambda s, c: (0, 0))
+    return pl.pallas_call(
+        mix_backward_kernel,
+        grid=(seqs, chunks),
+        in_specs=[valued, valued, valued, whole_gain, keyed],
+        out_specs=[valued, valued, item_spec((HEADS, DV, DK)), item_spec((1, DV))],
+        out_shape=[
+            shaped((rows, VALUES)),
+            shaped((rows, VALUES), jnp.bfloat16),
+            shaped((seqs, HEADS, DV, DK)),
+            shaped((seqs, 1, DV)),
+        ],
+        compiler_params=ROOM,
+        name="mix_backward",
+    )(mixed_grad, attended, outgate, gain, forget)
+
+
+def from_neighbours(summary, step):
+    count = lax.axis_size("seq")
+    total, factor = None, None
+    for distance in range(1, count):
+        shift = step * distance
+        pairs = [(i, i + shift) for i in range(count) if 0 <= i + shift < count]
+        came = lax.ppermute(summary, "seq", pairs)
+        state, retain = came[:, :, :DV].astype(jnp.float32), came[:, :, DV : DV + 1].astype(jnp.float32)
+        if total is None:
+            total, factor = state, retain
+        else:
+            total, factor = total + factor * state, factor * retain
+    return total
 
 
 def product(left, right):
@@ -151,14 +444,6 @@
     seqs_here, seg_len, width = tokens.shape
     rows_here = seqs_here * seg_len
 
-    def to_items(array, size):
-        shaped = array.reshape(seqs_here, seg_len, HEADS, size).transpose(0, 2, 1, 3)
-        return shaped.reshape(seqs_here * HEADS, seg_len, size)
-
-    def from_items(array, size):
-        shaped = array.reshape(seqs_here, HEADS, seg_len, size).transpose(0, 2, 1, 3)
-        return shaped.reshape(rows_here, HEADS * size)
-
     mixer_full = (
         lax.all_gather(mixer_gain, "seq", axis=0, tiled=True),
         lax.all_gather(query_weight, "seq", axis=0, tiled=True),
@@ -194,26 +479,14 @@
         )
 
     gates = gate_fn(low_rank, decay_up_f, decay_bias_f)
-    item_query = to_items(queries * DK ** (-0.5), DK)
-    item_key = to_items(keys_all, DK)
-    item_value = to_items(values_all, DV)
-    item_gate = to_items(gates, DK)
-    segment_output, query_forget_factor, summary, retain = lax.map(
-        segment_item, (item_query, item_key, item_value, item_gate)
-    )
-    identity = (jnp.ones_like(retain), jnp.zeros_like(summary))
-    incoming_state = prefix((retain, summary), "seq", combine, identity)[1]
-    attention_result = segment_output + jnp.einsum(
-        "ywm,ymb->ywb", query_forget_factor, incoming_state, precision=highest_precision
-    )
-    attended_rows = from_items(attention_result, DV).reshape(rows_here, HEADS, DV)
-
-    def mix_fn(attended_in, gain_in, outgate_in):
-        return (normalize(attended_in) * gain_in).reshape(rows_here, HEADS * DV) * jax.nn.silu(
-            outgate_in
-        )
-
-    mixed = mix_fn(attended_rows, head_gain_f, outgate).astype(jnp.bfloat16)
+    chunk = min(CHUNK, seg_len)
+    local_out, forget, scores, states, starts, summary = scan_forward(
+        queries, keys_all, values_all, gates, seqs_here, chunk
+    )
+    incoming_state = from_neighbours(summary, 1)
+    attended, mixed = mix_forward(
+        local_out, forget, incoming_state, outgate, head_gain_f[None, :], seqs_here, chunk
+    )
     resid = inputs + product(mixed, mixer_full[9])
     ffn_full = (
         lax.all_gather(channel_gain, "seq", axis=0, tiled=True),
@@ -266,21 +539,17 @@
     branch_grad = resid_grad.astype(jnp.bfloat16)
     output_weight_grad = product_left(mixed, branch_grad)
     mixed_grad = product_right(branch_grad, mixer_back[9])
-    mix_pulled = jax.vjp(mix_fn, attended_rows, head_gain_f, outgate)[1](mixed_grad)
-    head_gain_grad = mix_pulled[1]
-    outgate_grad = mix_pulled[2].astype(jnp.bfloat16)
-    attention_result_grad = to_items(mix_pulled[0].reshape(rows_here, HEADS * DV), DV)
-    segment_state_grad = jnp.einsum(
-        "azr,azq->arq", query_forget_factor, attention_result_grad, precision=highest_precision
-    )
-    later_grad = carried_in((retain, segment_state_grad), "seq", combine, identity)[1]
-    segment_pulled = jax.vjp(
-        whole_segment, item_query, item_key, item_value, item_gate, incoming_state
-    )[1]((attention_result_grad, later_grad))
-    query_grad = (from_items(segment_pulled[0], DK) * DK ** (-0.5)).astype(jnp.bfloat16)
-    key_grad = from_items(segment_pulled[1], DK).astype(jnp.bfloat16)
-    value_grad = from_items(segment_pulled[2], DV).astype(jnp.bfloat16)
-    gates_grad = from_items(segment_pulled[3], DK)
+    attended_grad, outgate_grad, state_grad, head_gain_grad = mix_backward(
+        mixed_grad, attended, outgate, head_gain_f[None, :], forget, seqs_here, chunk
+    )
+    head_gain_grad = head_gain_grad.sum((0, 1))
+    later_grad = from_neighbours(
+        jnp.concatenate([state_grad, summary[:, :, DV:]], axis=2).astype(jnp.bfloat16), -1
+    )
+    query_grad, key_grad, value_grad, gates_grad = scan_backward(
+        queries, keys_all, values_all, gates, scores, states, starts, incoming_state,
+        attended_grad, later_grad, seqs_here, chunk,
+    )
     gate_pulled = jax.vjp(gate_fn, low_rank, decay_up_f, decay_bias_f)[1](gates_grad)
     low_rank_grad = gate_pulled[0].astype(jnp.bfloat16)
     decay_up_grad = gate_pulled[1]

time: 1760 us -> 1070 us (0.61)
  other arithmetic: 325 us -> 26.9 us
  local copies, waits for them, and re-layouts: 248 us -> 18.8 us
  matrix products: 285 us -> 120 us
  waiting for transfers between devices: 756 us -> 734 us
  Pallas kernels: 0 us -> 21 us
    dot_general x451 -> x0, matrix products: 163 us -> none  [the longest x96 42.4 us: span_item(): intra = jnp.dot(scores, values_in, precision=highest_precision)]
    dot_general x96 -> x0, other arithmetic: 144 us -> none  [span_item(): jnp.einsum('ik,jk,ijk->ij', queries, keys_in, pairwise, precision=highest...]
    squeeze x312 -> x0, local copies, waits for them, and re-layouts: 114 us -> none  [the longest x192 79.4 us: segment_item(): lax.scan(jax.checkpoint(span_item), start, (split(queries), split(keys_in...]
    reduce_sum x67 -> x0, other arithmetic: 74.1 us -> none  [the longest x32 68.4 us: span_item(): differ = cumul[:, None, :] - cumul[None, :, :]]
    dynamic_update_slice x104 -> x0, local copies, waits for them, and re-layouts: 53.9 us -> none  [the longest x52 31.5 us: local(): lax.map(segment_item, (item_query, item_key, item_value, item_gate))]
    dynamic_update_slice x96 -> x0, other arithmetic: 42.2 us -> none  [segment_item(): lax.scan(jax.checkpoint(span_item), start, (split(queries), split(keys_in...]
    dynamic_slice x40 -> x0, local copies, waits for them, and re-layouts: 35.6 us -> none  [local(): lax.map(segment_item, (item_query, item_key, item_value, item_gate))]
    all_gather x1, waiting for transfers between devices: 24.7 us -> 0.02 us  [local(): lax.all_gather(outgate_weight, 'seq', axis=0, tiled=True)]
  transfers between devices with their start and end apart: 21 -> 25, of which waited for: 17 -> 18; matrix products, arithmetic and copies ran while one was open for 12% -> 11% of each run, Pallas kernels for 0% -> 1%
where the time goes in v1:
time: 1070 us; the launch traced here: 1060 us
  waiting for transfers between devices  734 us (69%)
  matrix products  120 us (11%)
  blocking collectives  102 us (10%)
  other arithmetic  26.9 us (3%)
  Pallas kernels  21 us (2%)
  local copies, waits for them, and re-layouts  18.8 us (2%)
  starting transfers between devices  18 us (2%)
  between operations  17.7 us (2%)
    psum x1, waiting for transfers between devices, local(): lax.psum(shares[1].astype(jnp.bfloat16), 'rep').astype(jnp.float32)  112 us
    reduce_scatter x1, waiting for transfers between devices, local(): lax.psum_scatter(down_weight_grad.astype(jnp.bfloat16), 'seq', scatter_di...  69 us
    reduce_scatter x1, waiting for transfers between devices, local(): lax.psum_scatter(gate_weight_grad.astype(jnp.bfloat16), 'seq', scatter_di...  68.9 us
    reduce_scatter x1, waiting for transfers between devices, local(): lax.psum_scatter(up_weight_grad.astype(jnp.bfloat16), 'seq', scatter_dime...  68.9 us
    all_gather x1, waiting for transfers between devices, local(): lax.all_gather(up_weight, 'seq', axis=0, tiled=True)  61.5 us
    all_gather x1, waiting for transfers between devices, local(): lax.all_gather(gate_weight, 'seq', axis=0, tiled=True)  59.1 us
    all_gather x1, waiting for transfers between devices, local(): lax.all_gather(down_weight, 'seq', axis=0, tiled=True)  59.1 us
    dot_general x9, matrix products, product_left(): lax.dot_general(left, right, (((0,), (0,)), ((), ())), preferred_element_...  41.5 us
  transfers between devices with their start and end apart: 25, of which 18 were waited for; matrix products, arithmetic and copies ran while one was open for 11% of the time, Pallas kernels for 1%

profile of v1, /device:TPU:0, one launch (start us, length us, event | category | flops | bytes accessed | tf_op | source)
XLA Modules:
  0.0 1058.3 jit_solution(9583011191040586222)
XLA Ops:
  12.8 9.4 all-gather.1
  37.3 8.2 all_gather.55
  50.9 17.1 %all-gather.12.cloned.1.call-done = bf16[1024,512]{1,0:T(8,128)(2,1)} async-done(((bf16[256,512]{1,0:T(8,128)(2,1)}), bf16[1024,512]{1,0:T(8,128)(2,1)}) %all-gather.12.cloned.1.call-update) | async-done | bytes 1048592 | tf_op jit(solution)/shard_map/all_gather | solution.py:449
  70.3 34.9 %all-gather.16.cloned.1.call-done = bf16[1024,1024]{1,0:T(8,128)(2,1)} async-done(((bf16[256,1024]{1,0:T(8,128)(2,1)}), bf16[1024,1024]{1,0:T(8,128)(2,1)}) %all-gather.16.cloned.1.call-update) | async-done | bytes 2097168 | tf_op jit(solution)/shard_map/all_gather | solution.py:451
  127.8 24.2 %all-reduce = bf16[256]{0:T(256)(128)(2,1)S(1)} all-reduce(bf16[256]{0:T(256)(128)(2,1)S(1)} %dynamic-update-slice), channel_id=1, replica_groups=mesh['rep'=8,'seq'=4] {'seq'}, use_global_device_ids=true, to_apply=%add | all-reduce | flops 256 | bytes 1024
  182.5 15.8 %all-gather.20.cloned.1.call-done = bf16[1024,1024]{1,0:T(8,128)(2,1)} async-done(((bf16[256,1024]{1,0:T(8,128)(2,1)}), bf16[1024,1024]{1,0:T(8,128)(2,1)}) %all-gather.20.cloned.1.call-update) | async-done | bytes 2097168 | tf_op jit(solution)/shard_map/all_gather | solution.py:457
  204.3 61.5 %all-gather.24.cloned.1.call-done = bf16[1024,2816]{1,0:T(8,128)(2,1)} async-done(((bf16[256,2816]{1,0:T(8,128)(2,1)}), bf16[1024,2816]{1,0:T(8,128)(2,1)}) %all-gather.24.cloned.1.call-update) | async-done | bytes 5767184 | tf_op jit(solution)/shard_map/all_gather | solution.py:494
  265.8 8.6 fusion.51
  274.4 59.1 %all-gather.22.cloned.1.call-done = bf16[1024,2816]{1,0:T(8,128)(2,1)} async-done(((bf16[256,2816]{1,0:T(8,128)(2,1)}), bf16[1024,2816]{1,0:T(8,128)(2,1)}) %all-gather.22.cloned.1.call-update) | async-done | bytes 5767184 | tf_op jit(solution)/shard_map/all_gather | solution.py:493
  333.5 8.6 fusion.50
  342.1 59.1 %all-gather.26.cloned.1.call-done = bf16[2816,1024]{1,0:T(8,128)(2,1)} async-done(((bf16[704,1024]{1,0:T(8,128)(2,1)}), bf16[2816,1024]{1,0:T(8,128)(2,1)}) %all-gather.26.cloned.1.call-update) | async-done | bytes 5767184 | tf_op jit(solution)/shard_map/all_gather | solution.py:495
  401.2 11.3 %multiply_convert_fusion = (bf16[512,2816]{1,0:T(8,128)(2,1)S(1)}, bf16[512,2816]{1,0:T(8,128)(2,1)S(1)}, bf16[512,2816]{1,0:T(8,128)(2,1)}) fusion(f32[512,2816]{1,0:T(8,128)} %fusion.50, f32[512,2816]{1,0:T(8,128)} %fusion.51, bf16[2816,1024]{1,0:T(8,128)(2,1)} %all-gather.26.cloned.1.call-done, bf16[1,512,1024]{2,1,0:T(8,128)(2,1)} %param.31), kind=kOutput, calls=%fused_computation.4 | convolution fusion | flops 2975858688 | bytes 27000832 | tf_op jit(solution)/shard_map/dot_general | solution.py:421
  447.2 10.6 scan_backward.1
  518.4 38.2 %reduce-scatter.21.cloned.1.call-done = bf16[256,1024]{1,0:T(8,128)(2,1)} async-done(((bf16[1024,1024]{1,0:T(8,128)(2,1)}), bf16[256,1024]{1,0:T(8,128)(2,1)}) %reduce-scatter.21.cloned.1.call-update) | async-done | bytes 524304 | tf_op jit(solution)/shard_map/reduce_scatter | solution.py:594
  556.6 38.3 %reduce-scatter.23.cloned.1.call-done = bf16[256,1024]{1,0:T(8,128)(2,1)} async-done(((bf16[1024,1024]{1,0:T(8,128)(2,1)}), bf16[256,1024]{1,0:T(8,128)(2,1)}) %reduce-scatter.23.cloned.1.call-update) | async-done | bytes 524304 | tf_op jit(solution)/shard_map/reduce_scatter | solution.py:600
  595.0 38.2 %reduce-scatter.17.cloned.1.call-done = bf16[256,1024]{1,0:T(8,128)(2,1)} async-done(((bf16[1024,1024]{1,0:T(8,128)(2,1)}), bf16[256,1024]{1,0:T(8,128)(2,1)}) %reduce-scatter.17.cloned.1.call-update) | async-done | bytes 524304 | tf_op jit(solution)/shard_map/reduce_scatter | solution.py:582
  633.2 69.0 %reduce-scatter.29.cloned.1.call-done = bf16[704,1024]{1,0:T(8,128)(2,1)} async-done(((bf16[2816,1024]{1,0:T(8,128)(2,1)}), bf16[704,1024]{1,0:T(8,128)(2,1)}) %reduce-scatter.29.cloned.1.call-update) | async-done | bytes 1441808 | tf_op jit(solution)/shard_map/reduce_scatter | solution.py:612
  702.1 68.9 %reduce-scatter.27.cloned.1.call-done = bf16[256,2816]{1,0:T(8,128)(2,1)} async-done(((bf16[1024,2816]{1,0:T(8,128)(2,1)}), bf16[256,2816]{1,0:T(8,128)(2,1)}) %reduce-scatter.27.cloned.1.call-update) | async-done | bytes 1441808 | tf_op jit(solution)/shard_map/reduce_scatter | solution.py:609
  771.1 68.9 %reduce-scatter.25.cloned.1.call-done = bf16[256,2816]{1,0:T(8,128)(2,1)} async-done(((bf16[1024,2816]{1,0:T(8,128)(2,1)}), bf16[256,2816]{1,0:T(8,128)(2,1)}) %reduce-scatter.25.cloned.1.call-update) | async-done | bytes 1441808 | tf_op jit(solution)/shard_map/reduce_scatter | solution.py:606
  840.0 8.3 fusion.13
  855.2 9.0 all-reduce.7
  868.8 24.1 %reduce-scatter.19.cloned.1.call-done = bf16[256,16]{0,1:T(8,128)(2,1)} async-done(((bf16[1024,16]{0,1:T(8,128)(2,1)}), bf16[256,16]{0,1:T(8,128)(2,1)}) %reduce-scatter.19.cloned.1.call-update) | async-done | bytes 8208 | tf_op jit(solution)/shard_map/reduce_scatter | solution.py:585
  892.9 29.2 %all-reduce.5 = (bf16[256]{0:T(256)(128)(2,1)S(1)}, bf16[256,16]{0,1:T(8,128)(2,1)S(1)}, bf16[16,128]{1,0:T(8,128)(2,1)S(1)}, bf16[128]{0:T(256)(128)(2,1)S(1)},...) all-reduce(bf16[256]{0:T(256)(128)(2,1)S(1)} %dynamic-slice.2, ...), channel_id=1, replica_groups=mesh['rep'=8,'seq'=4] {'rep'}, use_global_device_ids=true, to_apply=%region_6.7 | all-reduce | flops 6848 | bytes 27392 | tf_op jit(solution)/shard_map/psum | solution.py:617
  925.4 111.9 %all-reduce.10.cloned.1.call-done = (bf16[256,512]{1,0:T(8,128)(2,1)}, bf16[256,512]{1,0:T(8,128)(2,1)}, bf16[256,1024]{1,0:T(8,128)(2,1)}, bf16[256,1024]{1,0:T...) async-done(((bf16[256,512]{1,0:T(8,128)(2,1)}, bf16[256,512]{1,0:T(8,128)(2,1)}, ...) | async-done | bytes 6422544 | tf_op jit(solution)/shard_map/psum | solution.py:618
  (241 shorter events, 208.1 us)
Async XLA Ops:
  7.2 41.3 %all-gather.14.cloned.1.call-start = ((), (), s32[]{:S(2)}) async-start(), calls=%async_computation.11 | async-start | bytes 1310720 | tf_op jit(solution)/shard_map/all_gather | solution.py:450
  7.9 60.1 %all-gather.12.cloned.1.call-start = ((), (), s32[]{:S(2)}) async-start(), calls=%async_computation.10 | async-start | bytes 1310720 | tf_op jit(solution)/shard_map/all_gather | solution.py:449
  8.7 96.5 %all-gather.16.cloned.1.call-start = ((), (), s32[]{:S(2)}) async-start(), calls=%async_computation.12 | async-start | bytes 2621440 | tf_op jit(solution)/shard_map/all_gather | solution.py:451
  9.4 155.6 %all-gather.18.cloned.1.call-start = ((), (), s32[]{:S(2)}) async-start(), calls=%async_computation.13 | async-start | bytes 2621440 | tf_op jit(solution)/shard_map/all_gather | solution.py:455
  10.0 188.3 %all-gather.20.cloned.1.call-start = ((), (), s32[]{:S(2)}) async-start(), calls=%async_computation.14 | async-start | bytes 2621440 | tf_op jit(solution)/shard_map/all_gather | solution.py:457
  10.6 255.2 %all-gather.24.cloned.1.call-start = ((), (), s32[]{:S(2)}) async-start(), calls=%async_computation.16 | async-start | bytes 7208960 | tf_op jit(solution)/shard_map/all_gather | solution.py:494
  11.2 322.3 %all-gather.22.cloned.1.call-start = ((), (), s32[]{:S(2)}) async-start(), calls=%async_computation.15 | async-start | bytes 7208960 | tf_op jit(solution)/shard_map/all_gather | solution.py:493
  11.9 389.2 %all-gather.26.cloned.1.call-start = ((), (), s32[]{:S(2)}) async-start(), calls=%async_computation.17 | async-start | bytes 7208960 | tf_op jit(solution)/shard_map/all_gather | solution.py:495
  12.7 504.2 %reduce-scatter.13.cloned.1.call-start = ((), (), s32[]{:S(2)}) async-start(), calls=%async_computation.18 | async-start | bytes 1310720 | tf_op jit(solution)/shard_map/reduce_scatter | solution.py:576
  118.8 49.6 %collective-permute-start.1 = (f32[1,4,264,128]{3,2,1,0:T(8,128)}, f32[1,4,264,128]{3,2,1,0:T(8,128)}, u32[]{:S(2)}, u32[]{:S(2)}) collective-permute-start(f32[1,4,264,128]{3,2,1,0:T(8,128)} %get-tuple-element.34), channel_id=1, source_target_pairs={{0,2},{1,3},{4,6},{5,7},{8,10},{9,11},{12,14},{13,15},{16,18},{17,... | collective-permute-start | bytes 1622024 | tf_op jit(solution)/shard_map/ppermute | solution.py:401
  123.0 45.5 %collective-permute-start = (f32[1,4,264,128]{3,2,1,0:T(8,128)}, f32[1,4,264,128]{3,2,1,0:T(8,128)}, u32[]{:S(2)}, u32[]{:S(2)}) collective-permute-start(f32[1,4,264,128]{3,2,1,0:T(8,128)} %get-tuple-element.34), channel_id=1, source_target_pairs={{0,1},{1,2},{2,3},{4,5},{5,6},{6,7},{8,9},{9,10},{10,11},{12,13},{... | collective-permute-start | bytes 1622024 | tf_op jit(solution)/shard_map/ppermute | solution.py:401
  159.8 17.3 %collective-permute-start.2 = (f32[1,4,264,128]{3,2,1,0:T(8,128)}, f32[1,4,264,128]{3,2,1,0:T(8,128)}, u32[]{:S(2)}, u32[]{:S(2)}) collective-permute-start(f32[1,4,264,128]{3,2,1,0:T(8,128)} %get-tuple-element.34), channel_id=1, source_target_pairs={{0,3},{4,7},{8,11},{12,15},{16,19},{20,23},{24,27},{28,31}} | collective-permute-start | bytes 1622024 | tf_op jit(solution)/shard_map/ppermute | solution.py:401
  430.2 16.8 %collective-permute-start.4 = (bf16[1,4,264,128]{3,2,1,0:T(8,128)(2,1)S(1)}, bf16[1,4,264,128]{3,2,1,0:T(8,128)(2,1)S(1)}, u32[]{:S(2)}, u32[]{:S(2)}) collective-permute-start(bf16[1,4,264,128]{3,2,1,0:T(8,128)(2,1)S(1)} %pad_maximum_fusion), channel_id=1, source_target_pairs={{2,0},{3,1},{6,4},{7,5},{10,8},{11,9},{14,12},{15,13},{18,16},{19,... | collective-permute-start | bytes 811016 | tf_op jit(solution)/shard_map/ppermute | solution.py:401
  431.5 15.5 %collective-permute-start.5 = (bf16[1,4,264,128]{3,2,1,0:T(8,128)(2,1)S(1)}, bf16[1,4,264,128]{3,2,1,0:T(8,128)(2,1)S(1)}, u32[]{:S(2)}, u32[]{:S(2)}) collective-permute-start(bf16[1,4,264,128]{3,2,1,0:T(8,128)(2,1)S(1)} %pad_maximum_fusion), channel_id=1, source_target_pairs={{3,0},{7,4},{11,8},{15,12},{19,16},{23,20},{27,24},{31,28}} | collective-permute-start | bytes 811016 | tf_op jit(solution)/shard_map/ppermute | solution.py:401
  460.7 57.7 %reduce-scatter.15.cloned.1.call-start = ((), (), s32[]{:S(2)}) async-start(), calls=%async_computation.19 | async-start | bytes 1310720 | tf_op jit(solution)/shard_map/reduce_scatter | solution.py:579
  463.9 92.8 %reduce-scatter.21.cloned.1.call-start = ((), (), s32[]{:S(2)}) async-start(), calls=%async_computation.22 | async-start | bytes 2621440 | tf_op jit(solution)/shard_map/reduce_scatter | solution.py:594
  467.9 127.1 %reduce-scatter.23.cloned.1.call-start = ((), (), s32[]{:S(2)}) async-start(), calls=%async_computation.23 | async-start | bytes 2621440 | tf_op jit(solution)/shard_map/reduce_scatter | solution.py:600
  473.3 159.9 %reduce-scatter.17.cloned.1.call-start = ((), (), s32[]{:S(2)}) async-start(), calls=%async_computation.20 | async-start | bytes 2621440 | tf_op jit(solution)/shard_map/reduce_scatter | solution.py:582
  478.5 223.6 %reduce-scatter.29.cloned.1.call-start = ((), (), s32[]{:S(2)}) async-start(), calls=%async_computation.26 | async-start | bytes 7208960 | tf_op jit(solution)/shard_map/reduce_scatter | solution.py:612
  486.5 284.6 %reduce-scatter.27.cloned.1.call-start = ((), (), s32[]{:S(2)}) async-start(), calls=%async_computation.25 | async-start | bytes 7208960 | tf_op jit(solution)/shard_map/reduce_scatter | solution.py:609
  494.4 345.6 %reduce-scatter.25.cloned.1.call-start = ((), (), s32[]{:S(2)}) async-start(), calls=%async_computation.24 | async-start | bytes 7208960 | tf_op jit(solution)/shard_map/reduce_scatter | solution.py:606
  502.3 365.7 %reduce-scatter.31.cloned.1.call-start = ((), (), s32[]{:S(2)}) async-start(), calls=%async_computation.27 | async-start | bytes 163840
  515.7 377.2 %reduce-scatter.19.cloned.1.call-start = ((), (), s32[]{:S(2)}) async-start(), calls=%async_computation.21 | async-start | bytes 40960 | tf_op jit(solution)/shard_map/reduce_scatter | solution.py:585
  516.8 520.5 %all-reduce.10.cloned.1.call-start = ((), (), s32[]{:S(2)}) async-start(), calls=%async_computation.28 | async-start | bytes 12845056 | tf_op jit(solution)/shard_map/psum | solution.py:618
  (54 other events, 615.5 us)
Sparse Core Ops, SparseCore 0:
  9.9 29.5 all-gather.13
  41.3 26.6 all-gather.11
  69.9 35.2 all-gather.15
  106.9 50.0 all-gather.17
  158.7 39.5 all-gather.19
  200.0 65.7 all-gather.23
  267.7 65.7 all-gather.21
  335.3 65.7 all-gather.25
  460.8 26.8 reduce-scatter.12
  490.7 27.7 reduce-scatter.14
  521.4 35.1 reduce-scatter.20
  559.7 35.1 reduce-scatter.22
  597.9 35.1 reduce-scatter.16
  636.3 65.8 reduce-scatter.28
  705.2 65.7 reduce-scatter.26
  774.2 65.7 reduce-scatter.24
  843.4 23.7 reduce-scatter.30
  870.4 22.4 reduce-scatter.18
  895.8 141.4 all-reduce.9

commit v2 on v1

--- a/solution.py
+++ b/solution.py
@@ -5,7 +5,7 @@
 from jax import lax
 from jax.experimental import pallas as pl
 from jax.experimental.pallas import tpu as pltpu
-from jax.sharding import PartitionSpec as P
+from jax.sharding import Mesh, PartitionSpec as P
 
 HEADS = 4
 DK = 128
@@ -150,8 +150,8 @@
 
 
 def scan_backward_kernel(
-    chunk, q_ref, k_ref, v_ref, g_ref, a_ref, st_ref, cs_ref, in_ref, do_ref, later_ref,
-    dq_ref, dk_ref, dv_ref, dg_ref, later, dqi, dki, dci,
+    chunk, q_ref, k_ref, v_ref, g_ref, a_ref, st_ref, cs_ref, in_ref, do_ref, later_ref, dog_ref,
+    out_ref, dg_ref, later, dqi, dki, dci,
 ):
     @pl.when(pl.program_id(1) == 0)
     def _():
@@ -224,9 +224,11 @@
         keys = k_ref[:, ks] * faded[:, ks]
         from_state = dot_nn(grad_out, low(held))
         from_later = dot_nn(values, ahead_low)
-        dq_ref[:, ks] = low((dqi[:, ks] + grown[:, ks] * from_state) * scale)
-        dk_ref[:, ks] = low(dki[:, ks] + faded[:, ks] * from_later)
-        dv_ref[:, vs] = low(dot_tn(a_ref[0, h], grad_out) + dot_nt(low(keys), ahead_low))
+        out_ref[:, ks] = low((dqi[:, ks] + grown[:, ks] * from_state) * scale)
+        out_ref[:, KEYS + h * DK : KEYS + (h + 1) * DK] = low(dki[:, ks] + faded[:, ks] * from_later)
+        out_ref[:, 2 * KEYS + h * DV : 2 * KEYS + (h + 1) * DV] = low(
+            dot_tn(a_ref[0, h], grad_out) + dot_nt(low(keys), ahead_low)
+        )
         through = kept[:, ks] * jnp.sum(held * ahead, axis=0, keepdims=True)
         dg_ref[:, ks] = (
             exact_sum(after, dci[:, ks] + queries * from_state)
@@ -234,6 +236,7 @@
             + through
         )
         later[h] = ahead * kept[:, ks] + dot_tn(grad_out, low(queries))
+    out_ref[:, 2 * KEYS + VALUES :] = dog_ref[...]
 
 
 def mix_forward_kernel(o_ref, qf_ref, in_ref, og_ref, gain_ref, att_ref, mixed_ref):
@@ -288,18 +291,27 @@
     return jax.ShapeDtypeStruct(shape, kind)
 
 
+def packed_specs(chunk, chunks, backward=False):
+    def at(width, place):
+        whole = rows_spec(chunk, chunks, width, backward)
+        return pl.BlockSpec(whole.block_shape, lambda s, c: (whole.index_map(s, c)[0], place))
+
+    return [at(KEYS, 0), at(KEYS, 1), at(VALUES, 1), at(VALUES, 2)]
+
+
 KEYS, VALUES = HEADS * DK, HEADS * DV
+PACKED = 2 * KEYS + 2 * VALUES
 ROOM = pltpu.CompilerParams(vmem_limit_bytes=40 * 1024 * 1024)
 
 
-def scan_forward(queries, keys, values, gates, seqs, chunk):
-    rows = queries.shape[0]
+def scan_forward(projected, gates, seqs, chunk):
+    rows = projected.shape[0]
     chunks = rows // seqs // chunk
     keyed, valued = rows_spec(chunk, chunks, KEYS), rows_spec(chunk, chunks, VALUES)
     return pl.pallas_call(
         functools.partial(scan_forward_kernel, chunk),
         grid=(seqs, chunks),
-        in_specs=[keyed, keyed, valued, keyed],
+        in_specs=packed_specs(chunk, chunks)[:3] + [keyed],
         out_specs=[
             valued,
             keyed,
@@ -323,39 +335,40 @@
         ],
         compiler_params=ROOM,
         name="scan_forward",
-    )(queries, keys, values, gates)
-
-
-def scan_backward(queries, keys, values, gates, scores, states, starts, incoming, grad_out, later, seqs, chunk):
-    rows = queries.shape[0]
+    )(projected, projected, projected, gates)
+
+
+def scan_backward(
+    projected, gates, scores, states, starts, incoming, grad_out, later, outgate_grad, seqs, chunk
+):
+    rows = projected.shape[0]
     chunks = rows // seqs // chunk
     keyed, valued = rows_spec(chunk, chunks, KEYS, True), rows_spec(chunk, chunks, VALUES, True)
     return pl.pallas_call(
         functools.partial(scan_backward_kernel, chunk),
         grid=(seqs, chunks),
         in_specs=[
-            keyed, keyed, valued, keyed,
+            *packed_specs(chunk, chunks, True)[:3],
+            keyed,
             chunk_spec(chunks, (HEADS, chunk, chunk), True),
             chunk_spec(chunks, (HEADS, DV, DK), True),
             chunk_spec(chunks, (1, KEYS), True),
             item_spec((HEADS, DV, DK)),
             valued,
             item_spec((HEADS, DV, DK)),
+            valued,
         ],
-        out_specs=[keyed, keyed, valued, keyed],
-        out_shape=[
-            shaped((rows, KEYS), jnp.bfloat16),
-            shaped((rows, KEYS), jnp.bfloat16),
-            shaped((rows, VALUES), jnp.bfloat16),
-            shaped((rows, KEYS)),
-        ],
+        out_specs=[rows_spec(chunk, chunks, PACKED, True), keyed],
+        out_shape=[shaped((rows, PACKED), jnp.bfloat16), shaped((rows, KEYS))],
         scratch_shapes=[pltpu.VMEM((HEADS, DV, DK), jnp.float32)] + [pltpu.VMEM((chunk, KEYS), jnp.float32)] * 3,
         compiler_params=ROOM,
         name="scan_backward",
-    )(queries, keys, values, gates, scores, states, starts, incoming, grad_out, later)
-
-
-def mix_forward(local_out, forget, incoming, outgate, gain, seqs, chunk):
+    )(
+        projected, projected, projected, gates, scores, states, starts, incoming, grad_out, later, outgate_grad
+    )
+
+
+def mix_forward(local_out, forget, incoming, projected, gain, seqs, chunk):
     rows = local_out.shape[0]
     chunks = rows // seqs // chunk
     keyed, valued = rows_spec(chunk, chunks, KEYS), rows_spec(chunk, chunks, VALUES)
@@ -363,15 +376,15 @@
     return pl.pallas_call(
         mix_forward_kernel,
         grid=(seqs, chunks),
-        in_specs=[valued, keyed, item_spec((HEADS, DV, DK)), valued, whole_gain],
+        in_specs=[valued, keyed, item_spec((HEADS, DV, DK)), packed_specs(chunk, chunks)[3], whole_gain],
         out_specs=[valued, valued],
         out_shape=[shaped((rows, VALUES)), shaped((rows, VALUES), jnp.bfloat16)],
         compiler_params=ROOM,
         name="mix_forward",
-    )(local_out, forget, incoming, outgate, gain)
-
-
-def mix_backward(mixed_grad, attended, outgate, gain, forget, seqs, chunk):
+    )(local_out, forget, incoming, projected, gain)
+
+
+def mix_backward(mixed_grad, attended, projected, gain, forget, seqs, chunk):
     rows = attended.shape[0]
     chunks = rows // seqs // chunk
     keyed, valued = rows_spec(chunk, chunks, KEYS), rows_spec(chunk, chunks, VALUES)
@@ -379,7 +392,7 @@
     return pl.pallas_call(
         mix_backward_kernel,
         grid=(seqs, chunks),
-        in_specs=[valued, valued, valued, whole_gain, keyed],
+        in_specs=[valued, valued, packed_specs(chunk, chunks)[3], whole_gain, keyed],
         out_specs=[valued, valued, item_spec((HEADS, DV, DK)), item_spec((1, DV))],
         out_shape=[
             shaped((rows, VALUES)),
@@ -389,7 +402,7 @@
         ],
         compiler_params=ROOM,
         name="mix_backward",
-    )(mixed_grad, attended, outgate, gain, forget)
+    )(mixed_grad, attended, projected, gain, forget)
 
 
 def from_neighbours(summary, step):
@@ -421,6 +434,42 @@
     return lax.dot_general(
         left, right, (((1,), (1,)), ((), ())), preferred_element_type=jnp.float32
     )
+
+
+EVERYWHERE = ("z", "core", "seq")
+
+
+def swapped(array):
+    return lax.ppermute(array, "core", [(0, 1), (1, 0)])
+
+
+def own_half(array, dim, other=False):
+    core = lax.axis_index("core")
+    size = array.shape[dim] // 2
+    return lax.dynamic_slice_in_dim(array, ((1 - core) if other else core) * size, size, dim)
+
+
+def joined(mine, theirs, dim):
+    first = lax.axis_index("core") == 0
+    return jnp.where(
+        first, jnp.concatenate([mine, theirs], dim), jnp.concatenate([theirs, mine], dim)
+    )
+
+
+def core_columns(array, other=False):
+    count = lax.axis_size("seq")
+    rows, width = array.shape
+    split = array.reshape(rows, count, width // count)
+    return own_half(split, 2, other).reshape(rows, width // 2)
+
+
+def pair_sum(left_theirs, left_mine, right_theirs, right_mine):
+    theirs = swapped(low(product_left(left_theirs, right_theirs)))
+    return low(product_left(left_mine, right_mine) + theirs.astype(jnp.float32))
+
+
+def scattered(array):
+    return lax.psum_scatter(array, "seq", scatter_dimension=0, tiled=True)
 
 
 def local(
@@ -443,34 +492,53 @@
 ):
     seqs_here, seg_len, width = tokens.shape
     rows_here = seqs_here * seg_len
-
-    mixer_full = (
-        lax.all_gather(mixer_gain, "seq", axis=0, tiled=True),
-        lax.all_gather(query_weight, "seq", axis=0, tiled=True),
-        lax.all_gather(key_weight, "seq", axis=0, tiled=True),
-        lax.all_gather(value_weight, "seq", axis=0, tiled=True),
-        lax.all_gather(decay_down, "seq", axis=0, tiled=True),
-        lax.all_gather(decay_up, "seq", axis=1, tiled=True),
-        lax.all_gather(decay_bias, "seq", axis=0, tiled=True),
-        lax.all_gather(outgate_weight, "seq", axis=0, tiled=True),
-        lax.all_gather(head_gain, "seq", axis=0, tiled=True),
-        lax.all_gather(output_weight, "seq", axis=0, tiled=True),
-    )
-    gain_one = mixer_full[0].astype(jnp.float32)
-    decay_up_f = mixer_full[5].astype(jnp.float32)
-    decay_bias_f = mixer_full[6].astype(jnp.float32)
-    head_gain_f = mixer_full[8].astype(jnp.float32)
+    count, place = lax.axis_size("seq"), lax.axis_index("seq")
+    ff = gate_weight.shape[1]
+
+    half_rows = query_weight.shape[0] // 2
+    smalls = [mixer_gain, decay_down, decay_up, decay_bias, head_gain, channel_gain]
+    flat = jnp.concatenate([small.reshape(-1) for small in smalls])
+    extra = -(-flat.size // (half_rows * 128)) * 128
+    flat = jnp.pad(flat, (0, half_rows * extra - flat.size)).reshape(half_rows, extra)
+    mixer_packed = jnp.concatenate(
+        [
+            own_half(weight, 0)
+            for weight in (query_weight, key_weight, value_weight, outgate_weight, output_weight)
+        ]
+        + [flat],
+        axis=1,
+    )
+    mixer_mine = lax.all_gather(mixer_packed, "seq")
+    mixer_theirs = swapped(mixer_mine)
+    wide = PACKED + width
+    mixer_full = joined(mixer_mine[:, :, :wide], mixer_theirs[:, :, :wide], 1).reshape(width, wide)
+    projections, output_full = mixer_full[:, :PACKED], mixer_full[:, PACKED:]
+    small_all = mixer_mine[:, :, wide:].reshape(count, -1)
+    pieces, begin = [], 0
+    for small in smalls:
+        pieces.append(small_all[:, begin : begin + small.size].reshape((count,) + small.shape))
+        begin += small.size
+    gain_one = pieces[0].reshape(-1).astype(jnp.float32)
+    decay_down_all = pieces[1].reshape(width, -1)
+    decay_up_f = pieces[2].transpose(1, 0, 2).reshape(decay_up.shape[0], -1).astype(jnp.float32)
+    decay_bias_f = pieces[3].reshape(-1).astype(jnp.float32)
+    head_gain_f = pieces[4].reshape(-1).astype(jnp.float32)
+    gain_two = pieces[5].reshape(-1).astype(jnp.float32)
+
+    ffn_packed = jnp.concatenate([own_half(gate_weight, 0), own_half(up_weight, 0)], axis=1)
+    ffn_mine = lax.all_gather(ffn_packed, "seq")
+    ffn_full = joined(ffn_mine, swapped(ffn_mine), 1).reshape(width, 2 * ff)
+    down_mine = lax.all_gather(own_half(down_weight, 1), "seq", tiled=True)
+    down_full = joined(down_mine, swapped(down_mine), 1)
+
     inputs = tokens.reshape(rows_here, width).astype(jnp.float32)
 
     def first_norm(inputs_in, gain_in):
         return normalize(inputs_in) * gain_in
 
     normed_one = first_norm(inputs, gain_one).astype(jnp.bfloat16)
-    queries = product(normed_one, mixer_full[1])
-    keys_all = product(normed_one, mixer_full[2])
-    values_all = product(normed_one, mixer_full[3])
-    low_rank = product(normed_one, mixer_full[4])
-    outgate = product(normed_one, mixer_full[7])
+    projected = product(normed_one, projections)
+    low_rank = product(normed_one, decay_down_all)
 
     def gate_fn(rank_in, up_in, bias_in):
         return (
@@ -480,210 +548,147 @@
 
     gates = gate_fn(low_rank, decay_up_f, decay_bias_f)
     chunk = min(CHUNK, seg_len)
-    local_out, forget, scores, states, starts, summary = scan_forward(
-        queries, keys_all, values_all, gates, seqs_here, chunk
-    )
+    local_out, forget, scores, states, starts, summary = scan_forward(projected, gates, seqs_here, chunk)
     incoming_state = from_neighbours(summary, 1)
     attended, mixed = mix_forward(
-        local_out, forget, incoming_state, outgate, head_gain_f[None, :], seqs_here, chunk
-    )
-    resid = inputs + product(mixed, mixer_full[9])
-    ffn_full = (
-        lax.all_gather(channel_gain, "seq", axis=0, tiled=True),
-        lax.all_gather(gate_weight, "seq", axis=0, tiled=True),
-        lax.all_gather(up_weight, "seq", axis=0, tiled=True),
-        lax.all_gather(down_weight, "seq", axis=0, tiled=True),
-    )
-    gain_two = ffn_full[0].astype(jnp.float32)
+        local_out, forget, incoming_state, projected, head_gain_f[None, :], seqs_here, chunk
+    )
+    resid = inputs + product(mixed, output_full)
     normed_two = first_norm(resid, gain_two).astype(jnp.bfloat16)
-    gate_pre = product(normed_two, ffn_full[1])
-    up_pre = product(normed_two, ffn_full[2])
-
-    def swiglu(gate_in, up_in):
-        return jax.nn.silu(gate_in) * up_in
-
-    hidden = swiglu(gate_pre, up_pre).astype(jnp.bfloat16)
-    result = resid + product(hidden, ffn_full[3])
+    both_pre = product(normed_two, ffn_full)
+
+    def swiglu(both):
+        return jax.nn.silu(both[:, :ff]) * both[:, ff:]
+
+    hidden = swiglu(both_pre).astype(jnp.bfloat16)
+    result = resid + product(hidden, down_full)
     block_out = result.astype(jnp.bfloat16).reshape(tokens.shape)
-    mixer_back = (
-        lax.all_gather(mixer_gain, "seq", axis=0, tiled=True),
-        lax.all_gather(query_weight, "seq", axis=0, tiled=True),
-        lax.all_gather(key_weight, "seq", axis=0, tiled=True),
-        lax.all_gather(value_weight, "seq", axis=0, tiled=True),
-        lax.all_gather(decay_down, "seq", axis=0, tiled=True),
-        lax.all_gather(decay_up, "seq", axis=1, tiled=True),
-        lax.all_gather(decay_bias, "seq", axis=0, tiled=True),
-        lax.all_gather(outgate_weight, "seq", axis=0, tiled=True),
-        lax.all_gather(head_gain, "seq", axis=0, tiled=True),
-        lax.all_gather(output_weight, "seq", axis=0, tiled=True),
-    )
-    ffn_back = (
-        lax.all_gather(channel_gain, "seq", axis=0, tiled=True),
-        lax.all_gather(gate_weight, "seq", axis=0, tiled=True),
-        lax.all_gather(up_weight, "seq", axis=0, tiled=True),
-        lax.all_gather(down_weight, "seq", axis=0, tiled=True),
-    )
-    grad_out = cotangent.reshape(rows_here, width).astype(jnp.float32)
-    grad_low = grad_out.astype(jnp.bfloat16)
-    down_weight_grad = product_left(hidden, grad_low)
-    hidden_grad = product_right(grad_low, ffn_back[3])
-    swiglu_pulled = jax.vjp(swiglu, gate_pre, up_pre)[1](hidden_grad)
-    gate_grad = swiglu_pulled[0].astype(jnp.bfloat16)
-    up_grad = swiglu_pulled[1].astype(jnp.bfloat16)
-    gate_weight_grad = product_left(normed_two, gate_grad)
-    up_weight_grad = product_left(normed_two, up_grad)
-    normed_two_grad = product_right(gate_grad, ffn_back[1]) + product_right(up_grad, ffn_back[2])
+
+    grad_low = cotangent.reshape(rows_here, width)
+    grad_out = grad_low.astype(jnp.float32)
+    down_share = scattered(pair_sum(hidden, hidden, own_half(grad_low, 1, True), own_half(grad_low, 1)))
+    hidden_grad = product_right(grad_low, down_full)
+    gate_pre, up_pre = both_pre[:, :ff], both_pre[:, ff:]
+    sigma = jax.nn.sigmoid(gate_pre)
+    both_grad = jnp.concatenate(
+        [
+            low(hidden_grad * up_pre * (sigma + gate_pre * sigma * (1.0 - sigma))),
+            low(hidden_grad * (gate_pre * sigma)),
+        ],
+        axis=1,
+    )
+    ffn_share = scattered(
+        pair_sum(core_columns(normed_two, True), core_columns(normed_two), both_grad, both_grad)
+    )
+    normed_two_grad = product_right(both_grad, ffn_full)
     norm_pulled = jax.vjp(first_norm, resid, gain_two)[1](normed_two_grad)
     resid_grad = grad_out + norm_pulled[0]
     channel_gain_grad = norm_pulled[1]
     branch_grad = resid_grad.astype(jnp.bfloat16)
-    output_weight_grad = product_left(mixed, branch_grad)
-    mixed_grad = product_right(branch_grad, mixer_back[9])
+    mixed_grad = product_right(branch_grad, output_full)
     attended_grad, outgate_grad, state_grad, head_gain_grad = mix_backward(
-        mixed_grad, attended, outgate, head_gain_f[None, :], forget, seqs_here, chunk
+        mixed_grad, attended, projected, head_gain_f[None, :], forget, seqs_here, chunk
     )
     head_gain_grad = head_gain_grad.sum((0, 1))
     later_grad = from_neighbours(
         jnp.concatenate([state_grad, summary[:, :, DV:]], axis=2).astype(jnp.bfloat16), -1
     )
-    query_grad, key_grad, value_grad, gates_grad = scan_backward(
-        queries, keys_all, values_all, gates, scores, states, starts, incoming_state,
-        attended_grad, later_grad, seqs_here, chunk,
+    packed_grad, gates_grad = scan_backward(
+        projected, gates, scores, states, starts, incoming_state,
+        attended_grad, later_grad, outgate_grad, seqs_here, chunk,
     )
     gate_pulled = jax.vjp(gate_fn, low_rank, decay_up_f, decay_bias_f)[1](gates_grad)
     low_rank_grad = gate_pulled[0].astype(jnp.bfloat16)
-    decay_up_grad = gate_pulled[1]
-    decay_bias_grad = gate_pulled[2]
-    query_weight_grad = product_left(normed_one, query_grad)
-    key_weight_grad = product_left(normed_one, key_grad)
-    value_weight_grad = product_left(normed_one, value_grad)
     decay_down_grad = product_left(normed_one, low_rank_grad)
-    outgate_weight_grad = product_left(normed_one, outgate_grad)
-    normed_one_grad = (
-        product_right(query_grad, mixer_back[1])
-        + product_right(key_grad, mixer_back[2])
-        + product_right(value_grad, mixer_back[3])
-        + product_right(low_rank_grad, mixer_back[4])
-        + product_right(outgate_grad, mixer_back[7])
-    )
+    normed_one_grad = product_right(packed_grad, projections) + product_right(low_rank_grad, decay_down_all)
     first_pulled = jax.vjp(first_norm, inputs, gain_one)[1](normed_one_grad)
     tokens_grad = (resid_grad + first_pulled[0]).reshape(tokens.shape)
-    mixer_gain_grad = first_pulled[1]
-    shares = (
-        lax.psum_scatter(
-            mixer_gain_grad.astype(jnp.bfloat16), "seq", scatter_dimension=0, tiled=True
-        ).astype(jnp.float32),
-        lax.psum_scatter(
-            query_weight_grad.astype(jnp.bfloat16), "seq", scatter_dimension=0, tiled=True
-        ).astype(jnp.float32),
-        lax.psum_scatter(
-            key_weight_grad.astype(jnp.bfloat16), "seq", scatter_dimension=0, tiled=True
-        ).astype(jnp.float32),
-        lax.psum_scatter(
-            value_weight_grad.astype(jnp.bfloat16), "seq", scatter_dimension=0, tiled=True
-        ).astype(jnp.float32),
-        lax.psum_scatter(
-            decay_down_grad.astype(jnp.bfloat16), "seq", scatter_dimension=0, tiled=True
-        ).astype(jnp.float32),
-        lax.psum_scatter(
-            decay_up_grad.astype(jnp.bfloat16), "seq", scatter_dimension=1, tiled=True
-        ).astype(jnp.float32),
-        lax.psum_scatter(
-            decay_bias_grad.astype(jnp.bfloat16), "seq", scatter_dimension=0, tiled=True
-        ).astype(jnp.float32),
-        lax.psum_scatter(
-            outgate_weight_grad.astype(jnp.bfloat16), "seq", scatter_dimension=0, tiled=True
-        ).astype(jnp.float32),
-        lax.psum_scatter(
-            head_gain_grad.astype(jnp.bfloat16), "seq", scatter_dimension=0, tiled=True
-        ).astype(jnp.float32),
-        lax.psum_scatter(
-            output_weight_grad.astype(jnp.bfloat16), "seq", scatter_dimension=0, tiled=True
-        ).astype(jnp.float32),
-        lax.psum_scatter(
-            channel_gain_grad.astype(jnp.bfloat16), "seq", scatter_dimension=0, tiled=True
-        ).astype(jnp.float32),
-        lax.psum_scatter(
-            gate_weight_grad.astype(jnp.bfloat16), "seq", scatter_dimension=0, tiled=True
-        ).astype(jnp.float32),
-        lax.psum_scatter(
-            up_weight_grad.astype(jnp.bfloat16), "seq", scatter_dimension=0, tiled=True
-        ).astype(jnp.float32),
-        lax.psum_scatter(
-            down_weight_grad.astype(jnp.bfloat16), "seq", scatter_dimension=0, tiled=True
-        ).astype(jnp.float32),
-    )
-    totals = (
-        lax.psum(shares[0].astype(jnp.bfloat16), "rep").astype(jnp.float32),
-        lax.psum(shares[1].astype(jnp.bfloat16), "rep").astype(jnp.float32),
-        lax.psum(shares[2].astype(jnp.bfloat16), "rep").astype(jnp.float32),
-        lax.psum(shares[3].astype(jnp.bfloat16), "rep").astype(jnp.float32),
-        lax.psum(shares[4].astype(jnp.bfloat16), "rep").astype(jnp.float32),
-        lax.psum(shares[5].astype(jnp.bfloat16), "rep").astype(jnp.float32),
-        lax.psum(shares[6].astype(jnp.bfloat16), "rep").astype(jnp.float32),
-        lax.psum(shares[7].astype(jnp.bfloat16), "rep").astype(jnp.float32),
-        lax.psum(shares[8].astype(jnp.bfloat16), "rep").astype(jnp.float32),
-        lax.psum(shares[9].astype(jnp.bfloat16), "rep").astype(jnp.float32),
-        lax.psum(shares[10].astype(jnp.bfloat16), "rep").astype(jnp.float32),
-        lax.psum(shares[11].astype(jnp.bfloat16), "rep").astype(jnp.float32),
-        lax.psum(shares[12].astype(jnp.bfloat16), "rep").astype(jnp.float32),
-        lax.psum(shares[13].astype(jnp.bfloat16), "rep").astype(jnp.float32),
+
+    packed_theirs = swapped(
+        jnp.concatenate(
+            [
+                low(product_left(core_columns(normed_one, True), packed_grad)),
+                low(product_left(core_columns(mixed, True), branch_grad)),
+            ],
+            axis=1,
+        )
+    ).astype(jnp.float32)
+    mixer_share = scattered(
+        jnp.concatenate(
+            [
+                low(product_left(core_columns(normed_one), packed_grad) + packed_theirs[:, :PACKED]),
+                low(product_left(core_columns(mixed), branch_grad) + packed_theirs[:, PACKED:]),
+            ],
+            axis=1,
+        )
+    )
+
+    def whole(share, dim):
+        total = lax.psum(share, "z")
+        return joined(total, swapped(total), dim).astype(jnp.float32)
+
+    down_weight_grad = whole(down_share, 1)
+    ffn_total = whole(ffn_share, 0)
+    mixer_total = whole(mixer_share, 0)
+
+    small_grads = [
+        first_pulled[1], decay_down_grad, gate_pulled[1], gate_pulled[2], head_gain_grad, channel_gain_grad,
+    ]
+    summed = lax.psum(jnp.concatenate([grad.reshape(-1) for grad in small_grads]), EVERYWHERE)
+    shares, begin = [], 0
+    for grad in small_grads:
+        shares.append(summed[begin : begin + grad.size].reshape(grad.shape))
+        begin += grad.size
+
+    def own_share(array, dim=0):
+        size = array.shape[dim] // count
+        return lax.dynamic_slice_in_dim(array, place * size, size, dim)
+
+    columns = (0, KEYS, 2 * KEYS, 2 * KEYS + VALUES, PACKED, wide)
+    query_g, key_g, value_g, outgate_g, output_g = (
+        mixer_total[:, a:b] for a, b in zip(columns[:-1], columns[1:])
     )
     return (
         block_out,
         tokens_grad,
-        totals[0],
-        totals[1],
-        totals[2],
-        totals[3],
-        totals[4],
-        totals[5],
-        totals[6],
-        totals[7],
-        totals[8],
-        totals[9],
-        totals[10],
-        totals[11],
-        totals[12],
-        totals[13],
+        own_share(shares[0]),
+        query_g,
+        key_g,
+        value_g,
+        own_share(shares[1]),
+        own_share(shares[2], 1),
+        own_share(shares[3]),
+        outgate_g,
+        own_share(shares[4]),
+        output_g,
+        own_share(shares[5]),
+        ffn_total[:, :ff],
+        ffn_total[:, ff:],
+        down_weight_grad,
     )
 
 
 def solution(mesh):
+    rep, seq = mesh.shape["rep"], mesh.shape["seq"]
+    cores = Mesh(mesh.devices.reshape(rep // 2, 2, seq), EVERYWHERE)
+    sequences, weights = P(("z", "core"), "seq", None), P("seq", None)
     in_specs = (
-        P("rep", "seq", None),
+        sequences,
         P("seq"),
-        P("seq", None),
-        P("seq", None),
-        P("seq", None),
-        P("seq", None),
+        weights,
+        weights,
+        weights,
+        weights,
         P(None, "seq"),
         P("seq"),
-        P("seq", None),
+        weights,
         P("seq"),
-        P("seq", None),
+        weights,
         P("seq"),
-        P("seq", None),
-        P("seq", None),
-        P("seq", None),
-        P("rep", "seq", None),
-    )
-    out_specs = (
-        P("rep", "seq", None),
-        P("rep", "seq", None),
-        P("seq"),
-        P("seq", None),
-        P("seq", None),
-        P("seq", None),
-        P("seq", None),
-        P(None, "seq"),
-        P("seq"),
-        P("seq", None),
-        P("seq"),
-        P("seq", None),
-        P("seq"),
-        P("seq", None),
-        P("seq", None),
-        P("seq", None),
-    )
-    return jax.shard_map(local, mesh=mesh, in_specs=in_specs, out_specs=out_specs, check_vma=False)
+        weights,
+        weights,
+        weights,
+        sequences,
+    )
+    out_specs = (sequences, *in_specs[:15])
+    return jax.shard_map(local, mesh=cores, in_specs=in_specs, out_specs=out_specs, check_vma=False)

time: 1070 us -> 817 us (0.76)
  waiting for transfers between devices: 734 us -> 555 us
  blocking collectives: 102 us -> 0 us
  local copies, waits for them, and re-layouts: 18.8 us -> 60.5 us
  matrix products: 120 us -> 95.4 us
  other arithmetic: 26.9 us -> 41.5 us
    reduce_scatter x9 -> x3, waiting for transfers between devices: 347 us -> 122 us  [scattered(): return lax.psum_scatter(array, 'seq', scatter_dimension=0, tiled=True)]
    psum x1 -> x2, waiting for transfers between devices: 112 us -> 229 us  [the longest x1 120 us: local(): lax.psum(jnp.concatenate([grad.reshape(-1) for grad in small_grads]), EVE...]
    all_gather x8 -> x3, waiting for transfers between devices: 247 us -> 163 us  [the longest x1 68.2 us: local(): ffn_mine = lax.all_gather(ffn_packed, 'seq')]
    all_gather x5 -> x0, blocking collectives: 39.8 us -> none  [the longest x1 9.38 us: local(): lax.all_gather(decay_bias, 'seq', axis=0, tiled=True)]
    unnamed x2 -> x0, blocking collectives: 33.3 us -> none
    psum x1 -> x0, blocking collectives: 29.2 us -> none  [local(): lax.psum(shares[0].astype(jnp.bfloat16), 'rep').astype(jnp.float32)]
    slice x0 -> x12, local copies, waits for them, and re-layouts: none -> 18.3 us  [the longest x5 4.9 us: local(): shares.append(summed[begin:begin + grad.size].reshape(grad.shape))]
    dot_general x9 -> x5, matrix products: 40.8 us -> 26.9 us  [product(): return jnp.dot(left, right, preferred_element_type=jnp.float32)]
  transfers between devices with their start and end apart: 25 -> 23, of which waited for: 18 -> 13; matrix products, arithmetic and copies ran while one was open for 11% -> 18% of each run, Pallas kernels for 1% -> 3%
where the time goes in v2:
time: 817 us; the launch traced here: 808 us
  waiting for transfers between devices  555 us (68%)
  matrix products  95.4 us (12%)
  local copies, waits for them, and re-layouts  60.5 us (7%)
  other arithmetic  41.5 us (5%)
  Pallas kernels  24.4 us (3%)
  between operations  15.4 us (2%)
  starting transfers between devices  15.3 us (2%)
    reduce_scatter x3, waiting for transfers between devices, scattered(): return lax.psum_scatter(array, 'seq', scatter_dimension=0, tiled=True)  122 us
    psum x1, waiting for transfers between devices, local(): lax.psum(jnp.concatenate([grad.reshape(-1) for grad in small_grads]), EVE...  120 us
    psum x1, waiting for transfers between devices, whole(): total = lax.psum(share, 'z')  109 us
    all_gather x1, waiting for transfers between devices, local(): ffn_mine = lax.all_gather(ffn_packed, 'seq')  68.2 us
    all_gather x1, waiting for transfers between devices, local(): mixer_mine = lax.all_gather(mixer_packed, 'seq')  52.9 us
    all_gather x1, waiting for transfers between devices, local(): down_mine = lax.all_gather(own_half(down_weight, 1), 'seq', tiled=True)  41.5 us
    dot_general x5, matrix products, product_right(): lax.dot_general(left, right, (((1,), (1,)), ((), ())), preferred_element_...  35.8 us
    ppermute x6, waiting for transfers between devices, from_neighbours(): came = lax.ppermute(summary, 'seq', pairs)  28.6 us
  transfers between devices with their start and end apart: 23, of which 13 were waited for; matrix products, arithmetic and copies ran while one was open for 18% of the time, Pallas kernels for 3%

profile of v2, /device:TPU:0, one launch (start us, length us, event | category | flops | bytes accessed | tf_op | source)
XLA Modules:
  0.0 807.5 jit_solution(11872878045191547053)
XLA Ops:
  21.3 52.9 %all-gather.8.cloned.1.call-done = bf16[512,4224]{1,0:T(8,128)(2,1)} async-done(((bf16[128,4224]{1,0:T(8,128)(2,1)}), bf16[512,4224]{1,0:T(8,128)(2,1)}) %all-gather.8.cloned.1.call-update) | async-done | bytes 4325392 | tf_op jit(solution)/shard_map/all_gather | solution.py:511
  74.2 68.2 %all-gather.10.cloned.1.call-done = bf16[512,5632]{1,0:T(8,128)(2,1)} async-done(((bf16[128,5632]{1,0:T(8,128)(2,1)}), bf16[512,5632]{1,0:T(8,128)(2,1)}) %all-gather.10.cloned.1.call-update) | async-done | bytes 5767184 | tf_op jit(solution)/shard_map/all_gather | solution.py:529
  145.2 41.5 %all-gather.6.cloned.1.call-done = bf16[2816,512]{1,0:T(8,128)(2,1)} async-done(((bf16[704,512]{1,0:T(8,128)(2,1)}), bf16[2816,512]{1,0:T(8,128)(2,1)}) %all-gather.6.cloned.1.call-update) | async-done | bytes 2883600 | tf_op jit(solution)/shard_map/all_gather | solution.py:531
  186.7 4.7 slice.169
  206.0 6.4 scan_forward.1
  228.7 13.4 %collective-permute-done.2 = f32[1,4,264,128]{3,2,1,0:T(8,128)} collective-permute-done((f32[1,4,264,128]{3,2,1,0:T(8,128)}, f32[1,4,264,128]{3,2,1,0:T(8,128)}, u32[]{:S(2)}, u32[]{:S(2)}) %collective-permute-start.2) | collective-permute-done | bytes 540704 | tf_op jit(solution)/shard_map/ppermute | solution.py:414
  259.1 9.6 %maximum_select_fusion = bf16[4,256,5632]{2,1,0:T(8,128)(2,1)S(1)} fusion(bf16[4,128,5632]{2,1,0:T(8,128)(2,1)} %collective-permute-done.4, bf16[4,128,5632]{2,1,0:T(8,128)(2,1)} %bitcast.146, pred[]{:T(512)S(6)} %eq.18), kind=kLoop, calls=%fused_computation | loop fusion | flops 51904512 | bytes 23068672 | tf_op jit(solution)/shard_map/jit(_where)/select_n | solution.py:454
  268.7 8.8 %fusion.104 = f32[512,5632]{1,0:T(8,128)} fusion(bf16[512,1024]{1,0:T(8,128)(2,1)S(1)} %copy-done.29, bf16[1024,5632]{1,0:T(8,128)(2,1)S(1)} %bitcast.139), kind=kOutput, calls=%fused_computation.175 | convolution fusion | flops 5905580032 | bytes 24117248 | tf_op jit(solution)/shard_map/dot_general | solution.py:424
  277.6 11.5 %fusion.2 = (bf16[512,2816]{1,0:T(8,128)(2,1)}, bf16[512,2816]{1,0:T(8,128)(2,1)}, bf16[512,2816]{1,0:T(8,128)(2,1)}) fusion(f32[512,5632]{1,0:T(8,128)} %fusion.104, bf16[1,512,1024]{2,1,0:T(8,128)(2,1)S(1)} %copy-done.36, bf16[2816,512]{1,0:T(8,128)(2,1)} %collective-permute-done.5, bf16[2816,512]{1,0:T(8,128)(2,1)S(1)} %copy-done.42, pred[]{:T(512)S(6)} %eq.18), kind=kOutput, calls=%fused_computation.11 | convolution fusion | flops 2998927360 | bytes 27000832 | tf_op jit(solution)/shard_map/dot_general | solution.py:434
  289.1 12.2 %multiply_reduce_fusion = (f32[1024]{0:T(1024)S(1)}, f32[512]{0:T(512)S(1)}, f32[512,1024]{1,0:T(8,128)S(1)}) fusion(f32[512,1024]{1,0:T(8,128)S(1)} %copy-done.28, f32[512]{0:T(512)S(1)} %fusion.86, f32[1024]{0:T(1024)S(1)} %bitcast.165, bf16[1024,5632]{1,0:T(8,128)(2,1)} %bitcast.140, bf16[512,2816]{1,0:T(8,128)(2,1)} %get-tuple-element.70, ...), kind=kOutput, calls=%fused_computation.54 | convolution fusion | flops 5920258560 | bytes 21508096 | tf_op jit(solution)/shard_map/dot_general | solution.py:434
  301.4 5.2 convolution_convert_fusion.1
  310.9 4.3 mix_backward.1
  320.2 8.7 %collective-permute-done.6 = bf16[1,4,264,128]{3,2,1,0:T(8,128)(2,1)S(1)} collective-permute-done((bf16[1,4,264,128]{3,2,1,0:T(8,128)(2,1)S(1)}, bf16[1,4,264,128]{3,2,1,0:T(8,128)(2,1)S(1)}, u32[]{:S(2)}, u32[]{:S(2)}) %collective-permute-start.6) | collective-permute-done | bytes 270368 | tf_op jit(solution)/shard_map/ppermute | solution.py:414
  333.3 12.0 %scan_backward.1 = (bf16[512,3072]{1,0:T(8,128)(2,1)S(1)}, f32[512,512]{1,0:T(8,128)S(1)}) custom-call(f32[512,3072]{1,0:T(8,128)} %copy-done.2, f32[512,3072]{1,0:T(8,128)} %copy-done.2, f32[512,3072]{1,0:T(8,128)} %copy-done.2, f32[512,512]{1,0:T(8,128)S(1)} %copy-done.7, bf16[4,4,128,128]{3,2,1,0:T(8,128)(2,1)S(1)} %copy-done.16, ...), custom_call_target="tpu_custom_call" | custom-call | tf_op jit(solution)/shard_map/scan_backward/pallas_call | solution.py:347
  367.1 6.4 convolution_convert_fusion
  373.8 9.2 %collective-permute-done.11 = bf16[512,5632]{1,0:T(8,128)(2,1)S(1)} collective-permute-done((bf16[512,5632]{1,0:T(8,128)(2,1)S(1)}, bf16[512,5632]{1,0:T(8,128)(2,1)S(1)}, u32[]{:S(2)}, u32[]{:S(2)}) %collective-permute-start.11) | collective-permute-done | bytes 5767200 | tf_op jit(solution)/shard_map/ppermute | solution.py:443
  383.0 6.0 add_convert_fusion
  389.0 10.1 %fusion.34 = bf16[1,512,1024]{2,1,0:T(8,128)(2,1)} fusion(f32[512,1024]{1,0:T(8,128)} %copy-done.27, bf16[512,2816]{1,0:T(8,128)(2,1)} %get-tuple-element.71, bf16[2816,512]{1,0:T(8,128)(2,1)} %collective-permute-done.5, bf16[2816,512]{1,0:T(8,128)(2,1)} %all-gather.6.cloned.1.call-done, pred[]{:T(512)S(6)} %eq.18), kind=kOutput, calls=%fused_computation.70 | convolution fusion | flops 2979790848 | bytes 11796481 | tf_op jit(solution)/shard_map/dot_general | solution.py:424
  399.1 53.4 %reduce-scatter.4.cloned.1.call-done = bf16[128,4096]{1,0:T(8,128)(2,1)} async-done(((bf16[512,4096]{1,0:T(8,128)(2,1)}), bf16[128,4096]{1,0:T(8,128)(2,1)}) %reduce-scatter.4.cloned.1.call-update) | async-done | bytes 1048592 | tf_op jit(solution)/shard_map/reduce_scatter | solution.py:472
  452.5 68.9 %reduce-scatter.6.cloned.1.call-done = bf16[128,5632]{1,0:T(8,128)(2,1)} async-done(((bf16[512,5632]{1,0:T(8,128)(2,1)}), bf16[128,5632]{1,0:T(8,128)(2,1)}) %reduce-scatter.6.cloned.1.call-update) | async-done | bytes 1441808 | tf_op jit(solution)/shard_map/reduce_scatter | solution.py:472
  531.2 7.9 fusion.17
  539.2 108.9 %all-reduce.7.cloned.1.call-done = (bf16[128,4096]{1,0:T(8,128)(2,1)}, bf16[128,5632]{1,0:T(8,128)(2,1)}, bf16[704,512]{1,0:T(8,128)(2,1)}) async-done(((bf16[128,4096]{1,0:T(8,128)(2,1)}, bf16[128,5632]{1,0:T(8,128)(2,1)}, bf16[704,512]{1,0:T(8,128)(2,1)}), (bf16[128,4096]{1,0:T(8,128)(2,1)}, bf16[128,5632]{1,0:T(8,128)(2,1)}, bf16[704,512]{1,0:T(8,128)(2,1)})) %all-reduce.7.cloned.1.call-update) | async-done | bytes 3211280 | tf_op jit(solution)/shard_map/psum | solution.py:627
  649.3 4.5 fusion.11
  653.8 119.9 %all-reduce.5.cloned.1.call-done = f32[27392]{0:T(1024)} async-done(((f32[27392]{0:T(1024)}), f32[27392]{0:T(1024)}) %all-reduce.5.cloned.1.call-update) | async-done | bytes 109584 | tf_op jit(solution)/shard_map/psum | solution.py:637
  (229 shorter events, 137.6 us)
Async XLA Ops:
  7.2 67.0 %all-gather.8.cloned.1.call-start = ((), (), s32[]{:S(2)}) async-start(), calls=%async_computation.8 | async-start | bytes 5406720 | tf_op jit(solution)/shard_map/all_gather | solution.py:511
  17.5 124.9 %all-gather.10.cloned.1.call-start = ((), (), s32[]{:S(2)}) async-start(), calls=%async_computation.9 | async-start | bytes 7208960 | tf_op jit(solution)/shard_map/all_gather | solution.py:529
  20.2 166.4 %all-gather.6.cloned.1.call-start = ((), (), s32[]{:S(2)}) async-start(), calls=%async_computation.3 | async-start | bytes 3604480 | tf_op jit(solution)/shard_map/all_gather | solution.py:531
  21.2 377.9 %reduce-scatter.8.cloned.1.call-start = ((), (), s32[]{:S(2)}) async-start(), calls=%async_computation.7 | async-start | bytes 3604480 | tf_op jit(solution)/shard_map/reduce_scatter | solution.py:472
  74.2 121.3 %collective-permute-start = (bf16[4,128,4224]{2,1,0:T(8,128)(2,1)}, bf16[4,128,4224]{2,1,0:T(8,128)(2,1)}, u32[]{:S(2)}, u32[]{:S(2)}) collective-permute-start(bf16[4,128,4224]{2,1,0:T(8,128)(2,1)} %bitcast.147), channel_id=1, source_target_pairs={{0,4},{4,0},{1,5},{5,1},{2,6},{6,2},{3,7},{7,3},{8,12},{12,8},{9,1... | collective-permute-start | bytes 12976136 | tf_op jit(solution)/shard_map/ppermute | solution.py:443
  142.4 116.7 %collective-permute-start.4 = (bf16[4,128,5632]{2,1,0:T(8,128)(2,1)}, bf16[4,128,5632]{2,1,0:T(8,128)(2,1)}, u32[]{:S(2)}, u32[]{:S(2)}) collective-permute-start(bf16[4,128,5632]{2,1,0:T(8,128)(2,1)} %bitcast.145), channel_id=1, source_target_pairs={{0,4},{4,0},{1,5},{5,1},{2,6},{6,2},{3,7},{7,3},{8,12},{12,8},{9,1... | collective-permute-start | bytes 17301512 | tf_op jit(solution)/shard_map/ppermute | solution.py:443
  186.7 90.9 %collective-permute-start.5 = (bf16[2816,512]{1,0:T(8,128)(2,1)}, bf16[2816,512]{1,0:T(8,128)(2,1)}, u32[]{:S(2)}, u32[]{:S(2)}) collective-permute-start(bf16[2816,512]{1,0:T(8,128)(2,1)} %all-gather.6.cloned.1.call-done), channel_id=1, source_target_pairs={{0,4},{4,0},{1,5},{5,1},{2,6},{6,2},{3,7},{7,3},{8,12},{12,8},{9,1... | collective-permute-start | bytes 8650760 | tf_op jit(solution)/shard_map/ppermute | solution.py:443
  214.6 27.4 %collective-permute-start.2 = (f32[1,4,264,128]{3,2,1,0:T(8,128)}, f32[1,4,264,128]{3,2,1,0:T(8,128)}, u32[]{:S(2)}, u32[]{:S(2)}) collective-permute-start(f32[1,4,264,128]{3,2,1,0:T(8,128)} %get-tuple-element.32), channel_id=1, source_target_pairs={{0,2},{1,3},{4,6},{5,7},{8,10},{9,11},{12,14},{13,15},{16,18},{17,... | collective-permute-start | bytes 1622024 | tf_op jit(solution)/shard_map/ppermute | solution.py:414
  218.8 23.3 %collective-permute-start.1 = (f32[1,4,264,128]{3,2,1,0:T(8,128)}, f32[1,4,264,128]{3,2,1,0:T(8,128)}, u32[]{:S(2)}, u32[]{:S(2)}) collective-permute-start(f32[1,4,264,128]{3,2,1,0:T(8,128)} %get-tuple-element.32), channel_id=1, source_target_pairs={{0,1},{1,2},{2,3},{4,5},{5,6},{6,7},{8,9},{9,10},{10,11},{12,13},{... | collective-permute-start | bytes 1622024 | tf_op jit(solution)/shard_map/ppermute | solution.py:414
  222.2 22.9 %collective-permute-start.3 = (f32[1,4,264,128]{3,2,1,0:T(8,128)}, f32[1,4,264,128]{3,2,1,0:T(8,128)S(1)}, u32[]{:S(2)}, u32[]{:S(2)}) collective-permute-start(f32[1,4,264,128]{3,2,1,0:T(8,128)} %get-tuple-element.32), channel_id=1, source_target_pairs={{0,3},{4,7},{8,11},{12,15},{16,19},{20,23},{24,27},{28,31}} | collective-permute-start | bytes 1622024 | tf_op jit(solution)/shard_map/ppermute | solution.py:414
  306.6 44.0 %collective-permute-start.13 = (bf16[2816,512]{1,0:T(8,128)(2,1)}, bf16[2816,512]{1,0:T(8,128)(2,1)S(1)}, u32[]{:S(2)}, u32[]{:S(2)}) collective-permute-start(bf16[2816,512]{1,0:T(8,128)(2,1)} %convolution_convert_fusion.1), channel_id=1, source_target_pairs={{0,4},{4,0},{1,5},{5,1},{2,6},{6,2},{3,7},{7,3},{8,12},{12,8},{9,1... | collective-permute-start | bytes 8650760 | tf_op jit(solution)/shard_map/ppermute | solution.py:443
  315.3 17.9 %collective-permute-start.8 = (bf16[1,4,264,128]{3,2,1,0:T(8,128)(2,1)S(1)}, bf16[1,4,264,128]{3,2,1,0:T(8,128)(2,1)S(1)}, u32[]{:S(2)}, u32[]{:S(2)}) collective-permute-start(bf16[1,4,264,128]{3,2,1,0:T(8,128)(2,1)S(1)} %pad_maximum_fusion.9), channel_id=1, source_target_pairs={{3,0},{7,4},{11,8},{15,12},{19,16},{23,20},{27,24},{31,28}} | collective-permute-start | bytes 811016 | tf_op jit(solution)/shard_map/ppermute | solution.py:414
  316.8 16.3 %collective-permute-start.7 = (bf16[1,4,264,128]{3,2,1,0:T(8,128)(2,1)S(1)}, bf16[1,4,264,128]{3,2,1,0:T(8,128)(2,1)S(1)}, u32[]{:S(2)}, u32[]{:S(2)}) collective-permute-start(bf16[1,4,264,128]{3,2,1,0:T(8,128)(2,1)S(1)} %pad_maximum_fusion.9), channel_id=1, source_target_pairs={{2,0},{3,1},{6,4},{7,5},{10,8},{11,9},{14,12},{15,13},{18,16},{19,... | collective-permute-start | bytes 811016 | tf_op jit(solution)/shard_map/ppermute | solution.py:414
  318.1 10.8 %collective-permute-start.6 = (bf16[1,4,264,128]{3,2,1,0:T(8,128)(2,1)S(1)}, bf16[1,4,264,128]{3,2,1,0:T(8,128)(2,1)S(1)}, u32[]{:S(2)}, u32[]{:S(2)}) collective-permute-start(bf16[1,4,264,128]{3,2,1,0:T(8,128)(2,1)S(1)} %pad_maximum_fusion.9), channel_id=1, source_target_pairs={{1,0},{2,1},{3,2},{5,4},{6,5},{7,6},{9,8},{10,9},{11,10},{13,12},{... | collective-permute-start | bytes 811016 | tf_op jit(solution)/shard_map/ppermute | solution.py:414
  350.5 7.5 collective-permute-start.9
  354.6 97.8 %reduce-scatter.4.cloned.1.call-start = ((), (), s32[]{:S(2)}) async-start(), calls=%async_computation.5 | async-start | bytes 5242880 | tf_op jit(solution)/shard_map/reduce_scatter | solution.py:472
  366.8 154.6 %reduce-scatter.6.cloned.1.call-start = ((), (), s32[]{:S(2)}) async-start(), calls=%async_computation.6 | async-start | bytes 7208960 | tf_op jit(solution)/shard_map/reduce_scatter | solution.py:472
  373.5 9.5 %collective-permute-start.11 = (bf16[512,5632]{1,0:T(8,128)(2,1)S(1)}, bf16[512,5632]{1,0:T(8,128)(2,1)S(1)}, u32[]{:S(2)}, u32[]{:S(2)}) collective-permute-start(bf16[512,5632]{1,0:T(8,128)(2,1)S(1)} %convolution_convert_fusion), channel_id=1, source_target_pairs={{0,4},{4,0},{1,5},{5,1},{2,6},{6,2},{3,7},{7,3},{8,12},{12,8},{9,1... | collective-permute-start | bytes 17301512 | tf_op jit(solution)/shard_map/ppermute | solution.py:443
  389.0 259.1 %all-reduce.7.cloned.1.call-start = ((), (), s32[]{:S(2)}) async-start(), calls=%async_computation.10 | async-start | bytes 6422528 | tf_op jit(solution)/shard_map/psum | solution.py:627
  521.4 252.3 %all-reduce.5.cloned.1.call-start = ((), (), s32[]{:S(2)}) async-start(), calls=%async_computation.4 | async-start | bytes 221184 | tf_op jit(solution)/shard_map/psum | solution.py:637
  648.1 145.0 %collective-permute-start.10 = (bf16[128,4096]{1,0:T(8,128)(2,1)}, bf16[128,4096]{1,0:T(8,128)(2,1)S(1)}, u32[]{:S(2)}, u32[]{:S(2)}) collective-permute-start(bf16[128,4096]{1,0:T(8,128)(2,1)} %get-tuple-element.64), channel_id=1, source_target_pairs={{0,4},{4,0},{1,5},{5,1},{2,6},{6,2},{3,7},{7,3},{8,12},{12,8},{9,1... | collective-permute-start | bytes 3145736 | tf_op jit(solution)/shard_map/ppermute | solution.py:443
  648.7 140.4 %collective-permute-start.14 = (bf16[704,512]{1,0:T(8,128)(2,1)}, bf16[704,512]{1,0:T(8,128)(2,1)}, u32[]{:S(2)}, u32[]{:S(2)}) collective-permute-start(bf16[704,512]{1,0:T(8,128)(2,1)} %get-tuple-element.66), channel_id=1, source_target_pairs={{0,4},{4,0},{1,5},{5,1},{2,6},{6,2},{3,7},{7,3},{8,12},{12,8},{9,1... | collective-permute-start | bytes 2162696 | tf_op jit(solution)/shard_map/ppermute | solution.py:443
  653.8 139.3 %copy-start.35 = (bf16[128,4096]{1,0:T(8,128)(2,1)S(1)}, bf16[128,4096]{1,0:T(8,128)(2,1)}, u32[]{:S(2)}) copy-start(bf16[128,4096]{1,0:T(8,128)(2,1)} %get-tuple-element.64) | copy-start | bytes 3145732
  787.4 9.0 %collective-permute-start.12 = (bf16[128,5632]{1,0:T(8,128)(2,1)S(1)}, bf16[128,5632]{1,0:T(8,128)(2,1)S(1)}, u32[]{:S(2)}, u32[]{:S(2)}) collective-permute-start(bf16[128,5632]{1,0:T(8,128)(2,1)S(1)} %copy-done.33), channel_id=1, source_target_pairs={{0,4},{4,0},{1,5},{5,1},{2,6},{6,2},{3,7},{7,3},{8,12},{12,8},{9,1... | collective-permute-start | bytes 4325384 | tf_op jit(solution)/shard_map/ppermute | solution.py:443
  (45 other events, 580.7 us)
Sparse Core Ops, SparseCore 0:
  17.6 56.4 all-gather.7
  76.6 65.7 all-gather.9
  144.8 41.7 all-gather.5
  354.7 42.1 reduce-scatter.7
  399.7 52.6 reduce-scatter.3
  455.6 65.7 reduce-scatter.5
  524.2 123.8 all-reduce.6
  654.2 119.4 all-reduce.4

commit v3 on v2

v3 whole, which is shorter than its diff:
```python
import functools

import jax
import jax.numpy as jnp
from jax import lax
from jax.experimental import pallas as pl
from jax.experimental.pallas import tpu as pltpu
from jax.sharding import Mesh, PartitionSpec as P

HEADS = 4
DK = 128
DV = 256
PAIR = HEADS // 2
CHUNK = 128
SAFE = 60.0


epsilon = 1e-06
normalizer = 16.0
highest_precision = lax.Precision.HIGHEST


def normalize(values_in):
    return values_in * lax.rsqrt(jnp.mean(values_in * values_in, axis=-1, keepdims=True) + epsilon)


def dot_nn(left, right):
    return lax.dot_general(left, right, (((1,), (0,)), ((), ())), preferred_element_type=jnp.float32)


def dot_nt(left, right):
    return lax.dot_general(left, right, (((1,), (1,)), ((), ())), preferred_element_type=jnp.float32)


def dot_tn(left, right):
    return lax.dot_general(left, right, (((0,), (0,)), ((), ())), preferred_element_type=jnp.float32)


def low(array):
    return array.astype(jnp.bfloat16)


def exact_sum(selector, array):
    high = low(array)
    rest = low(array - high.astype(jnp.float32))
    return dot_nn(selector, high) + dot_nn(selector, rest)


def halves(array):
    high = low(array)
    return high, low(array - high.astype(jnp.float32))


def close_dot(dot, left, right):
    (left_high, left_rest), (right_high, right_rest) = halves(left), halves(right)
    return dot(left_high, right_high) + (dot(left_high, right_rest) + dot(left_rest, right_high))


def at_head(refs, head, size):
    place = head % PAIR
    return refs[head // PAIR][:, place * size : (place + 1) * size]


def positions(chunk):
    row = lax.broadcasted_iota(jnp.int32, (chunk, chunk), 0)
    column = lax.broadcasted_iota(jnp.int32, (chunk, chunk), 1)
    return row, column


def as_selector(mask):
    return low(jnp.where(mask, 1.0, 0.0))


def halvings(chunk):
    sizes, half = [], chunk // 2
    while half >= 1:
        sizes.append(half)
        half //= 2
    return sizes


def halving_parts(chunk, half):
    row, column = positions(chunk)
    row_late = (row & half) != 0
    pairs = ((row & -(2 * half)) == (column & -(2 * half))) & row_late & ((column & half) == 0)
    middle = (row & -(2 * half)) + (half - 1)
    late = row_late & (column > middle) & (column <= row)
    early = jnp.logical_not(row_late) & (column > row) & (column <= middle)
    return pairs, as_selector(late | early)


def scan_forward_kernel(chunk, q0, k0, v0, q1, k1, v1, g_ref, o_ref, qf_ref, a_ref, st_ref, cs_ref, sum_ref, state, start, table):
    step, steps = pl.program_id(1), pl.num_programs(1)
    q_refs, k_refs, v_refs = (q0, q1), (k0, k1), (v0, v1)

    @pl.when(step == 0)
    def _():
        state[...] = jnp.zeros_like(state)
        start[...] = jnp.zeros_like(start)

    row, column = positions(chunk)
    gates = g_ref[...]
    cumul = exact_sum(as_selector(row >= column), gates)
    left = exact_sum(as_selector(row < column), gates)
    finish = cumul[chunk - 1 : chunk, :]
    mild = jnp.min(finish) > -SAFE
    begin = start[...]
    cs_ref[0] = begin
    grown = jnp.exp(cumul)
    faded = jnp.exp(left)
    begun = jnp.exp(begin)
    kept = jnp.exp(finish)
    scale = DK ** (-0.5)

    @pl.when(mild)
    def _():
        for h in range(HEADS):
            ks = slice(h * DK, (h + 1) * DK)
            far = at_head(q_refs, h, DK) * scale * grown[:, ks]
            near = at_head(k_refs, h, DK) * jnp.exp(-cumul[:, ks])
            table[h] = jnp.where(row >= column, close_dot(dot_nt, far, near), 0.0)

    @pl.when(jnp.logical_not(mild))
    def _():
        for h in range(HEADS):
            ks = slice(h * DK, (h + 1) * DK)
            queries, keys, decay = at_head(q_refs, h, DK) * scale, at_head(k_refs, h, DK), g_ref[:, ks]
            total = jnp.where(row == column, close_dot(dot_nt, queries, keys), 0.0)
            for half in halvings(chunk):
                pairs, selector = halving_parts(chunk, half)
                factor = jnp.exp(exact_sum(selector, decay))
                total = jnp.where(pairs, close_dot(dot_nt, queries * factor, keys * factor), total)
            table[h] = total

    for h in range(HEADS):
        ks, vs = slice(h * DK, (h + 1) * DK), slice(h * DV, (h + 1) * DV)
        queries = at_head(q_refs, h, DK) * scale * grown[:, ks]
        own_values = at_head(v_refs, h, DV)
        values = low(own_values)
        held = state[h]
        st_ref[0, h] = held
        scores = table[h]
        a_ref[0, h] = low(scores)
        o_ref[:, vs] = close_dot(dot_nn, scores, own_values) + dot_nt(low(queries), low(held))
        qf_ref[:, ks] = low(queries * begun[:, ks])
        state[h] = held * kept[:, ks] + dot_tn(values, low(at_head(k_refs, h, DK) * faded[:, ks]))
    start[...] = begin + finish

    @pl.when(step == steps - 1)
    def _():
        for h in range(HEADS):
            ks = slice(h * DK, (h + 1) * DK)
            sum_ref[0, h, :DV] = state[h]
            sum_ref[0, h, DV:] = jnp.broadcast_to(jnp.exp(begin[:, ks] + finish[:, ks]), (8, DK))


def scan_backward_kernel(
    chunk, q0, k0, v0, q1, k1, v1, g_ref, a_ref, st_ref, cs_ref, in_ref, do_ref, later_ref, dog0, dog1,
    out0, out1, dg_ref, later, dqi, dki, dci,
):
    q_refs, k_refs, v_refs = (q0, q1), (k0, k1), (v0, v1)

    @pl.when(pl.program_id(1) == 0)
    def _():
        later[...] = later_ref[0]

    row, column = positions(chunk)
    lower = row >= column
    gates = g_ref[...]
    cumul = exact_sum(as_selector(lower), gates)
    left = exact_sum(as_selector(row < column), gates)
    finish = cumul[chunk - 1 : chunk, :]
    mild = jnp.min(finish) > -SAFE
    grown = jnp.exp(cumul)
    faded = jnp.exp(left)
    kept = jnp.exp(finish)
    begun = jnp.exp(cs_ref[0])
    scale = DK ** (-0.5)

    def overlap(h, vs):
        return close_dot(dot_nt, do_ref[:, vs], at_head(v_refs, h, DV))

    @pl.when(mild)
    def _():
        for h in range(HEADS):
            ks, vs = slice(h * DK, (h + 1) * DK), slice(h * DV, (h + 1) * DV)
            shrunk = jnp.exp(-cumul[:, ks])
            far = low(at_head(q_refs, h, DK) * scale * grown[:, ks])
            near = low(at_head(k_refs, h, DK) * shrunk)
            pairs = low(jnp.where(lower, overlap(h, vs), 0.0))
            for_q, for_k = dot_nn(pairs, near), dot_tn(pairs, far)
            dqi[:, ks] = grown[:, ks] * for_q
            dki[:, ks] = shrunk * for_k
            dci[:, ks] = far.astype(jnp.float32) * for_q - near.astype(jnp.float32) * for_k

    @pl.when(jnp.logical_not(mild))
    def _():
        for h in range(HEADS):
            ks, vs = slice(h * DK, (h + 1) * DK), slice(h * DV, (h + 1) * DV)
            queries, keys, decay = at_head(q_refs, h, DK) * scale, at_head(k_refs, h, DK), g_ref[:, ks]
            both = overlap(h, vs)
            pairs = low(jnp.where(row == column, both, 0.0))
            grad_q, grad_k = dot_nn(pairs, low(keys)), dot_tn(pairs, low(queries))
            grad_c = jnp.zeros_like(grad_q)
            for half in halvings(chunk):
                here, selector = halving_parts(chunk, half)
                factor = jnp.exp(exact_sum(selector, decay))
                far, near = low(queries * factor), low(keys * factor)
                pairs = low(jnp.where(here, both, 0.0))
                for_q, for_k = dot_nn(pairs, near), dot_tn(pairs, far)
                grad_q += factor * for_q
                grad_k += factor * for_k
                grad_c += far.astype(jnp.float32) * for_q - near.astype(jnp.float32) * for_k
            dqi[:, ks] = grad_q
            dki[:, ks] = grad_k
            dci[:, ks] = grad_c

    before = as_selector(row > column)
    after = as_selector(row <= column)
    for h in range(HEADS):
        ks, vs = slice(h * DK, (h + 1) * DK), slice(h * DV, (h + 1) * DV)
        values, grad_out = low(at_head(v_refs, h, DV)), low(do_ref[:, vs])
        held = st_ref[0, h] + in_ref[0, h] * begun[:, ks]
        ahead = later[h]
        ahead_low = low(ahead)
        queries = at_head(q_refs, h, DK) * scale * grown[:, ks]
        keys = at_head(k_refs, h, DK) * faded[:, ks]
        out_ref, place = (out0, out1)[h // PAIR], h % PAIR
        from_state = dot_nn(grad_out, low(held))
        from_later = dot_nn(values, ahead_low)
        out_ref[:, place * DK : (place + 1) * DK] = low((dqi[:, ks] + grown[:, ks] * from_state) * scale)
        out_ref[:, KEYS // 2 + place * DK : KEYS // 2 + (place + 1) * DK] = low(dki[:, ks] + faded[:, ks] * from_later)
        out_ref[:, KEYS + place * DV : KEYS + (place + 1) * DV] = low(
            dot_tn(a_ref[0, h], grad_out) + dot_nt(low(keys), ahead_low)
        )
        through = kept[:, ks] * jnp.sum(held * ahead, axis=0, keepdims=True)
        dg_ref[:, ks] = (
            exact_sum(after, dci[:, ks] + queries * from_state)
            + exact_sum(before, keys * from_later)
            + through
        )
        later[h] = ahead * kept[:, ks] + dot_tn(grad_out, low(queries))
    out0[:, KEYS + VALUES // 2 :] = dog0[...]
    out1[:, KEYS + VALUES // 2 :] = dog1[...]


def mix_forward_kernel(o_ref, qf_ref, in_ref, og0, og1, gain_ref, att_ref, mixed_ref):
    gain = gain_ref[...]
    for h in range(HEADS):
        ks, vs = slice(h * DK, (h + 1) * DK), slice(h * DV, (h + 1) * DV)
        attended = o_ref[:, vs] + dot_nt(qf_ref[:, ks], low(in_ref[0, h]))
        att_ref[:, vs] = attended
        outgate = at_head((og0, og1), h, DV)
        mixed_ref[:, vs] = low(normalize(attended) * gain * (outgate * jax.nn.sigmoid(outgate)))


def mix_backward_kernel(dm_ref, att_ref, og0, og1, gain_ref, qf_ref, do_ref, dog0, dog1, grad_ref, dgain_ref):
    @pl.when(pl.program_id(1) == 0)
    def _():
        grad_ref[...] = jnp.zeros_like(grad_ref)
        dgain_ref[...] = jnp.zeros_like(dgain_ref)

    gain = gain_ref[...]
    for h in range(HEADS):
        ks, vs = slice(h * DK, (h + 1) * DK), slice(h * DV, (h + 1) * DV)
        attended, outgate, grad = att_ref[:, vs], at_head((og0, og1), h, DV), dm_ref[:, vs]
        dog_ref, place = (dog0, dog1)[h // PAIR], h % PAIR
        inverse = lax.rsqrt(jnp.mean(attended * attended, axis=-1, keepdims=True) + epsilon)
        normed = attended * inverse
        sigma = jax.nn.sigmoid(outgate)
        gated = grad * (outgate * sigma)
        dog_ref[:, place * DV : (place + 1) * DV] = low(grad * normed * gain * (sigma + outgate * sigma * (1.0 - sigma)))
        dgain_ref[0] += jnp.sum(gated * normed, axis=0, keepdims=True)
        inner = gated * gain
        result = inverse * (inner - normed * jnp.mean(inner * normed, axis=-1, keepdims=True))
        do_ref[:, vs] = result
        grad_ref[0, h] += dot_tn(low(result), qf_ref[:, ks])


def rows_spec(chunk, chunks, width, backward=False):
    if backward:
        return pl.BlockSpec((chunk, width), lambda s, c: (s * chunks + chunks - 1 - c, 0))
    return pl.BlockSpec((chunk, width), lambda s, c: (s * chunks + c, 0))


def item_spec(shape):
    return pl.BlockSpec((1,) + shape, lambda s, c: (s,) + (0,) * len(shape))


def chunk_spec(chunks, shape, backward=False):
    if backward:
        return pl.BlockSpec((1,) + shape, lambda s, c: (s * chunks + chunks - 1 - c,) + (0,) * len(shape))
    return pl.BlockSpec((1,) + shape, lambda s, c: (s * chunks + c,) + (0,) * len(shape))


def shaped(shape, kind=jnp.float32):
    return jax.ShapeDtypeStruct(shape, kind)


def packed_specs(chunk, chunks, backward=False):
    def at(width, place):
        whole = rows_spec(chunk, chunks, width, backward)
        return pl.BlockSpec(whole.block_shape, lambda s, c: (whole.index_map(s, c)[0], place))

    return [at(KEYS // 2, 0), at(KEYS // 2, 1), at(VALUES // 2, 1), at(VALUES // 2, 2)]


KEYS, VALUES = HEADS * DK, HEADS * DV
PACKED = KEYS + VALUES
ROOM = pltpu.CompilerParams(vmem_limit_bytes=40 * 1024 * 1024)


def scan_forward(mine, theirs, gates, seqs, chunk):
    rows = gates.shape[0]
    chunks = rows // seqs // chunk
    keyed, valued = rows_spec(chunk, chunks, KEYS), rows_spec(chunk, chunks, VALUES)
    return pl.pallas_call(
        functools.partial(scan_forward_kernel, chunk),
        grid=(seqs, chunks),
        in_specs=packed_specs(chunk, chunks)[:3] * 2 + [keyed],
        out_specs=[
            valued,
            keyed,
            chunk_spec(chunks, (HEADS, chunk, chunk)),
            chunk_spec(chunks, (HEADS, DV, DK)),
            chunk_spec(chunks, (1, KEYS)),
            item_spec((HEADS, DV + 8, DK)),
        ],
        out_shape=[
            shaped((rows, VALUES)),
            shaped((rows, KEYS), jnp.bfloat16),
            shaped((seqs * chunks, HEADS, chunk, chunk), jnp.bfloat16),
            shaped((seqs * chunks, HEADS, DV, DK)),
            shaped((seqs * chunks, 1, KEYS)),
            shaped((seqs, HEADS, DV + 8, DK)),
        ],
        scratch_shapes=[
            pltpu.VMEM((HEADS, DV, DK), jnp.float32),
            pltpu.VMEM((1, KEYS), jnp.float32),
            pltpu.VMEM((HEADS, chunk, chunk), jnp.float32),
        ],
        compiler_params=ROOM,
        name="scan_forward",
    )(mine, mine, mine, theirs, theirs, theirs, gates)


def scan_backward(
    mine, theirs, gates, scores, states, starts, incoming, grad_out, later, outgate_grads, seqs, chunk
):
    rows = gates.shape[0]
    chunks = rows // seqs // chunk
    keyed, valued = rows_spec(chunk, chunks, KEYS, True), rows_spec(chunk, chunks, VALUES, True)
    return pl.pallas_call(
        functools.partial(scan_backward_kernel, chunk),
        grid=(seqs, chunks),
        in_specs=[
            *packed_specs(chunk, chunks, True)[:3] * 2,
            keyed,
            chunk_spec(chunks, (HEADS, chunk, chunk), True),
            chunk_spec(chunks, (HEADS, DV, DK), True),
            chunk_spec(chunks, (1, KEYS), True),
            item_spec((HEADS, DV, DK)),
            valued,
            item_spec((HEADS, DV, DK)),
            *[rows_spec(chunk, chunks, VALUES // 2, True)] * 2,
        ],
        out_specs=[*[rows_spec(chunk, chunks, PACKED, True)] * 2, keyed],
        out_shape=[*[shaped((rows, PACKED), jnp.bfloat16)] * 2, shaped((rows, KEYS))],
        scratch_shapes=[pltpu.VMEM((HEADS, DV, DK), jnp.float32)] + [pltpu.VMEM((chunk, KEYS), jnp.float32)] * 3,
        compiler_params=ROOM,
        name="scan_backward",
    )(
        mine, mine, mine, theirs, theirs, theirs,
        gates, scores, states, starts, incoming, grad_out, later, *outgate_grads,
    )


def mix_forward(local_out, forget, incoming, mine, theirs, gain, seqs, chunk):
    rows = local_out.shape[0]
    chunks = rows // seqs // chunk
    keyed, valued = rows_spec(chunk, chunks, KEYS), rows_spec(chunk, chunks, VALUES)
    whole_gain = pl.BlockSpec((1, DV), lambda s, c: (0, 0))
    return pl.pallas_call(
        mix_forward_kernel,
        grid=(seqs, chunks),
        in_specs=[valued, keyed, item_spec((HEADS, DV, DK)), *packed_specs(chunk, chunks)[3:] * 2, whole_gain],
        out_specs=[valued, valued],
        out_shape=[shaped((rows, VALUES)), shaped((rows, VALUES), jnp.bfloat16)],
        compiler_params=ROOM,
        name="mix_forward",
    )(local_out, forget, incoming, mine, theirs, gain)


def mix_backward(mixed_grad, attended, mine, theirs, gain, forget, seqs, chunk):
    rows = attended.shape[0]
    chunks = rows // seqs // chunk
    keyed, valued = rows_spec(chunk, chunks, KEYS), rows_spec(chunk, chunks, VALUES)
    whole_gain = pl.BlockSpec((1, DV), lambda s, c: (0, 0))
    return pl.pallas_call(
        mix_backward_kernel,
        grid=(seqs, chunks),
        in_specs=[valued, valued, *packed_specs(chunk, chunks)[3:] * 2, whole_gain, keyed],
        out_specs=[
            valued,
            *[rows_spec(chunk, chunks, VALUES // 2)] * 2,
            item_spec((HEADS, DV, DK)),
            item_spec((1, DV)),
        ],
        out_shape=[
            shaped((rows, VALUES)),
            *[shaped((rows, VALUES // 2), jnp.bfloat16)] * 2,
            shaped((seqs, HEADS, DV, DK)),
            shaped((seqs, 1, DV)),
        ],
        compiler_params=ROOM,
        name="mix_backward",
    )(mixed_grad, attended, mine, theirs, gain, forget)


def from_neighbours(summary, step):
    count = lax.axis_size("seq")
    total, factor = None, None
    for distance in range(1, count):
        shift = step * distance
        pairs = [(i, i + shift) for i in range(count) if 0 <= i + shift < count]
        came = lax.ppermute(summary, "seq", pairs)
        state, retain = came[:, :, :DV].astype(jnp.float32), came[:, :, DV : DV + 1].astype(jnp.float32)
        if total is None:
            total, factor = state, retain
        else:
            total, factor = total + factor * state, factor * retain
    return total


def product(left, right):
    return jnp.dot(left, right, preferred_element_type=jnp.float32)


def product_left(left, right):
    return lax.dot_general(
        left, right, (((0,), (0,)), ((), ())), preferred_element_type=jnp.float32
    )


def product_right(left, right):
    return lax.dot_general(
        left, right, (((1,), (1,)), ((), ())), preferred_element_type=jnp.float32
    )


EVERYWHERE = ("z", "core", "seq")


def swapped(array):
    return lax.ppermute(array, "core", [(0, 1), (1, 0)])


def after(array, other):
    def nothing(array_ref, other_ref, out_ref):
        pass

    anywhere = pl.BlockSpec(memory_space=pl.ANY)
    return pl.pallas_call(
        nothing,
        in_specs=[anywhere, anywhere],
        out_specs=anywhere,
        out_shape=shaped(array.shape, array.dtype),
        input_output_aliases={0: 0},
        name="after",
    )(array, other)


def first_core():
    return lax.axis_index("core") == 0


def own_half(array, dim, other=False):
    core = lax.axis_index("core")
    size = array.shape[dim] // 2
    return lax.dynamic_slice_in_dim(array, ((1 - core) if other else core) * size, size, dim)


def joined(mine, theirs, dim):
    return jnp.where(
        first_core(), jnp.concatenate([mine, theirs], dim), jnp.concatenate([theirs, mine], dim)
    )


def halves_of(array):
    half = array.shape[1] // 2
    first = first_core()
    return (
        jnp.where(first, array[:, :half], array[:, half:]),
        jnp.where(first, array[:, half:], array[:, :half]),
    )


def scattered(array):
    return lax.psum_scatter(array, "seq", scatter_dimension=0, tiled=True)


def line_sum(array):
    count, me = lax.axis_size("z"), lax.axis_index("z")
    if count % 2:
        return (lax.psum(array, "z"),) * 2
    middle = count // 2
    total = array

    def send(pairs):
        return lax.ppermute(total, "z", pairs)

    for step in range(middle - 1):
        came = send([(step, step + 1), (count - 1 - step, count - 2 - step)])
        total = low(total.astype(jnp.float32) + came.astype(jnp.float32))
    came = send([(middle - 1, middle), (middle, middle - 1)])
    total = low(total.astype(jnp.float32) + came.astype(jnp.float32))
    at_middle = total
    for step in reversed(range(middle - 1)):
        came = send([(step + 1, step), (count - 2 - step, count - 1 - step)])
        total = jnp.where((me == step) | (me == count - 1 - step), came, total)
    return total, at_middle


def local(
    tokens,
    mixer_gain,
    query_weight,
    key_weight,
    value_weight,
    decay_down,
    decay_up,
    decay_bias,
    outgate_weight,
    head_gain,
    output_weight,
    channel_gain,
    gate_weight,
    up_weight,
    down_weight,
    cotangent,
):
    seqs_here, seg_len, width = tokens.shape
    rows_here = seqs_here * seg_len
    count = lax.axis_size("seq")
    ff = gate_weight.shape[1]

    shard_rows = query_weight.shape[0]
    smalls = [mixer_gain, decay_down, decay_up, decay_bias, head_gain, channel_gain]
    flat = jnp.concatenate([small.reshape(-1) for small in smalls])
    flat_size = flat.size
    extra = -(-flat_size // (shard_rows * 128)) * 128
    flat = jnp.pad(flat, (0, shard_rows * extra - flat_size)).reshape(shard_rows, extra)
    mixer_packed = jnp.concatenate(
        [
            own_half(weight, 1)
            for weight in (query_weight, key_weight, value_weight, outgate_weight, output_weight)
        ]
        + [flat],
        axis=1,
    )
    ffn_packed = jnp.concatenate([own_half(gate_weight, 1), own_half(up_weight, 1)], axis=1)
    down_packed = own_half(down_weight, 1)
    wide = PACKED + width // 2
    mixer_mine = lax.all_gather(mixer_packed, "seq", tiled=True)
    ffn_mine = lax.all_gather(ffn_packed, "seq", tiled=True)
    down_mine = lax.all_gather(down_packed, "seq", tiled=True)
    mixer_theirs = swapped(mixer_mine)
    projection_mine, projection_theirs = mixer_mine[:, :PACKED], mixer_theirs[:, :PACKED]
    output_mine, output_theirs = mixer_mine[:, PACKED:wide], mixer_theirs[:, PACKED:wide]
    small_all = mixer_mine[:, wide:].reshape(count, -1)
    pieces, begin = [], 0
    for small in smalls:
        pieces.append(small_all[:, begin : begin + small.size].reshape((count,) + small.shape))
        begin += small.size
    gain_one = pieces[0].reshape(-1).astype(jnp.float32)
    decay_down_all = pieces[1].reshape(width, -1)
    decay_up_f = pieces[2].transpose(1, 0, 2).reshape(decay_up.shape[0], -1).astype(jnp.float32)
    decay_bias_f = pieces[3].reshape(1, -1).astype(jnp.float32)
    head_gain_f = pieces[4].reshape(-1).astype(jnp.float32)
    gain_two = pieces[5].reshape(-1).astype(jnp.float32)
    decay_up_f = jnp.concatenate(halves_of(decay_up_f), 1)
    decay_bias_f = jnp.concatenate(halves_of(decay_bias_f), 1)

    inputs = tokens.reshape(rows_here, width).astype(jnp.float32)

    def first_norm(inputs_in, gain_in):
        return normalize(inputs_in) * gain_in

    normed_one = first_norm(inputs, gain_one).astype(jnp.bfloat16)
    low_rank = product(normed_one, decay_down_all)

    def gate_fn(rank_in, up_in, bias_in):
        return (
            jax.nn.log_sigmoid(jnp.dot(rank_in, up_in, precision=highest_precision) + bias_in)
            / normalizer
        )

    gates = gate_fn(low_rank, decay_up_f, decay_bias_f)
    mine = product(normed_one, projection_mine)
    theirs = product(normed_one, projection_theirs)
    chunk = min(CHUNK, seg_len)
    local_out, forget, scores, states, starts, summary = scan_forward(mine, theirs, gates, seqs_here, chunk)
    incoming_state = from_neighbours(summary, 1)
    attended, mixed = mix_forward(
        local_out, forget, incoming_state, mine, theirs, head_gain_f[None, :], seqs_here, chunk
    )
    ffn_mine = after(ffn_mine, mixed)
    mixed = jnp.concatenate(halves_of(mixed), 1)
    resid = inputs + joined(product(mixed, output_mine), product(mixed, output_theirs), 1)
    normed_two = first_norm(resid, gain_two).astype(jnp.bfloat16)
    ffn_theirs = swapped(ffn_mine)

    def swiglu(both):
        gate_pre, up_pre = both[:, : ff // 2], both[:, ff // 2 :]
        return low(gate_pre * jax.nn.sigmoid(gate_pre) * up_pre)

    both_mine, both_theirs = product(normed_two, ffn_mine), product(normed_two, ffn_theirs)
    hidden = joined(swiglu(both_mine), swiglu(both_theirs), 1)
    down_mine = after(down_mine, normed_two)
    down_theirs = swapped(down_mine)
    result = resid + joined(product(hidden, down_mine), product(hidden, down_theirs), 1)
    block_out = result.astype(jnp.bfloat16).reshape(tokens.shape)

    grad_low = cotangent.reshape(rows_here, width)
    grad_out = grad_low.astype(jnp.float32)
    low_mine, low_theirs = halves_of(grad_low)
    down_came = swapped(low(product_left(hidden, low_theirs)))
    hidden_grad = product_right(low_mine, down_mine) + product_right(low_theirs, down_theirs)

    def swiglu_back(both, grad):
        gate_pre, up_pre = both[:, : ff // 2], both[:, ff // 2 :]
        sigma = jax.nn.sigmoid(gate_pre)
        return jnp.concatenate(
            [
                low(grad * up_pre * (sigma + gate_pre * sigma * (1.0 - sigma))),
                low(grad * (gate_pre * sigma)),
            ],
            axis=1,
        )

    grad_mine, grad_theirs = halves_of(hidden_grad)
    back_mine, back_theirs = swiglu_back(both_mine, grad_mine), swiglu_back(both_theirs, grad_theirs)
    down_pair = low(product_left(hidden, low_mine) + down_came.astype(jnp.float32))
    down_share = scattered(down_pair)

    ffn_came = swapped(low(product_left(normed_two, back_theirs)))
    normed_two_grad = product_right(back_mine, ffn_mine) + product_right(back_theirs, ffn_theirs)
    norm_pulled = jax.vjp(first_norm, resid, gain_two)[1](normed_two_grad)
    resid_grad = grad_out + norm_pulled[0]
    channel_gain_grad = norm_pulled[1]
    branch_grad = resid_grad.astype(jnp.bfloat16)
    branch_mine, branch_theirs = halves_of(branch_grad)
    mixed_grad = product_right(branch_mine, output_mine) + product_right(branch_theirs, output_theirs)
    mixed_grad = jnp.concatenate(halves_of(mixed_grad), 1)
    ffn_pair = low(product_left(normed_two, back_mine) + ffn_came.astype(jnp.float32))
    ffn_share = scattered(ffn_pair)
    mixed_grad = after(mixed_grad, ffn_pair)

    attended_grad, *outgate_grads, state_grad, head_gain_grad = mix_backward(
        mixed_grad, attended, mine, theirs, head_gain_f[None, :], forget, seqs_here, chunk
    )
    head_gain_grad = head_gain_grad.sum((0, 1))
    later_grad = from_neighbours(
        jnp.concatenate([state_grad, summary[:, :, DV:]], axis=2).astype(jnp.bfloat16), -1
    )
    packed_mine, packed_theirs, gates_grad = scan_backward(
        mine, theirs, gates, scores, states, starts, incoming_state,
        attended_grad, later_grad, outgate_grads, seqs_here, chunk,
    )
    output_theirs_grad = low(product_left(mixed, branch_theirs))
    packed_came = swapped(
        jnp.concatenate([low(product_left(normed_one, packed_theirs)), output_theirs_grad], axis=1)
    ).astype(jnp.float32)
    gate_pulled = jax.vjp(gate_fn, low_rank, decay_up_f, decay_bias_f)[1](gates_grad)
    low_rank_grad = gate_pulled[0].astype(jnp.bfloat16)
    decay_up_grad = jnp.concatenate(halves_of(gate_pulled[1]), 1)
    decay_bias_grad = jnp.concatenate(halves_of(gate_pulled[2]), 1)[0]
    decay_down_grad = product_left(normed_one, low_rank_grad)
    normed_one_grad = (
        product_right(packed_mine, projection_mine)
        + product_right(packed_theirs, projection_theirs)
        + product_right(low_rank_grad, decay_down_all)
    )
    first_pulled = jax.vjp(first_norm, inputs, gain_one)[1](normed_one_grad)
    tokens_grad = (resid_grad + first_pulled[0]).reshape(tokens.shape)

    def by_shard(grad, dim=0):
        shape = grad.shape[:dim] + (count, grad.shape[dim] // count) + grad.shape[dim + 1 :]
        return jnp.moveaxis(grad.reshape(shape), dim, 0).reshape(count, -1)

    small_grads = jnp.concatenate(
        [
            by_shard(first_pulled[1]),
            by_shard(decay_down_grad),
            by_shard(decay_up_grad, 1),
            by_shard(decay_bias_grad),
            by_shard(head_gain_grad),
            by_shard(channel_gain_grad),
        ],
        axis=1,
    )
    small_grads = jnp.pad(low(small_grads), ((0, 0), (0, shard_rows * extra - flat_size)))
    mixer_pair = jnp.concatenate(
        [
            low(product_left(normed_one, packed_mine) + packed_came[:, :PACKED]),
            low(product_left(mixed, branch_mine) + packed_came[:, PACKED:]),
            small_grads.reshape(count * shard_rows, extra),
        ],
        axis=1,
    )
    mixer_share = scattered(mixer_pair)

    down_total, down_middle = line_sum(down_share)
    down_weight_grad = joined(down_total, swapped(down_total), 1).astype(jnp.float32)
    ffn_total, ffn_middle = line_sum(after(ffn_share, down_middle))
    ffn_other = swapped(ffn_total)
    mixer_total, _ = line_sum(after(mixer_share, ffn_middle))
    mixer_other = swapped(mixer_total)

    def both_cores(total, other, begin, end):
        return joined(total[:, begin:end], other[:, begin:end], 1).astype(jnp.float32)

    summed = mixer_total[:, wide:].astype(jnp.float32) + mixer_other[:, wide:].astype(jnp.float32)
    summed, shares, begin = summed.reshape(-1), [], 0
    for small in smalls:
        shares.append(summed[begin : begin + small.size].reshape(small.shape))
        begin += small.size

    columns = (0, KEYS // 2, KEYS, KEYS + VALUES // 2, PACKED, wide)
    query_g, key_g, value_g, outgate_g, output_g = (
        both_cores(mixer_total, mixer_other, a, b) for a, b in zip(columns[:-1], columns[1:])
    )
    return (
        block_out,
        tokens_grad,
        shares[0],
        query_g,
        key_g,
        value_g,
        shares[1],
        shares[2],
        shares[3],
        outgate_g,
        shares[4],
        output_g,
        shares[5],
        both_cores(ffn_total, ffn_other, 0, ff // 2),
        both_cores(ffn_total, ffn_other, ff // 2, ff),
        down_weight_grad,
    )


def solution(mesh):
    rep, seq = mesh.shape["rep"], mesh.shape["seq"]
    cores = Mesh(mesh.devices.reshape(rep // 2, 2, seq), EVERYWHERE)
    sequences, weights = P(("z", "core"), "seq", None), P("seq", None)
    in_specs = (
        sequences,
        P("seq"),
        weights,
        weights,
        weights,
        weights,
        P(None, "seq"),
        P("seq"),
        weights,
        P("seq"),
        weights,
        P("seq"),
        weights,
        weights,
        weights,
        sequences,
    )
    out_specs = (sequences, *in_specs[:15])
    return jax.shard_map(local, mesh=cores, in_specs=in_specs, out_specs=out_specs, check_vma=False)
```

time: 817 us -> 600 us (0.73)
  waiting for transfers between devices: 555 us -> 282 us
  starting transfers between devices: 15.3 us -> 85.1 us
  local copies, waits for them, and re-layouts: 60.5 us -> 34.1 us
    psum x2 -> x0, waiting for transfers between devices: 229 us -> none  [the longest x1 120 us: local(): lax.psum(jnp.concatenate([grad.reshape(-1) for grad in small_grads]), EVE...]
    ppermute x0 -> x9, waiting for transfers between devices: none -> 125 us  [send(): return lax.ppermute(total, 'z', pairs)]
    reduce_scatter x3, waiting for transfers between devices: 122 us -> 0.02 us  [scattered(): return lax.psum_scatter(array, 'seq', scatter_dimension=0, tiled=True)]
    all_gather x3, waiting for transfers between devices: 163 us -> 90.1 us  [the longest x1 55.1 us: local(): mixer_mine = lax.all_gather(mixer_packed, 'seq', tiled=True)]
    ppermute x0 -> x9, starting transfers between devices: none -> 70.1 us  [send(): return lax.ppermute(total, 'z', pairs)]
    ppermute x6, waiting for transfers between devices: 28.6 us -> 62.8 us  [from_neighbours(): came = lax.ppermute(summary, 'seq', pairs)]
    convert_element_type x7 -> x17, other arithmetic: 11.5 us -> 26.9 us  [the longest x7 12 us: low(): return array.astype(jnp.bfloat16)]
    slice x10 -> x13, local copies, waits for them, and re-layouts: 18.2 us -> 4.17 us  [the longest x6 2.83 us: local(): shares.append(summed[begin:begin + small.size].reshape(small.shape))]
  transfers between devices with their start and end apart: 23 -> 30, of which waited for: 13 -> 14; matrix products, arithmetic and copies ran while one was open for 18% -> 23% of each run, Pallas kernels for 3% -> 4%
where the time goes in v3:
time: 600 us; the launch traced here: 591 us
  waiting for transfers between devices  282 us (47%)
  matrix products  102 us (17%)
  starting transfers between devices  85.1 us (14%)
  other arithmetic  47.1 us (8%)
  local copies, waits for them, and re-layouts  34.1 us (6%)
  Pallas kernels  24.6 us (4%)
  between operations  16 us (3%)
    ppermute x9, waiting for transfers between devices, send(): return lax.ppermute(total, 'z', pairs)  125 us
    ppermute x9, starting transfers between devices, send(): return lax.ppermute(total, 'z', pairs)  70.1 us
    ppermute x6, waiting for transfers between devices, from_neighbours(): came = lax.ppermute(summary, 'seq', pairs)  62.8 us
    all_gather x1, waiting for transfers between devices, local(): mixer_mine = lax.all_gather(mixer_packed, 'seq', tiled=True)  55.1 us
    all_gather x1, waiting for transfers between devices, local(): down_mine = lax.all_gather(down_packed, 'seq', tiled=True)  35 us
    dot_general x9, matrix products, product_right(): lax.dot_general(left, right, (((1,), (1,)), ((), ())), preferred_element_...  33.1 us
    dot_general x9, matrix products, product(): return jnp.dot(left, right, preferred_element_type=jnp.float32)  31.9 us
    dot_general x9, matrix products, product_left(): lax.dot_general(left, right, (((0,), (0,)), ((), ())), preferred_element_...  29.8 us
  transfers between devices with their start and end apart: 30, of which 14 were waited for; matrix products, arithmetic and copies ran while one was open for 23% of the time, Pallas kernels for 4%

profile of v3, /device:TPU:0, one launch (start us, length us, event | category | flops | bytes accessed | tf_op | source)
XLA Modules:
  0.0 590.8 jit_solution(15007134254173060706)
XLA Ops:
  16.9 55.1 %all-gather.4.cloned.1.call-done = bf16[1024,2176]{1,0:T(8,128)(2,1)} async-done(((bf16[256,2176]{1,0:T(8,128)(2,1)}), bf16[1024,2176]{1,0:T(8,128)(2,1)}) %all-gather.4.cloned.1.call-update) | async-done | bytes 4456464 | tf_op jit(solution)/shard_map/all_gather | solution.py:564
  82.6 5.1 fusion.8.q1.k1.v1.og1
  87.8 6.5 %scan_forward.1 = (f32[512,1024]{1,0:T(8,128)S(1)}, bf16[512,512]{1,0:T(8,128)(2,1)S(1)}, bf16[4,4,128,128]{3,2,1,0:T(8,128)(2,1)S(1)}, f32[4,4,256,128]{3,2,1,0...) custom-call(f32[512,1536]{1,0:T(8,128)S(1)} %fusion.12.q0.k0.v0.og0, ...), custom_call_target="tpu_custom_call" | custom-call | tf_op jit(solution)/shard_map/scan_forward/pallas_call | solution.py:317
  109.1 26.0 %collective-permute-done.2 = f32[1,4,264,128]{3,2,1,0:T(8,128)} collective-permute-done((f32[1,4,264,128]{3,2,1,0:T(8,128)}, f32[1,4,264,128]{3,2,1,0:T(8,128)}, u32[]{:S(2)}, u32[]{:S(2)}) %collective-permute-start.2) | collective-permute-done | bytes 540704 | tf_op jit(solution)/shard_map/ppermute | solution.py:426
  135.8 15.9 %collective-permute-done.3 = f32[1,4,264,128]{3,2,1,0:T(8,128)} collective-permute-done((f32[1,4,264,128]{3,2,1,0:T(8,128)}, f32[1,4,264,128]{3,2,1,0:T(8,128)}, u32[]{:S(2)}, u32[]{:S(2)}) %collective-permute-start.3) | collective-permute-done | bytes 540704 | tf_op jit(solution)/shard_map/ppermute | solution.py:426
  170.5 35.0 %all-gather.8.cloned.1.call-done.array_ref = bf16[2816,512]{1,0:T(8,128)(2,1)} async-done(((bf16[704,512]{1,0:T(8,128)(2,1)}), bf16[2816,512]{1,0:T(8,128)(2,1)}) %all-gather.8.cloned.1.call-update) | async-done | bytes 2883600 | tf_op jit(solution)/shard_map/all_gather | solution.py:566
  209.4 5.9 fusion.98
  217.1 5.8 fusion.99
  232.0 5.1 convolution_convert_fusion
  246.8 10.0 %add_convert_fusion.other_ref = bf16[1024,2816]{1,0:T(8,128)(2,1)} fusion(bf16[1024,2816]{1,0:T(8,128)(2,1)} %collective-permute-done.6, bf16[512,1024]{1,0:T(8,128)(2,1)} %multiply_convert_fusion.6.other_ref, bf16[512,1408]{1,0:T(8,128)(2,1)} %get-tuple-element.92, bf16[512,1408]{1,0:T(8,128)(2,1)} %get-tuple-element.93), kind=kOutput, calls=%fused_computation | convolution fusion | flops 2967207936 | bytes 15466496 | tf_op jit(solution)/shard_map/dot_general | solution.py:440
  257.6 6.7 %fusion.30 = f32[512,1024]{1,0:T(8,128)S(1)} fusion(bf16[1024,2816]{1,0:T(8,128)(2,1)} %after.5, bf16[512,1408]{1,0:T(8,128)(2,1)} %get-tuple-element.92, bf16[512,1408]{1,0:T(8,128)(2,1)} %get-tuple-element.93), kind=kOutput, calls=%fused_computation.76 | convolution fusion | flops 2958557184 | bytes 10747904 | tf_op jit(solution)/shard_map/dot_general | solution.py:446
  264.3 6.3 %multiply_reduce_fusion = (bf16[1024]{0:T(1024)(128)(2,1)S(1)}, f32[512]{0:T(512)S(1)}, f32[512,1024]{1,0:T(8,128)S(1)}) fusion(f32[512,1024]{1,0:T(8,128)S(1)} %copy-done.25, f32[512]{0:T(512)S(1)} %fusion.69, f32[1024]{0:T(1024)S(1)} %bitcast.122, f32[512,1024]{1,0:T(8,128)S(1)} %fusion.30, bf16[1024,2816]{1,0:T(8,128)(2,1)} %collective-permute-done.4, ...), kind=kOutput, calls=%fused_computation.69 | convolution fusion | flops 2962225664 | bytes 14952448 | tf_op jit(solution)/shard_map/dot_general | solution.py:446
  291.8 8.5 %collective-permute-done.7 = bf16[1,4,264,128]{3,2,1,0:T(8,128)(2,1)S(1)} collective-permute-done((bf16[1,4,264,128]{3,2,1,0:T(8,128)(2,1)S(1)}, bf16[1,4,264,128]{3,2,1,0:T(8,128)(2,1)S(1)}, u32[]{:S(2)}, u32[]{:S(2)}) %collective-permute-start.7) | collective-permute-done | bytes 270368 | tf_op jit(solution)/shard_map/ppermute | solution.py:426
  300.3 9.1 %collective-permute-done.8 = bf16[1,4,264,128]{3,2,1,0:T(8,128)(2,1)S(1)} collective-permute-done((bf16[1,4,264,128]{3,2,1,0:T(8,128)(2,1)S(1)}, bf16[1,4,264,128]{3,2,1,0:T(8,128)(2,1)S(1)}, u32[]{:S(2)}, u32[]{:S(2)}) %collective-permute-start.8) | collective-permute-done | bytes 270368 | tf_op jit(solution)/shard_map/ppermute | solution.py:426
  312.8 12.2 %scan_backward.1 = (bf16[512,1536]{1,0:T(8,128)(2,1)S(1)}, bf16[512,1536]{1,0:T(8,128)(2,1)S(1)}, f32[512,512]{1,0:T(8,128)S(1)}) custom-call(f32[512,1536]{1,0:T(8,128)} %copy-done.2, f32[512,1536]{1,0:T(8,128)} %copy-done.2, f32[512,1536]{1,0:T(8,128)} %copy-done.2, f32[512,1536]{1,0:T(8,128)} %copy-done.3, f32[512,1536]{1,0:T(8,128)} %copy-done.3, ...), custom_call_target="tpu_custom_call" | custom-call | tf_op jit(solution)/shard_map/scan_backward/pallas_call | solution.py:353
  342.4 5.6 fusion.17
  361.0 16.0 %collective-permute-done.12 = bf16[704,512]{1,0:T(8,128)(2,1)S(1)} collective-permute-done((bf16[704,512]{1,0:T(8,128)(2,1)}, bf16[704,512]{1,0:T(8,128)(2,1)S(1)}, u32[]{:S(2)}, u32[]{:S(2)}) %collective-permute-start.12) | collective-permute-done | bytes 720928 | tf_op jit(solution)/shard_map/ppermute | solution.py:510
  380.4 23.0 %collective-permute-start.14 = (bf16[256,2816]{1,0:T(8,128)(2,1)}, bf16[256,2816]{1,0:T(8,128)(2,1)S(1)}, u32[]{:S(2)}, u32[]{:S(2)}) collective-permute-start(bf16[256,2816]{1,0:T(8,128)(2,1)} %after.8), channel_id=1, source_target_pairs={{0,8},{24,16},{1,9},{25,17},{2,10},{26,18},{3,11},{27,19},{4,12},{... | collective-permute-start | bytes 4325384 | tf_op jit(solution)/shard_map/ppermute | solution.py:510
  403.4 29.8 %collective-permute-done.14 = bf16[256,2816]{1,0:T(8,128)(2,1)S(1)} collective-permute-done((bf16[256,2816]{1,0:T(8,128)(2,1)}, bf16[256,2816]{1,0:T(8,128)(2,1)S(1)}, u32[]{:S(2)}, u32[]{:S(2)}) %collective-permute-start.14) | collective-permute-done | bytes 1441824 | tf_op jit(solution)/shard_map/ppermute | solution.py:510
  439.6 35.9 %collective-permute-start.16 = (bf16[256,2176]{1,0:T(8,128)(2,1)}, bf16[256,2176]{1,0:T(8,128)(2,1)S(1)}, u32[]{:S(2)}, u32[]{:S(2)}) collective-permute-start(bf16[256,2176]{1,0:T(8,128)(2,1)} %after.9), channel_id=1, source_target_pairs={{0,8},{24,16},{1,9},{25,17},{2,10},{26,18},{3,11},{27,19},{4,12},{... | collective-permute-start | bytes 3342344 | tf_op jit(solution)/shard_map/ppermute | solution.py:510
  481.4 15.0 %collective-permute-done.16 = bf16[256,2176]{1,0:T(8,128)(2,1)S(1)} collective-permute-done((bf16[256,2176]{1,0:T(8,128)(2,1)}, bf16[256,2176]{1,0:T(8,128)(2,1)S(1)}, u32[]{:S(2)}, u32[]{:S(2)}) %collective-permute-start.16) | collective-permute-done | bytes 1114144 | tf_op jit(solution)/shard_map/ppermute | solution.py:510
  504.8 18.3 %collective-permute-done.22 = bf16[704,512]{1,0:T(8,128)(2,1)S(1)} collective-permute-done((bf16[704,512]{1,0:T(8,128)(2,1)S(1)}, bf16[704,512]{1,0:T(8,128)(2,1)S(1)}, u32[]{:S(2)}, u32[]{:S(2)}) %collective-permute-start.22) | collective-permute-done | bytes 720928 | tf_op jit(solution)/shard_map/ppermute | solution.py:510
  524.9 29.1 %collective-permute-done.20 = bf16[256,2816]{1,0:T(8,128)(2,1)S(1)} collective-permute-done((bf16[256,2816]{1,0:T(8,128)(2,1)S(1)}, bf16[256,2816]{1,0:T(8,128)(2,1)S(1)}, u32[]{:S(2)}, u32[]{:S(2)}) %collective-permute-start.20) | collective-permute-done | bytes 1441824 | tf_op jit(solution)/shard_map/ppermute | solution.py:510
  556.4 16.3 %collective-permute-done.18 = bf16[256,2176]{1,0:T(8,128)(2,1)S(1)} collective-permute-done((bf16[256,2176]{1,0:T(8,128)(2,1)S(1)}, bf16[256,2176]{1,0:T(8,128)(2,1)S(1)}, u32[]{:S(2)}, u32[]{:S(2)}) %collective-permute-start.18) | collective-permute-done | bytes 1114144 | tf_op jit(solution)/shard_map/ppermute | solution.py:510
  (329 shorter events, 172.7 us)
Async XLA Ops:
  7.2 64.8 %all-gather.4.cloned.1.call-start = ((), (), s32[]{:S(2)}) async-start(), calls=%async_computation.3 | async-start | bytes 5570560 | tf_op jit(solution)/shard_map/all_gather | solution.py:564
  14.3 146.7 %all-gather.6.cloned.1.call-start = ((), (), s32[]{:S(2)}) async-start(), calls=%async_computation.4 | async-start | bytes 7208960 | tf_op jit(solution)/shard_map/all_gather | solution.py:565
  16.8 188.6 %all-gather.8.cloned.1.call-start = ((), (), s32[]{:S(2)}) async-start(), calls=%async_computation.5 | async-start | bytes 3604480 | tf_op jit(solution)/shard_map/all_gather | solution.py:566
  72.0 10.6 %collective-permute-start = (bf16[1024,2176]{1,0:T(8,128)(2,1)}, bf16[1024,2176]{1,0:T(8,128)(2,1)}, u32[]{:S(2)}, u32[]{:S(2)}) collective-permute-start(bf16[1024,2176]{1,0:T(8,128)(2,1)} %all-gather.4.cloned.1.call-done), channel_id=1, source_target_pairs={{0,4},{4,0},{1,5},{5,1},{2,6},{6,2},{3,7},{7,3},{8,12},{12,8},{9,1... | collective-permute-start | bytes 13369352 | tf_op jit(solution)/shard_map/ppermute | solution.py:455
  73.0 284.3 %reduce-scatter.8.cloned.1.call-start = ((), (), s32[]{:S(2)}) async-start(), calls=%async_computation.8 | async-start | bytes 3604480 | tf_op jit(solution)/shard_map/reduce_scatter | solution.py:499
  98.5 36.6 %collective-permute-start.2 = (f32[1,4,264,128]{3,2,1,0:T(8,128)}, f32[1,4,264,128]{3,2,1,0:T(8,128)}, u32[]{:S(2)}, u32[]{:S(2)}) collective-permute-start(f32[1,4,264,128]{3,2,1,0:T(8,128)} %get-tuple-element.34), channel_id=1, source_target_pairs={{0,2},{1,3},{4,6},{5,7},{8,10},{9,11},{12,14},{13,15},{16,18},{17,... | collective-permute-start | bytes 1622024 | tf_op jit(solution)/shard_map/ppermute | solution.py:426
  102.9 32.2 %collective-permute-start.1 = (f32[1,4,264,128]{3,2,1,0:T(8,128)}, f32[1,4,264,128]{3,2,1,0:T(8,128)}, u32[]{:S(2)}, u32[]{:S(2)}) collective-permute-start(f32[1,4,264,128]{3,2,1,0:T(8,128)} %get-tuple-element.34), channel_id=1, source_target_pairs={{0,1},{1,2},{2,3},{4,5},{5,6},{6,7},{8,9},{9,10},{10,11},{12,13},{... | collective-permute-start | bytes 1622024 | tf_op jit(solution)/shard_map/ppermute | solution.py:426
  106.0 45.8 %collective-permute-start.3 = (f32[1,4,264,128]{3,2,1,0:T(8,128)}, f32[1,4,264,128]{3,2,1,0:T(8,128)}, u32[]{:S(2)}, u32[]{:S(2)}) collective-permute-start(f32[1,4,264,128]{3,2,1,0:T(8,128)} %get-tuple-element.34), channel_id=1, source_target_pairs={{0,3},{4,7},{8,11},{12,15},{16,19},{20,23},{24,27},{28,31}} | collective-permute-start | bytes 1622024 | tf_op jit(solution)/shard_map/ppermute | solution.py:426
  161.0 56.1 %collective-permute-start.4 = (bf16[1024,2816]{1,0:T(8,128)(2,1)}, bf16[1024,2816]{1,0:T(8,128)(2,1)}, u32[]{:S(2)}, u32[]{:S(2)}) collective-permute-start(bf16[1024,2816]{1,0:T(8,128)(2,1)} %after.5), channel_id=1, source_target_pairs={{0,4},{4,0},{1,5},{5,1},{2,6},{6,2},{3,7},{7,3},{8,12},{12,8},{9,1... | collective-permute-start | bytes 17301512 | tf_op jit(solution)/shard_map/ppermute | solution.py:455
  242.0 138.5 %reduce-scatter.6.cloned.1.call-start = ((), (), s32[]{:S(2)}) async-start(), calls=%async_computation.7 | async-start | bytes 7208960 | tf_op jit(solution)/shard_map/reduce_scatter | solution.py:499
  256.8 182.8 %reduce-scatter.4.cloned.1.call-start = ((), (), s32[]{:S(2)}) async-start(), calls=%async_computation.6 | async-start | bytes 5570560 | tf_op jit(solution)/shard_map/reduce_scatter | solution.py:499
  286.9 13.4 %collective-permute-start.7 = (bf16[1,4,264,128]{3,2,1,0:T(8,128)(2,1)S(1)}, bf16[1,4,264,128]{3,2,1,0:T(8,128)(2,1)S(1)}, u32[]{:S(2)}, u32[]{:S(2)}) collective-permute-start(bf16[1,4,264,128]{3,2,1,0:T(8,128)(2,1)S(1)} %pad_maximum_fusion.15), channel_id=1, source_target_pairs={{1,0},{2,1},{3,2},{5,4},{6,5},{7,6},{9,8},{10,9},{11,10},{13,12},{... | collective-permute-start | bytes 811016 | tf_op jit(solution)/shard_map/ppermute | solution.py:426
  288.4 21.0 %collective-permute-start.8 = (bf16[1,4,264,128]{3,2,1,0:T(8,128)(2,1)S(1)}, bf16[1,4,264,128]{3,2,1,0:T(8,128)(2,1)S(1)}, u32[]{:S(2)}, u32[]{:S(2)}) collective-permute-start(bf16[1,4,264,128]{3,2,1,0:T(8,128)(2,1)S(1)} %pad_maximum_fusion.15), channel_id=1, source_target_pairs={{2,0},{3,1},{6,4},{7,5},{10,8},{11,9},{14,12},{15,13},{18,16},{19,... | collective-permute-start | bytes 811016 | tf_op jit(solution)/shard_map/ppermute | solution.py:426
  290.5 22.1 %collective-permute-start.9 = (bf16[1,4,264,128]{3,2,1,0:T(8,128)(2,1)S(1)}, bf16[1,4,264,128]{3,2,1,0:T(8,128)(2,1)S(1)}, u32[]{:S(2)}, u32[]{:S(2)}) collective-permute-start(bf16[1,4,264,128]{3,2,1,0:T(8,128)(2,1)S(1)} %pad_maximum_fusion.15), channel_id=1, source_target_pairs={{3,0},{7,4},{11,8},{15,12},{19,16},{23,20},{27,24},{31,28}} | collective-permute-start | bytes 811016 | tf_op jit(solution)/shard_map/ppermute | solution.py:426
  329.7 19.0 %collective-permute-start.10 = (bf16[1024,2048]{1,0:T(8,128)(2,1)}, bf16[1024,2048]{1,0:T(8,128)(2,1)}, u32[]{:S(2)}, u32[]{:S(2)}) collective-permute-start(bf16[1024,2048]{1,0:T(8,128)(2,1)} %pad_maximum_fusion.1), channel_id=1, source_target_pairs={{0,4},{4,0},{1,5},{5,1},{2,6},{6,2},{3,7},{7,3},{8,12},{12,8},{9,1... | collective-permute-start | bytes 12582920 | tf_op jit(solution)/shard_map/ppermute | solution.py:455
  357.3 19.7 %collective-permute-start.12 = (bf16[704,512]{1,0:T(8,128)(2,1)}, bf16[704,512]{1,0:T(8,128)(2,1)S(1)}, u32[]{:S(2)}, u32[]{:S(2)}) collective-permute-start(bf16[704,512]{1,0:T(8,128)(2,1)} %reduce-scatter.8.cloned.1.call-done), channel_id=1, source_target_pairs={{0,8},{24,16},{1,9},{25,17},{2,10},{26,18},{3,11},{27,19},{4,12},{... | collective-permute-start | bytes 2162696 | tf_op jit(solution)/shard_map/ppermute | solution.py:510
  380.4 52.8 %collective-permute-start.14 = (bf16[256,2816]{1,0:T(8,128)(2,1)}, bf16[256,2816]{1,0:T(8,128)(2,1)S(1)}, u32[]{:S(2)}, u32[]{:S(2)}) collective-permute-start(bf16[256,2816]{1,0:T(8,128)(2,1)} %after.8), channel_id=1, source_target_pairs={{0,8},{24,16},{1,9},{25,17},{2,10},{26,18},{3,11},{27,19},{4,12},{... | collective-permute-start | bytes 4325384 | tf_op jit(solution)/shard_map/ppermute | solution.py:510
  439.6 56.9 %collective-permute-start.16 = (bf16[256,2176]{1,0:T(8,128)(2,1)}, bf16[256,2176]{1,0:T(8,128)(2,1)S(1)}, u32[]{:S(2)}, u32[]{:S(2)}) collective-permute-start(bf16[256,2176]{1,0:T(8,128)(2,1)} %after.9), channel_id=1, source_target_pairs={{0,8},{24,16},{1,9},{25,17},{2,10},{26,18},{3,11},{27,19},{4,12},{... | collective-permute-start | bytes 3342344 | tf_op jit(solution)/shard_map/ppermute | solution.py:510
  496.7 26.6 %collective-permute-start.17 = (bf16[256,2176]{1,0:T(8,128)(2,1)S(1)}, bf16[256,2176]{1,0:T(8,128)(2,1)S(1)}, u32[]{:S(2)}, u32[]{:S(2)}) collective-permute-start(bf16[256,2176]{1,0:T(8,128)(2,1)S(1)} %add_convert_fusion.5), channel_id=1, source_target_pairs={{8,16},{16,8},{9,17},{17,9},{10,18},{18,10},{11,19},{19,11},{12,20... | collective-permute-start | bytes 3342344 | tf_op jit(solution)/shard_map/ppermute | solution.py:510
  499.8 23.3 %collective-permute-start.22 = (bf16[704,512]{1,0:T(8,128)(2,1)S(1)}, bf16[704,512]{1,0:T(8,128)(2,1)S(1)}, u32[]{:S(2)}, u32[]{:S(2)}) collective-permute-start(bf16[704,512]{1,0:T(8,128)(2,1)S(1)} %copy-done.38), channel_id=1, source_target_pairs={{8,0},{16,24},{9,1},{17,25},{10,2},{18,26},{11,3},{19,27},{12,4},{... | collective-permute-start | bytes 2162696 | tf_op jit(solution)/shard_map/ppermute | solution.py:510
  501.1 52.9 %collective-permute-start.20 = (bf16[256,2816]{1,0:T(8,128)(2,1)S(1)}, bf16[256,2816]{1,0:T(8,128)(2,1)S(1)}, u32[]{:S(2)}, u32[]{:S(2)}) collective-permute-start(bf16[256,2816]{1,0:T(8,128)(2,1)S(1)} %copy-done.32), channel_id=1, source_target_pairs={{8,0},{16,24},{9,1},{17,25},{10,2},{18,26},{11,3},{19,27},{12,4},{... | collective-permute-start | bytes 4325384 | tf_op jit(solution)/shard_map/ppermute | solution.py:510
  523.2 31.0 %collective-permute-start.23 = (bf16[704,512]{1,0:T(8,128)(2,1)S(1)}, bf16[704,512]{1,0:T(8,128)(2,1)S(1)}, u32[]{:S(2)}, u32[]{:S(2)}) collective-permute-start(bf16[704,512]{1,0:T(8,128)(2,1)S(1)} %broadcast_select_fusion.2), channel_id=1, source_target_pairs={{0,4},{4,0},{1,5},{5,1},{2,6},{6,2},{3,7},{7,3},{8,12},{12,8},{9,1... | collective-permute-start | bytes 2162696 | tf_op jit(solution)/shard_map/ppermute | solution.py:455
  523.6 49.1 %collective-permute-start.18 = (bf16[256,2176]{1,0:T(8,128)(2,1)S(1)}, bf16[256,2176]{1,0:T(8,128)(2,1)S(1)}, u32[]{:S(2)}, u32[]{:S(2)}) collective-permute-start(bf16[256,2176]{1,0:T(8,128)(2,1)S(1)} %add_convert_fusion.4), channel_id=1, source_target_pairs={{8,0},{16,24},{9,1},{17,25},{10,2},{18,26},{11,3},{19,27},{12,4},{... | collective-permute-start | bytes 3342344 | tf_op jit(solution)/shard_map/ppermute | solution.py:510
  554.1 18.7 %collective-permute-start.21 = (bf16[256,2816]{1,0:T(8,128)(2,1)S(1)}, bf16[256,2816]{1,0:T(8,128)(2,1)S(1)}, u32[]{:S(2)}, u32[]{:S(2)}) collective-permute-start(bf16[256,2816]{1,0:T(8,128)(2,1)S(1)} %broadcast_select_fusion), channel_id=1, source_target_pairs={{0,4},{4,0},{1,5},{5,1},{2,6},{6,2},{3,7},{7,3},{8,12},{12,8},{9,1... | collective-permute-start | bytes 4325384 | tf_op jit(solution)/shard_map/ppermute | solution.py:455
  (81 other events, 913.6 us)
Sparse Core Ops, SparseCore 0:
  14.4 57.5 all-gather.3
  74.4 85.5 all-gather.5
  162.4 42.9 all-gather.7
  242.1 41.8 reduce-scatter.7
  286.8 74.7 reduce-scatter.5
  364.6 54.8 reduce-scatter.3

commit v4 on v3

--- a/solution.py
+++ b/solution.py
@@ -499,26 +499,63 @@
     return lax.psum_scatter(array, "seq", scatter_dimension=0, tiled=True)
 
 
-def line_sum(array):
+def direct(count):
+    return count in (2, 4)
+
+
+def spread(array):
+    count, me = lax.axis_size("seq"), lax.axis_index("seq")
+    if not direct(count):
+        return lax.all_gather(array, "seq", tiled=True)
+    rows = array.shape[0]
+    whole = jnp.zeros((count * rows, array.shape[1]), array.dtype)
+    whole = lax.dynamic_update_slice_in_dim(whole, array, me * rows, 0)
+    for distance in range(1, count):
+        came = lax.ppermute(array, "seq", [(i, i ^ distance) for i in range(count)])
+        whole = lax.dynamic_update_slice_in_dim(whole, came, (me ^ distance) * rows, 0)
+    return whole
+
+
+def gathered_sum(array, late):
+    count, me = lax.axis_size("seq"), lax.axis_index("seq")
+    if not direct(count):
+        return scattered(array)
+    rows = array.shape[0] // count
+    total = lax.dynamic_slice_in_dim(array, me * rows, rows, 0).astype(jnp.float32)
+    for distance in range(1, count):
+        piece = lax.dynamic_slice_in_dim(array, (me ^ distance) * rows, rows, 0)
+        came = lax.ppermute(piece, "seq", [(i, i ^ distance) for i in range(count)])
+        total = total + after(came, late).astype(jnp.float32)
+    return low(total)
+
+
+def line_sum(array, parts, earlier=None):
     count, me = lax.axis_size("z"), lax.axis_index("z")
     if count % 2:
         return (lax.psum(array, "z"),) * 2
     middle = count // 2
-    total = array
+    rows = array.shape[0] // parts
+    totals = [array[i * rows : (i + 1) * rows] for i in range(parts)]
 
     def send(pairs):
-        return lax.ppermute(total, "z", pairs)
+        return [lax.ppermute(total, "z", pairs) for total in totals]
+
+    def add(came):
+        return [
+            low(total.astype(jnp.float32) + other.astype(jnp.float32)) for total, other in zip(totals, came)
+        ]
 
     for step in range(middle - 1):
-        came = send([(step, step + 1), (count - 1 - step, count - 2 - step)])
-        total = low(total.astype(jnp.float32) + came.astype(jnp.float32))
-    came = send([(middle - 1, middle), (middle, middle - 1)])
-    total = low(total.astype(jnp.float32) + came.astype(jnp.float32))
-    at_middle = total
+        totals = add(send([(step, step + 1), (count - 1 - step, count - 2 - step)]))
+    if earlier is not None:
+        totals[0] = after(totals[0], earlier)
+    totals = add(send([(middle - 1, middle), (middle, middle - 1)]))
+    at_middle = totals[-1]
     for step in reversed(range(middle - 1)):
         came = send([(step + 1, step), (count - 2 - step, count - 1 - step)])
-        total = jnp.where((me == step) | (me == count - 1 - step), came, total)
-    return total, at_middle
+        end = (me == step) | (me == count - 1 - step)
+        totals = [jnp.where(end, other, total) for total, other in zip(totals, came)]
+    return jnp.concatenate(totals, 0), at_middle
 
 
 def local(
@@ -553,21 +590,20 @@
     mixer_packed = jnp.concatenate(
         [
             own_half(weight, 1)
-            for weight in (query_weight, key_weight, value_weight, outgate_weight, output_weight)
+            for weight in (query_weight, key_weight, value_weight, outgate_weight)
         ]
         + [flat],
         axis=1,
     )
     ffn_packed = jnp.concatenate([own_half(gate_weight, 1), own_half(up_weight, 1)], axis=1)
-    down_packed = own_half(down_weight, 1)
-    wide = PACKED + width // 2
     mixer_mine = lax.all_gather(mixer_packed, "seq", tiled=True)
     ffn_mine = lax.all_gather(ffn_packed, "seq", tiled=True)
-    down_mine = lax.all_gather(down_packed, "seq", tiled=True)
-    mixer_theirs = swapped(mixer_mine)
+    output_mine = spread(own_half(output_weight, 1))
+    mixer_mine = after(after(mixer_mine, output_mine), ffn_packed)
+    down_mine = spread(after(own_half(down_weight, 1), mixer_mine))
+    mixer_theirs, output_theirs = swapped(mixer_mine), swapped(output_mine)
     projection_mine, projection_theirs = mixer_mine[:, :PACKED], mixer_theirs[:, :PACKED]
-    output_mine, output_theirs = mixer_mine[:, PACKED:wide], mixer_theirs[:, PACKED:wide]
-    small_all = mixer_mine[:, wide:].reshape(count, -1)
+    small_all = mixer_mine[:, PACKED:].reshape(count, -1)
     pieces, begin = [], 0
     for small in smalls:
         pieces.append(small_all[:, begin : begin + small.size].reshape((count,) + small.shape))
@@ -600,7 +636,7 @@
     theirs = product(normed_one, projection_theirs)
     chunk = min(CHUNK, seg_len)
     local_out, forget, scores, states, starts, summary = scan_forward(mine, theirs, gates, seqs_here, chunk)
-    incoming_state = from_neighbours(summary, 1)
+    incoming_state = after(from_neighbours(low(summary), 1), down_mine)
     attended, mixed = mix_forward(
         local_out, forget, incoming_state, mine, theirs, head_gain_f[None, :], seqs_here, chunk
     )
@@ -616,8 +652,7 @@
 
     both_mine, both_theirs = product(normed_two, ffn_mine), product(normed_two, ffn_theirs)
     hidden = joined(swiglu(both_mine), swiglu(both_theirs), 1)
-    down_mine = after(down_mine, normed_two)
-    down_theirs = swapped(down_mine)
+    down_theirs = swapped(after(down_mine, mixed))
     result = resid + joined(product(hidden, down_mine), product(hidden, down_theirs), 1)
     block_out = result.astype(jnp.bfloat16).reshape(tokens.shape)
 
@@ -641,7 +676,6 @@
     grad_mine, grad_theirs = halves_of(hidden_grad)
     back_mine, back_theirs = swiglu_back(both_mine, grad_mine), swiglu_back(both_theirs, grad_theirs)
     down_pair = low(product_left(hidden, low_mine) + down_came.astype(jnp.float32))
-    down_share = scattered(down_pair)
 
     ffn_came = swapped(low(product_left(normed_two, back_theirs)))
     normed_two_grad = product_right(back_mine, ffn_mine) + product_right(back_theirs, ffn_theirs)
@@ -655,6 +689,9 @@
     ffn_pair = low(product_left(normed_two, back_mine) + ffn_came.astype(jnp.float32))
     ffn_share = scattered(ffn_pair)
     mixed_grad = after(mixed_grad, ffn_pair)
+    mixed_later = after(mixed, mixed_grad)
+    output_came = swapped(low(product_left(mixed_later, branch_theirs)))
+    output_pair = low(product_left(mixed_later, branch_mine) + output_came.astype(jnp.float32))
 
     attended_grad, *outgate_grads, state_grad, head_gain_grad = mix_backward(
         mixed_grad, attended, mine, theirs, head_gain_f[None, :], forget, seqs_here, chunk
@@ -667,10 +704,9 @@
         mine, theirs, gates, scores, states, starts, incoming_state,
         attended_grad, later_grad, outgate_grads, seqs_here, chunk,
     )
-    output_theirs_grad = low(product_left(mixed, branch_theirs))
-    packed_came = swapped(
-        jnp.concatenate([low(product_left(normed_one, packed_theirs)), output_theirs_grad], axis=1)
-    ).astype(jnp.float32)
+    packed_came = swapped(low(product_left(normed_one, packed_theirs)))
+    down_share = gathered_sum(down_pair, gates_grad)
+    output_share = gathered_sum(output_pair, gates_grad)
     gate_pulled = jax.vjp(gate_fn, low_rank, decay_up_f, decay_bias_f)[1](gates_grad)
     low_rank_grad = gate_pulled[0].astype(jnp.bfloat16)
     decay_up_grad = jnp.concatenate(halves_of(gate_pulled[1]), 1)
@@ -702,32 +738,33 @@
     small_grads = jnp.pad(low(small_grads), ((0, 0), (0, shard_rows * extra - flat_size)))
     mixer_pair = jnp.concatenate(
         [
-            low(product_left(normed_one, packed_mine) + packed_came[:, :PACKED]),
-            low(product_left(mixed, branch_mine) + packed_came[:, PACKED:]),
+            low(product_left(normed_one, packed_mine) + packed_came.astype(jnp.float32)),
             small_grads.reshape(count * shard_rows, extra),
         ],
         axis=1,
     )
     mixer_share = scattered(mixer_pair)
 
-    down_total, down_middle = line_sum(down_share)
-    down_weight_grad = joined(down_total, swapped(down_total), 1).astype(jnp.float32)
-    ffn_total, ffn_middle = line_sum(after(ffn_share, down_middle))
+    others = after(jnp.concatenate([down_share, output_share], 0), mixer_pair)
+    others_total, others_middle = line_sum(others, 1)
+    others_other = swapped(others_total)
+    ffn_total, ffn_middle = line_sum(after(ffn_share, others_middle), 2, others_total)
     ffn_other = swapped(ffn_total)
-    mixer_total, _ = line_sum(after(mixer_share, ffn_middle))
+    mixer_total, _ = line_sum(after(mixer_share, ffn_middle), 2, ffn_total)
     mixer_other = swapped(mixer_total)
+    down_rows = down_weight.shape[0]
 
     def both_cores(total, other, begin, end):
         return joined(total[:, begin:end], other[:, begin:end], 1).astype(jnp.float32)
 
-    summed = mixer_total[:, wide:].astype(jnp.float32) + mixer_other[:, wide:].astype(jnp.float32)
+    summed = mixer_total[:, PACKED:].astype(jnp.float32) + mixer_other[:, PACKED:].astype(jnp.float32)
     summed, shares, begin = summed.reshape(-1), [], 0
     for small in smalls:
         shares.append(summed[begin : begin + small.size].reshape(small.shape))
         begin += small.size
 
-    columns = (0, KEYS // 2, KEYS, KEYS + VALUES // 2, PACKED, wide)
-    query_g, key_g, value_g, outgate_g, output_g = (
+    columns = (0, KEYS // 2, KEYS, KEYS + VALUES // 2, PACKED)
+    query_g, key_g, value_g, outgate_g = (
         both_cores(mixer_total, mixer_other, a, b) for a, b in zip(columns[:-1], columns[1:])
     )
     return (
@@ -742,11 +779,11 @@
         shares[3],
         outgate_g,
         shares[4],
-        output_g,
+        joined(others_total[down_rows:], others_other[down_rows:], 1).astype(jnp.float32),
         shares[5],
         both_cores(ffn_total, ffn_other, 0, ff // 2),
         both_cores(ffn_total, ffn_other, ff // 2, ff),
-        down_weight_grad,
+        joined(others_total[:down_rows], others_other[:down_rows], 1).astype(jnp.float32),
     )
 
 

time: 600 us -> 614 us (1.023)
  waiting for transfers between devices: 282 us -> 246 us
  local copies, waits for them, and re-layouts: 34.1 us -> 69.2 us
  starting transfers between devices: 85.1 us -> 95.5 us
    all_gather x1 -> x0, waiting for transfers between devices: 35 us -> none  [local(): down_mine = lax.all_gather(down_packed, 'seq', tiled=True)]
    all_gather x1, waiting for transfers between devices: 55.1 us -> 30.1 us  [local(): mixer_mine = lax.all_gather(mixer_packed, 'seq', tiled=True)]
    unnamed x160 -> x208, local copies, waits for them, and re-layouts: 25.3 us -> 39.8 us
    ppermute x9 -> x27, starting transfers between devices: 70.1 us -> 82 us  [the longest x15 61.7 us: send(): return [lax.ppermute(total, 'z', pairs) for total in totals]]
    ppermute x9 -> x27, waiting for transfers between devices: 125 us -> 135 us  [the longest x15 82.6 us: send(): return [lax.ppermute(total, 'z', pairs) for total in totals]]
    all_gather x1, waiting for transfers between devices: 0.01 us -> 8.85 us  [local(): ffn_mine = lax.all_gather(ffn_packed, 'seq', tiled=True)]
    ppermute x9 -> x11, waiting for transfers between devices: 4.77 us -> 12.7 us  [swapped(): return lax.ppermute(array, 'core', [(0, 1), (1, 0)])]
    dynamic_update_slice x0 -> x8, local copies, waits for them, and re-layouts: none -> 7.28 us  [the longest x6 6.33 us: spread(): lax.dynamic_update_slice_in_dim(whole, came, (me ^ distance) * rows, 0)]
  transfers between devices with their start and end apart: 30 -> 48, of which waited for: 14 -> 24; matrix products, arithmetic and copies ran while one was open for 23% -> 26% of each run, Pallas kernels for 4% -> 4%
where the time goes in v4:
time: 614 us; the launch traced here: 604 us
  waiting for transfers between devices  246 us (40%)
  matrix products  103 us (17%)
  starting transfers between devices  95.5 us (16%)
  local copies, waits for them, and re-layouts  69.2 us (11%)
  other arithmetic  49.6 us (8%)
  Pallas kernels  24.4 us (4%)
  between operations  15.6 us (3%)
    ppermute x15, waiting for transfers between devices, send(): return [lax.ppermute(total, 'z', pairs) for total in totals]  82.6 us
    ppermute x15, starting transfers between devices, send(): return [lax.ppermute(total, 'z', pairs) for total in totals]  61.7 us
    ppermute x6, waiting for transfers between devices, from_neighbours(): came = lax.ppermute(summary, 'seq', pairs)  59.8 us
    ppermute x6, waiting for transfers between devices, spread(): came = lax.ppermute(array, 'seq', [(i, i ^ distance) for i in range(count)])  41.8 us
    unnamed x208, local copies, waits for them, and re-layouts  39.8 us
    dot_general x9, matrix products, product_right(): lax.dot_general(left, right, (((1,), (1,)), ((), ())), preferred_element_...  35.6 us
    dot_general x9, matrix products, product_left(): lax.dot_general(left, right, (((0,), (0,)), ((), ())), preferred_element_...  32.5 us
    dot_general x9, matrix products, product(): return jnp.dot(left, right, preferred_element_type=jnp.float32)  30.4 us
  transfers between devices with their start and end apart: 48, of which 24 were waited for; matrix products, arithmetic and copies ran while one was open for 26% of the time, Pallas kernels for 4%

profile of v4, /device:TPU:0, one launch (start us, length us, event | category | flops | bytes accessed | tf_op | source)
XLA Modules:
  0.0 603.6 jit_solution(4281166479827269545)
XLA Ops:
  23.8 6.5 %collective-permute-done = bf16[256,512]{1,0:T(8,128)(2,1)S(1)} collective-permute-done((bf16[256,512]{1,0:T(8,128)(2,1)S(1)}, bf16[256,512]{1,0:T(8,128)(2,1)S(1)}, u32[]{:S(2)}, u32[]{:S(2)}) %collective-permute-start) | collective-permute-done | bytes 262176 | tf_op jit(solution)/shard_map/ppermute | solution.py:514
  30.3 6.5 %collective-permute-done.1 = bf16[256,512]{1,0:T(8,128)(2,1)S(1)} collective-permute-done((bf16[256,512]{1,0:T(8,128)(2,1)S(1)}, bf16[256,512]{1,0:T(8,128)(2,1)S(1)}, u32[]{:S(2)}, u32[]{:S(2)}) %collective-permute-start.1) | collective-permute-done | bytes 262176 | tf_op jit(solution)/shard_map/ppermute | solution.py:514
  41.2 30.1 %all-gather.3.cloned.1.call-done.array_ref = bf16[1024,1664]{1,0:T(8,128)(2,1)} async-done(((bf16[256,1664]{1,0:T(8,128)(2,1)}), bf16[1024,1664]{1,0:T(8,128)(2,1)}) %all-gather.3.cloned.1.call-update) | async-done | bytes 3407888 | tf_op jit(solution)/shard_map/all_gather | solution.py:599
  102.3 24.4 %collective-permute-done.7 = bf16[704,512]{1,0:T(8,128)(2,1)} collective-permute-done((bf16[704,512]{1,0:T(8,128)(2,1)}, bf16[704,512]{1,0:T(8,128)(2,1)}, u32[]{:S(2)}, u32[]{:S(2)}) %collective-permute-start.7) | collective-permute-done | bytes 720928 | tf_op jit(solution)/shard_map/ppermute | solution.py:514
  137.5 6.4 %collective-permute-done.5 = bf16[1,4,264,128]{3,2,1,0:T(8,128)(2,1)S(1)} collective-permute-done((bf16[1,4,264,128]{3,2,1,0:T(8,128)(2,1)S(1)}, bf16[1,4,264,128]{3,2,1,0:T(8,128)(2,1)S(1)}, u32[]{:S(2)}, u32[]{:S(2)}) %collective-permute-start.5) | collective-permute-done | bytes 270368 | tf_op jit(solution)/shard_map/ppermute | solution.py:426
  159.9 8.9 %all-gather.5.cloned.1.call-done.array_ref = bf16[1024,2816]{1,0:T(8,128)(2,1)} async-done(((bf16[256,2816]{1,0:T(8,128)(2,1)}), bf16[1024,2816]{1,0:T(8,128)(2,1)}) %all-gather.5.cloned.1.call-update) | async-done | bytes 5767184 | tf_op jit(solution)/shard_map/all_gather | solution.py:600
  195.6 5.8 fusion.93
  210.5 8.6 %collective-permute-done.13 = bf16[1024,2816]{1,0:T(8,128)(2,1)S(1)} collective-permute-done((bf16[1024,2816]{1,0:T(8,128)(2,1)S(1)}, bf16[1024,2816]{1,0:T(8,128)(2,1)S(1)}, u32[]{:S(2)}, u32[]{:S(2)}) %collective-permute-start.13) | collective-permute-done | bytes 5767200 | tf_op jit(solution)/shard_map/ppermute | solution.py:455
  224.2 6.4 %convolution_convert_fusion.1 = bf16[2816,512]{1,0:T(8,128)(2,1)} fusion(pred[]{:T(512)S(6)} %eq.16, bf16[512,1024]{1,0:T(8,128)(2,1)} %bitcast.116, bf16[512,1408]{1,0:T(8,128)(2,1)} %get-tuple-element.97, bf16[512,1408]{1,0:T(8,128)(2,1)} %get-tuple-element.96), kind=kOutput, calls=%fused_computation.5 | convolution fusion | flops 1491075072 | bytes 6816768 | tf_op jit(solution)/shard_map/dot_general | solution.py:440
  236.2 8.3 %multiply_reduce_fusion = (bf16[1024]{0:T(1024)(128)(2,1)S(1)}, f32[512]{0:T(512)S(1)}, f32[512,1024]{1,0:T(8,128)}) fusion(f32[512,1024]{1,0:T(8,128)S(1)} %copy-done.33, f32[512]{0:T(512)S(1)} %fusion.67, f32[1024]{0:T(1024)S(1)} %bitcast.129, f32[512,1024]{1,0:T(8,128)S(1)} %fusion.28, bf16[1024,2816]{1,0:T(8,128)(2,1)} %collective-permute-done.11, ...), kind=kOutput, calls=%fused_computation.62 | convolution fusion | flops 2962225664 | bytes 14952448 | tf_op jit(solution)/shard_map/dot_general | solution.py:446
  284.5 38.5 %collective-permute-done.14 = bf16[1,4,264,128]{3,2,1,0:T(8,128)(2,1)S(1)} collective-permute-done((bf16[1,4,264,128]{3,2,1,0:T(8,128)(2,1)S(1)}, bf16[1,4,264,128]{3,2,1,0:T(8,128)(2,1)S(1)}, u32[]{:S(2)}, u32[]{:S(2)}) %collective-permute-start.14) | collective-permute-done | bytes 270368 | tf_op jit(solution)/shard_map/ppermute | solution.py:426
  324.4 9.8 %collective-permute-done.16 = bf16[1,4,264,128]{3,2,1,0:T(8,128)(2,1)S(1)} collective-permute-done((bf16[1,4,264,128]{3,2,1,0:T(8,128)(2,1)S(1)}, bf16[1,4,264,128]{3,2,1,0:T(8,128)(2,1)S(1)}, u32[]{:S(2)}, u32[]{:S(2)}) %collective-permute-start.16) | collective-permute-done | bytes 270368 | tf_op jit(solution)/shard_map/ppermute | solution.py:426
  339.6 12.3 %scan_backward.1 = (bf16[512,1536]{1,0:T(8,128)(2,1)S(1)}, bf16[512,1536]{1,0:T(8,128)(2,1)S(1)}, f32[512,512]{1,0:T(8,128)S(1)}) custom-call(f32[512,1536]{1,0:T(8,128)} %copy-done.2, f32[512,1536]{1,0:T(8,128)} %copy-done.2, f32[512,1536]{1,0:T(8,128)} %copy-done.2, f32[512,1536]{1,0:T(8,128)} %copy-done.3, f32[512,1536]{1,0:T(8,128)} %copy-done.3, ...), custom_call_target="tpu_custom_call" | custom-call | tf_op jit(solution)/shard_map/scan_backward/pallas_call | solution.py:353
  367.2 6.6 %fusion.16 = (bf16[1024]{0:T(1024)(128)(2,1)S(1)}, f32[512]{0:T(512)S(1)}, f32[512,1024]{1,0:T(8,128)}) fusion(bf16[1,512,1024]{2,1,0:T(8,128)(2,1)S(1)} %copy-done.40, f32[512]{0:T(512)S(1)} %fusion.66, f32[1024]{0:T(1024)S(1)} %bitcast.138, f32[512,1024]{1,0:T(8,128)} %fusion.94, f32[512,1024]{1,0:T(8,128)} %fusion.5, ...), kind=kOutput, calls=%fused_computation.47 | convolution fusion | flops 1615329792 | bytes 12068864 | tf_op jit(solution)/shard_map/dot_general | solution.py:446
  407.4 19.9 %collective-permute-done.26 = bf16[960,512]{1,0:T(8,128)(2,1)} collective-permute-done((bf16[960,512]{1,0:T(8,128)(2,1)}, bf16[960,512]{1,0:T(8,128)(2,1)}, u32[]{:S(2)}, u32[]{:S(2)}) %collective-permute-start.26) | collective-permute-done | bytes 983072 | tf_op jit(solution)/shard_map/ppermute | solution.py:541
  431.4 6.3 %convolution_bitcast_fusion.1 = f32[1,512,512]{2,1,0:T(8,128)} fusion(bf16[2816,512]{1,0:T(8,128)(2,1)} %constant_dynamic-update-slice_fusion.other_ref, bf16[512,1408]{1,0:T(8,128)(2,1)} %get-tuple-element.97, bf16[512,1408]{1,0:T(8,128)(2,1)} %get-tuple-element.96, pred[]{:T(512)S(6)} %eq.16), kind=kOutput, calls=%fused_computation.104 | convolution fusion | flops 1489371136 | bytes 6815745 | tf_op jit(solution)/shard_map/dot_general | solution.py:436
  442.3 21.8 %collective-permute-start.31 = (bf16[128,2816]{1,0:T(8,128)(2,1)S(1)}, bf16[128,2816]{1,0:T(8,128)(2,1)S(1)}, u32[]{:S(2)}, u32[]{:S(2)}) collective-permute-start(bf16[128,2816]{1,0:T(8,128)(2,1)S(1)} %get-tuple-element.109), channel_id=1, source_target_pairs={{0,8},{24,16},{1,9},{25,17},{2,10},{26,18},{3,11},{27,19},{4,12},{... | collective-permute-start | bytes 2162696 | tf_op jit(solution)/shard_map/ppermute | solution.py:541
  472.5 6.6 %collective-permute-done.32 = bf16[960,512]{1,0:T(8,128)(2,1)} collective-permute-done((bf16[960,512]{1,0:T(8,128)(2,1)S(1)}, bf16[960,512]{1,0:T(8,128)(2,1)}, u32[]{:S(2)}, u32[]{:S(2)}) %collective-permute-start.32) | collective-permute-done | bytes 983072 | tf_op jit(solution)/shard_map/ppermute | solution.py:541
  480.8 11.9 %collective-permute-done.28 = bf16[128,2816]{1,0:T(8,128)(2,1)S(1)} collective-permute-done((bf16[128,2816]{1,0:T(8,128)(2,1)S(1)}, bf16[128,2816]{1,0:T(8,128)(2,1)S(1)}, u32[]{:S(2)}, u32[]{:S(2)}) %collective-permute-start.28) | collective-permute-done | bytes 720928 | tf_op jit(solution)/shard_map/ppermute | solution.py:541
  503.8 18.9 %collective-permute-start.30 = (bf16[128,1664]{1,0:T(8,128)(2,1)S(1)}, bf16[128,1664]{1,0:T(8,128)(2,1)S(1)}, u32[]{:S(2)}, u32[]{:S(2)}) collective-permute-start(bf16[128,1664]{1,0:T(8,128)(2,1)S(1)} %get-tuple-element.126), channel_id=1, source_target_pairs={{0,8},{24,16},{1,9},{25,17},{2,10},{26,18},{3,11},{27,19},{4,12},{... | collective-permute-start | bytes 1277960 | tf_op jit(solution)/shard_map/ppermute | solution.py:541
  535.3 12.8 %collective-permute-done.34 = bf16[128,2816]{1,0:T(8,128)(2,1)S(1)} collective-permute-done((bf16[128,2816]{1,0:T(8,128)(2,1)S(1)}, bf16[128,2816]{1,0:T(8,128)(2,1)S(1)}, u32[]{:S(2)}, u32[]{:S(2)}) %collective-permute-start.34) | collective-permute-done | bytes 720928 | tf_op jit(solution)/shard_map/ppermute | solution.py:541
  548.2 10.3 %collective-permute-done.35 = bf16[128,2816]{1,0:T(8,128)(2,1)S(1)} collective-permute-done((bf16[128,2816]{1,0:T(8,128)(2,1)S(1)}, bf16[128,2816]{1,0:T(8,128)(2,1)S(1)}, u32[]{:S(2)}, u32[]{:S(2)}) %collective-permute-start.35) | collective-permute-done | bytes 720928 | tf_op jit(solution)/shard_map/ppermute | solution.py:541
  564.6 11.7 %collective-permute-done.40 = bf16[128,1664]{1,0:T(8,128)(2,1)S(1)} collective-permute-done((bf16[128,1664]{1,0:T(8,128)(2,1)S(1)}, bf16[128,1664]{1,0:T(8,128)(2,1)S(1)}, u32[]{:S(2)}, u32[]{:S(2)}) %collective-permute-start.40) | collective-permute-done | bytes 426016 | tf_op jit(solution)/shard_map/ppermute | solution.py:541
  576.3 7.7 %collective-permute-done.37 = bf16[128,1664]{1,0:T(8,128)(2,1)S(1)} collective-permute-done((bf16[128,1664]{1,0:T(8,128)(2,1)S(1)}, bf16[128,1664]{1,0:T(8,128)(2,1)S(1)}, u32[]{:S(2)}, u32[]{:S(2)}) %collective-permute-start.37) | collective-permute-done | bytes 426016 | tf_op jit(solution)/shard_map/ppermute | solution.py:541
  (455 shorter events, 281.2 us)
Async XLA Ops:
  7.2 64.1 %all-gather.3.cloned.1.call-start = ((), (), s32[]{:S(2)}) async-start(), calls=%async_computation.2 | async-start | bytes 4259840 | tf_op jit(solution)/shard_map/all_gather | solution.py:599
  16.5 152.3 %all-gather.5.cloned.1.call-start = ((), (), s32[]{:S(2)}) async-start(), calls=%async_computation.3 | async-start | bytes 7208960 | tf_op jit(solution)/shard_map/all_gather | solution.py:600
  19.0 421.7 %reduce-scatter.5.cloned.1.call-start = ((), (), s32[]{:S(2)}) async-start(), calls=%async_computation.5 | async-start | bytes 7208960 | tf_op jit(solution)/shard_map/reduce_scatter | solution.py:499
  75.4 56.7 %collective-permute-start.9 = (bf16[704,512]{1,0:T(8,128)(2,1)}, bf16[704,512]{1,0:T(8,128)(2,1)}, u32[]{:S(2)}, u32[]{:S(2)}) collective-permute-start(bf16[704,512]{1,0:T(8,128)(2,1)} %after.21), channel_id=1, source_target_pairs={{0,3},{1,2},{2,1},{3,0},{4,7},{5,6},{6,5},{7,4},{8,11},{9,10},{10,... | collective-permute-start | bytes 2162696 | tf_op jit(solution)/shard_map/ppermute | solution.py:514
  77.0 51.7 %collective-permute-start.8 = (bf16[704,512]{1,0:T(8,128)(2,1)}, bf16[704,512]{1,0:T(8,128)(2,1)}, u32[]{:S(2)}, u32[]{:S(2)}) collective-permute-start(bf16[704,512]{1,0:T(8,128)(2,1)} %after.21), channel_id=1, source_target_pairs={{0,2},{1,3},{2,0},{3,1},{4,6},{5,7},{6,4},{7,5},{8,10},{9,11},{10,... | collective-permute-start | bytes 2162696 | tf_op jit(solution)/shard_map/ppermute | solution.py:514
  78.4 48.2 %collective-permute-start.7 = (bf16[704,512]{1,0:T(8,128)(2,1)}, bf16[704,512]{1,0:T(8,128)(2,1)}, u32[]{:S(2)}, u32[]{:S(2)}) collective-permute-start(bf16[704,512]{1,0:T(8,128)(2,1)} %after.21), channel_id=1, source_target_pairs={{0,1},{1,0},{2,3},{3,2},{4,5},{5,4},{6,7},{7,6},{8,9},{9,8},{10,11... | collective-permute-start | bytes 2162696 | tf_op jit(solution)/shard_map/ppermute | solution.py:514
  98.9 38.6 %collective-permute-start.4 = (bf16[1,4,264,128]{3,2,1,0:T(8,128)(2,1)S(1)}, bf16[1,4,264,128]{3,2,1,0:T(8,128)(2,1)S(1)}, u32[]{:S(2)}, u32[]{:S(2)}) collective-permute-start(bf16[1,4,264,128]{3,2,1,0:T(8,128)(2,1)S(1)} %convert_element_type.358), channel_id=1, source_target_pairs={{0,1},{1,2},{2,3},{4,5},{5,6},{6,7},{8,9},{9,10},{10,11},{12,13},{... | collective-permute-start | bytes 811016 | tf_op jit(solution)/shard_map/ppermute | solution.py:426
  168.8 26.8 %collective-permute-start.11 = (bf16[1024,2816]{1,0:T(8,128)(2,1)}, bf16[1024,2816]{1,0:T(8,128)(2,1)}, u32[]{:S(2)}, u32[]{:S(2)}) collective-permute-start(bf16[1024,2816]{1,0:T(8,128)(2,1)} %after.23), channel_id=1, source_target_pairs={{0,4},{4,0},{1,5},{5,1},{2,6},{6,2},{3,7},{7,3},{8,12},{12,8},{9,1... | collective-permute-start | bytes 17301512 | tf_op jit(solution)/shard_map/ppermute | solution.py:455
  224.2 278.4 %reduce-scatter.3.cloned.1.call-start = ((), (), s32[]{:S(2)}) async-start(), calls=%async_computation.4 | async-start | bytes 4259840 | tf_op jit(solution)/shard_map/reduce_scatter | solution.py:499
  262.0 113.0 %collective-permute-start.19 = (bf16[704,512]{1,0:T(8,128)(2,1)}, bf16[704,512]{1,0:T(8,128)(2,1)}, u32[]{:S(2)}, u32[]{:S(2)}) collective-permute-start(bf16[704,512]{1,0:T(8,128)(2,1)} %get-tuple-element.98), channel_id=1, source_target_pairs={{0,1},{1,0},{2,3},{3,2},{4,5},{5,4},{6,7},{7,6},{8,9},{9,8},{10,11... | collective-permute-start | bytes 2162696 | tf_op jit(solution)/shard_map/ppermute | solution.py:527
  267.5 107.5 %collective-permute-start.21 = (bf16[704,512]{1,0:T(8,128)(2,1)}, bf16[704,512]{1,0:T(8,128)(2,1)}, u32[]{:S(2)}, u32[]{:S(2)}) collective-permute-start(bf16[704,512]{1,0:T(8,128)(2,1)} %get-tuple-element.99), channel_id=1, source_target_pairs={{0,3},{1,2},{2,1},{3,0},{4,7},{5,6},{6,5},{7,4},{8,11},{9,10},{10,... | collective-permute-start | bytes 2162696 | tf_op jit(solution)/shard_map/ppermute | solution.py:527
  270.3 104.7 %collective-permute-start.20 = (bf16[704,512]{1,0:T(8,128)(2,1)}, bf16[704,512]{1,0:T(8,128)(2,1)}, u32[]{:S(2)}, u32[]{:S(2)}) collective-permute-start(bf16[704,512]{1,0:T(8,128)(2,1)} %get-tuple-element.100), channel_id=1, source_target_pairs={{0,2},{1,3},{2,0},{3,1},{4,6},{5,7},{6,4},{7,5},{8,10},{9,11},{10,... | collective-permute-start | bytes 2162696 | tf_op jit(solution)/shard_map/ppermute | solution.py:527
  279.6 44.7 %collective-permute-start.15 = (bf16[1,4,264,128]{3,2,1,0:T(8,128)(2,1)S(1)}, bf16[1,4,264,128]{3,2,1,0:T(8,128)(2,1)S(1)}, u32[]{:S(2)}, u32[]{:S(2)}) collective-permute-start(bf16[1,4,264,128]{3,2,1,0:T(8,128)(2,1)S(1)} %pad_maximum_fusion.17), channel_id=1, source_target_pairs={{2,0},{3,1},{6,4},{7,5},{10,8},{11,9},{14,12},{15,13},{18,16},{19,... | collective-permute-start | bytes 811016 | tf_op jit(solution)/shard_map/ppermute | solution.py:426
  281.2 41.7 %collective-permute-start.14 = (bf16[1,4,264,128]{3,2,1,0:T(8,128)(2,1)S(1)}, bf16[1,4,264,128]{3,2,1,0:T(8,128)(2,1)S(1)}, u32[]{:S(2)}, u32[]{:S(2)}) collective-permute-start(bf16[1,4,264,128]{3,2,1,0:T(8,128)(2,1)S(1)} %pad_maximum_fusion.17), channel_id=1, source_target_pairs={{1,0},{2,1},{3,2},{5,4},{6,5},{7,6},{9,8},{10,9},{11,10},{13,12},{... | collective-permute-start | bytes 811016 | tf_op jit(solution)/shard_map/ppermute | solution.py:426
  324.3 50.7 %collective-permute-start.22 = (bf16[1024,512]{1,0:T(8,128)(2,1)}, bf16[1024,512]{1,0:T(8,128)(2,1)}, u32[]{:S(2)}, u32[]{:S(2)}) collective-permute-start(bf16[1024,512]{1,0:T(8,128)(2,1)} %convolution_convert_fusion.3), channel_id=1, source_target_pairs={{0,4},{4,0},{1,5},{5,1},{2,6},{6,2},{3,7},{7,3},{8,12},{12,8},{9,1... | collective-permute-start | bytes 3145736 | tf_op jit(solution)/shard_map/ppermute | solution.py:455
  357.6 39.2 %collective-permute-start.17 = (bf16[1024,1536]{1,0:T(8,128)(2,1)}, bf16[1024,1536]{1,0:T(8,128)(2,1)}, u32[]{:S(2)}, u32[]{:S(2)}) collective-permute-start(bf16[1024,1536]{1,0:T(8,128)(2,1)} %convolution_convert_fusion.2), channel_id=1, source_target_pairs={{0,4},{4,0},{1,5},{5,1},{2,6},{6,2},{3,7},{7,3},{8,12},{12,8},{9,1... | collective-permute-start | bytes 9437192 | tf_op jit(solution)/shard_map/ppermute | solution.py:455
  439.4 39.8 %collective-permute-start.32 = (bf16[960,512]{1,0:T(8,128)(2,1)S(1)}, bf16[960,512]{1,0:T(8,128)(2,1)}, u32[]{:S(2)}, u32[]{:S(2)}) collective-permute-start(bf16[960,512]{1,0:T(8,128)(2,1)S(1)} %add_convert_fusion.4.other_ref), channel_id=1, source_target_pairs={{8,0},{16,24},{9,1},{17,25},{10,2},{18,26},{11,3},{19,27},{12,4},{... | collective-permute-start | bytes 2949128 | tf_op jit(solution)/shard_map/ppermute | solution.py:541
  442.3 38.4 %collective-permute-start.31 = (bf16[128,2816]{1,0:T(8,128)(2,1)S(1)}, bf16[128,2816]{1,0:T(8,128)(2,1)S(1)}, u32[]{:S(2)}, u32[]{:S(2)}) collective-permute-start(bf16[128,2816]{1,0:T(8,128)(2,1)S(1)} %get-tuple-element.109), channel_id=1, source_target_pairs={{0,8},{24,16},{1,9},{25,17},{2,10},{26,18},{3,11},{27,19},{4,12},{... | collective-permute-start | bytes 2162696 | tf_op jit(solution)/shard_map/ppermute | solution.py:541
  464.2 28.5 %collective-permute-start.28 = (bf16[128,2816]{1,0:T(8,128)(2,1)S(1)}, bf16[128,2816]{1,0:T(8,128)(2,1)S(1)}, u32[]{:S(2)}, u32[]{:S(2)}) collective-permute-start(bf16[128,2816]{1,0:T(8,128)(2,1)S(1)} %get-tuple-element.110), channel_id=1, source_target_pairs={{0,8},{24,16},{1,9},{25,17},{2,10},{26,18},{3,11},{27,19},{4,12},{... | collective-permute-start | bytes 2162696 | tf_op jit(solution)/shard_map/ppermute | solution.py:541
  498.9 25.4 %collective-permute-start.33 = (bf16[128,2816]{1,0:T(8,128)(2,1)}, bf16[128,2816]{1,0:T(8,128)(2,1)}, u32[]{:S(2)}, u32[]{:S(2)}) collective-permute-start(bf16[128,2816]{1,0:T(8,128)(2,1)} %after.36), channel_id=1, source_target_pairs={{8,16},{16,8},{9,17},{17,9},{10,18},{18,10},{11,19},{19,11},{12,20... | collective-permute-start | bytes 2162696 | tf_op jit(solution)/shard_map/ppermute | solution.py:541
  503.8 27.4 %collective-permute-start.30 = (bf16[128,1664]{1,0:T(8,128)(2,1)S(1)}, bf16[128,1664]{1,0:T(8,128)(2,1)S(1)}, u32[]{:S(2)}, u32[]{:S(2)}) collective-permute-start(bf16[128,1664]{1,0:T(8,128)(2,1)S(1)} %get-tuple-element.126), channel_id=1, source_target_pairs={{0,8},{24,16},{1,9},{25,17},{2,10},{26,18},{3,11},{27,19},{4,12},{... | collective-permute-start | bytes 1277960 | tf_op jit(solution)/shard_map/ppermute | solution.py:541
  530.0 28.5 %collective-permute-start.35 = (bf16[128,2816]{1,0:T(8,128)(2,1)S(1)}, bf16[128,2816]{1,0:T(8,128)(2,1)S(1)}, u32[]{:S(2)}, u32[]{:S(2)}) collective-permute-start(bf16[128,2816]{1,0:T(8,128)(2,1)S(1)} %copy-done.54), channel_id=1, source_target_pairs={{8,0},{16,24},{9,1},{17,25},{10,2},{18,26},{11,3},{19,27},{12,4},{... | collective-permute-start | bytes 2162696 | tf_op jit(solution)/shard_map/ppermute | solution.py:541
  533.9 26.8 %collective-permute-start.39 = (bf16[128,1664]{1,0:T(8,128)(2,1)S(1)}, bf16[128,1664]{1,0:T(8,128)(2,1)}, u32[]{:S(2)}, u32[]{:S(2)}) collective-permute-start(bf16[128,1664]{1,0:T(8,128)(2,1)S(1)} %get-tuple-element.125), channel_id=1, source_target_pairs={{8,16},{16,8},{9,17},{17,9},{10,18},{18,10},{11,19},{19,11},{12,20... | collective-permute-start | bytes 1277960 | tf_op jit(solution)/shard_map/ppermute | solution.py:541
  558.7 26.3 %collective-permute-start.43 = (bf16[256,2816]{1,0:T(8,128)(2,1)S(1)}, bf16[256,2816]{1,0:T(8,128)(2,1)}, u32[]{:S(2)}, u32[]{:S(2)}) collective-permute-start(bf16[256,2816]{1,0:T(8,128)(2,1)S(1)} %pad_maximum_fusion.10.other_ref), channel_id=1, source_target_pairs={{0,4},{4,0},{1,5},{5,1},{2,6},{6,2},{3,7},{7,3},{8,12},{12,8},{9,1... | collective-permute-start | bytes 4325384 | tf_op jit(solution)/shard_map/ppermute | solution.py:455
  (124 other events, 1352.9 us)
Sparse Core Ops, SparseCore 0:
  16.6 54.6 all-gather.2
  73.7 95.0 all-gather.4
  224.3 103.0 reduce-scatter.4
  407.5 45.4 reduce-scatter.2

commit v5 on v4

--- a/solution.py
+++ b/solution.py
@@ -602,6 +602,7 @@
     mixer_mine = after(after(mixer_mine, output_mine), ffn_packed)
     down_mine = spread(after(own_half(down_weight, 1), mixer_mine))
     mixer_theirs, output_theirs = swapped(mixer_mine), swapped(output_mine)
+    mixer_theirs = after(mixer_theirs, output_theirs)
     projection_mine, projection_theirs = mixer_mine[:, :PACKED], mixer_theirs[:, :PACKED]
     small_all = mixer_mine[:, PACKED:].reshape(count, -1)
     pieces, begin = [], 0
@@ -640,10 +641,10 @@
     attended, mixed = mix_forward(
         local_out, forget, incoming_state, mine, theirs, head_gain_f[None, :], seqs_here, chunk
     )
-    ffn_mine = after(ffn_mine, mixed)
     mixed = jnp.concatenate(halves_of(mixed), 1)
     resid = inputs + joined(product(mixed, output_mine), product(mixed, output_theirs), 1)
     normed_two = first_norm(resid, gain_two).astype(jnp.bfloat16)
+    ffn_mine = after(ffn_mine, normed_two)
     ffn_theirs = swapped(ffn_mine)
 
     def swiglu(both):
@@ -659,7 +660,6 @@
     grad_low = cotangent.reshape(rows_here, width)
     grad_out = grad_low.astype(jnp.float32)
     low_mine, low_theirs = halves_of(grad_low)
-    down_came = swapped(low(product_left(hidden, low_theirs)))
     hidden_grad = product_right(low_mine, down_mine) + product_right(low_theirs, down_theirs)
 
     def swiglu_back(both, grad):
@@ -675,7 +675,6 @@
 
     grad_mine, grad_theirs = halves_of(hidden_grad)
     back_mine, back_theirs = swiglu_back(both_mine, grad_mine), swiglu_back(both_theirs, grad_theirs)
-    down_pair = low(product_left(hidden, low_mine) + down_came.astype(jnp.float32))
 
     ffn_came = swapped(low(product_left(normed_two, back_theirs)))
     normed_two_grad = product_right(back_mine, ffn_mine) + product_right(back_theirs, ffn_theirs)
@@ -689,10 +688,6 @@
     ffn_pair = low(product_left(normed_two, back_mine) + ffn_came.astype(jnp.float32))
     ffn_share = scattered(ffn_pair)
     mixed_grad = after(mixed_grad, ffn_pair)
-    mixed_later = after(mixed, mixed_grad)
-    output_came = swapped(low(product_left(mixed_later, branch_theirs)))
-    output_pair = low(product_left(mixed_later, branch_mine) + output_came.astype(jnp.float32))
-
     attended_grad, *outgate_grads, state_grad, head_gain_grad = mix_backward(
         mixed_grad, attended, mine, theirs, head_gain_f[None, :], forget, seqs_here, chunk
     )
@@ -700,21 +695,26 @@
     later_grad = from_neighbours(
         jnp.concatenate([state_grad, summary[:, :, DV:]], axis=2).astype(jnp.bfloat16), -1
     )
+    down_came = swapped(low(product_left(hidden, after(low_theirs, attended_grad))))
+    down_pair = low(product_left(hidden, after(low_mine, attended_grad)) + down_came.astype(jnp.float32))
     packed_mine, packed_theirs, gates_grad = scan_backward(
         mine, theirs, gates, scores, states, starts, incoming_state,
         attended_grad, later_grad, outgate_grads, seqs_here, chunk,
     )
     packed_came = swapped(low(product_left(normed_one, packed_theirs)))
-    down_share = gathered_sum(down_pair, gates_grad)
-    output_share = gathered_sum(output_pair, gates_grad)
+    mixer_pair = low(product_left(normed_one, packed_mine) + packed_came.astype(jnp.float32))
+    mixer_share = gathered_sum(mixer_pair, mixer_pair)
+    down_share = gathered_sum(after(down_pair, mixer_pair), mixer_share)
+    output_came = swapped(low(product_left(mixed, after(branch_theirs, mixer_pair))))
+    output_pair = product_left(mixed, after(branch_mine, mixer_pair)) + output_came.astype(jnp.float32)
     gate_pulled = jax.vjp(gate_fn, low_rank, decay_up_f, decay_bias_f)[1](gates_grad)
     low_rank_grad = gate_pulled[0].astype(jnp.bfloat16)
     decay_up_grad = jnp.concatenate(halves_of(gate_pulled[1]), 1)
     decay_bias_grad = jnp.concatenate(halves_of(gate_pulled[2]), 1)[0]
     decay_down_grad = product_left(normed_one, low_rank_grad)
     normed_one_grad = (
-        product_right(packed_mine, projection_mine)
-        + product_right(packed_theirs, projection_theirs)
+        product_right(after(packed_mine, mixer_pair), projection_mine)
+        + product_right(after(packed_theirs, mixer_pair), projection_theirs)
         + product_right(low_rank_grad, decay_down_all)
     )
     first_pulled = jax.vjp(first_norm, inputs, gain_one)[1](normed_one_grad)
@@ -735,29 +735,30 @@
         ],
         axis=1,
     )
-    small_grads = jnp.pad(low(small_grads), ((0, 0), (0, shard_rows * extra - flat_size)))
-    mixer_pair = jnp.concatenate(
+    small_rows = -(-flat_size // (width // 2 * 16)) * 16
+    small_grads = jnp.pad(low(small_grads), ((0, 0), (0, small_rows * width // 2 - flat_size)))
+    rest_pair = jnp.concatenate(
         [
-            low(product_left(normed_one, packed_mine) + packed_came.astype(jnp.float32)),
-            small_grads.reshape(count * shard_rows, extra),
+            low(output_pair).reshape(count, shard_rows, width // 2),
+            small_grads.reshape(count, small_rows, width // 2),
         ],
         axis=1,
-    )
-    mixer_share = scattered(mixer_pair)
-
-    others = after(jnp.concatenate([down_share, output_share], 0), mixer_pair)
-    others_total, others_middle = line_sum(others, 1)
-    others_other = swapped(others_total)
-    ffn_total, ffn_middle = line_sum(after(ffn_share, others_middle), 2, others_total)
+    ).reshape(-1, width // 2)
+    rest_share = gathered_sum(rest_pair, mixer_pair)
+
+    ffn_total, ffn_middle = line_sum(after(ffn_share, mixer_pair), 2)
     ffn_other = swapped(ffn_total)
-    mixer_total, _ = line_sum(after(mixer_share, ffn_middle), 2, ffn_total)
+    mixer_total, mixer_middle = line_sum(after(mixer_share, ffn_middle), 2, ffn_total)
     mixer_other = swapped(mixer_total)
-    down_rows = down_weight.shape[0]
+    down_total, down_middle = line_sum(after(down_share, mixer_middle), 1, mixer_total)
+    down_other = swapped(down_total)
+    rest_total, _ = line_sum(after(rest_share, down_middle), 1, down_total)
+    rest_other = swapped(rest_total)
 
     def both_cores(total, other, begin, end):
         return joined(total[:, begin:end], other[:, begin:end], 1).astype(jnp.float32)
 
-    summed = mixer_total[:, PACKED:].astype(jnp.float32) + mixer_other[:, PACKED:].astype(jnp.float32)
+    summed = rest_total[shard_rows:].astype(jnp.float32) + rest_other[shard_rows:].astype(jnp.float32)
     summed, shares, begin = summed.reshape(-1), [], 0
     for small in smalls:
         shares.append(summed[begin : begin + small.size].reshape(small.shape))
@@ -779,11 +780,11 @@
         shares[3],
         outgate_g,
         shares[4],
-        joined(others_total[down_rows:], others_other[down_rows:], 1).astype(jnp.float32),
+        joined(rest_total[:shard_rows], rest_other[:shard_rows], 1).astype(jnp.float32),
         shares[5],
         both_cores(ffn_total, ffn_other, 0, ff // 2),
         both_cores(ffn_total, ffn_other, ff // 2, ff),
-        joined(others_total[:down_rows], others_other[:down_rows], 1).astype(jnp.float32),
+        joined(down_total, down_other, 1).astype(jnp.float32),
     )
 
 

time: 614 us -> 583 us (0.950)
  waiting for transfers between devices: 246 us -> 192 us
  other arithmetic: 49.6 us -> 65.2 us
  matrix products: 103 us -> 112 us
    ppermute x6, waiting for transfers between devices: 59.8 us -> 25.2 us  [from_neighbours(): came = lax.ppermute(summary, 'seq', pairs)]
    ppermute x6 -> x9, waiting for transfers between devices: 10.2 us -> 39.9 us  [gathered_sum(): came = lax.ppermute(piece, 'seq', [(i, i ^ distance) for i in range(count)])]
    ppermute x15 -> x18, waiting for transfers between devices: 82.6 us -> 53 us  [send(): return [lax.ppermute(total, 'z', pairs) for total in totals]]
    ppermute x11 -> x12, waiting for transfers between devices: 12.7 us -> 2.43 us  [swapped(): return lax.ppermute(array, 'core', [(0, 1), (1, 0)])]
    all_gather x1, waiting for transfers between devices: 8.85 us -> 1.36 us  [local(): ffn_mine = lax.all_gather(ffn_packed, 'seq', tiled=True)]
    dot_general x9, matrix products: 32.5 us -> 39.2 us  [product_left(): lax.dot_general(left, right, (((0,), (0,)), ((), ())), preferred_element_...]
    unnamed x208 -> x254, local copies, waits for them, and re-layouts: 39.8 us -> 34.5 us
    convert_element_type x12 -> x15, other arithmetic: 19 us -> 21.7 us  [low(): return array.astype(jnp.bfloat16)]
  transfers between devices with their start and end apart: 48 -> 54, of which waited for: 24 -> 24; matrix products, arithmetic and copies ran while one was open for 26% -> 33% of each run, Pallas kernels for 4% -> 4%
where the time goes in v5:
time: 583 us; the launch traced here: 572 us
  waiting for transfers between devices  192 us (33%)
  matrix products  112 us (19%)
  starting transfers between devices  91.1 us (16%)
  local copies, waits for them, and re-layouts  72.9 us (13%)
  other arithmetic  65.2 us (11%)
  Pallas kernels  23.6 us (4%)
  between operations  16 us (3%)
    ppermute x18, starting transfers between devices, send(): return [lax.ppermute(total, 'z', pairs) for total in totals]  60.3 us
    ppermute x18, waiting for transfers between devices, send(): return [lax.ppermute(total, 'z', pairs) for total in totals]  53 us
    ppermute x6, waiting for transfers between devices, spread(): came = lax.ppermute(array, 'seq', [(i, i ^ distance) for i in range(count)])  42.2 us
    ppermute x9, waiting for transfers between devices, gathered_sum(): came = lax.ppermute(piece, 'seq', [(i, i ^ distance) for i in range(count)])  39.9 us
    dot_general x9, matrix products, product_left(): lax.dot_general(left, right, (((0,), (0,)), ((), ())), preferred_element_...  39.2 us
    dot_general x9, matrix products, product_right(): lax.dot_general(left, right, (((1,), (1,)), ((), ())), preferred_element_...  36.9 us
    unnamed x254, local copies, waits for them, and re-layouts  34.5 us
    dot_general x9, matrix products, product(): return jnp.dot(left, right, preferred_element_type=jnp.float32)  30.9 us
  transfers between devices with their start and end apart: 54, of which 24 were waited for; matrix products, arithmetic and copies ran while one was open for 33% of the time, Pallas kernels for 4%

profile of v5, /device:TPU:0, one launch (start us, length us, event | category | flops | bytes accessed | tf_op | source)
XLA Modules:
  0.0 572.3 jit_solution(3994850866976569423)
XLA Ops:
  25.3 8.1 %collective-permute-done = bf16[256,512]{1,0:T(8,128)(2,1)S(1)} collective-permute-done((bf16[256,512]{1,0:T(8,128)(2,1)S(1)}, bf16[256,512]{1,0:T(8,128)(2,1)S(1)}, u32[]{:S(2)}, u32[]{:S(2)}) %collective-permute-start) | collective-permute-done | bytes 262176 | tf_op jit(solution)/shard_map/ppermute | solution.py:514
  45.0 27.8 %all-gather.3.cloned.1.call-done.array_ref = bf16[1024,1664]{1,0:T(8,128)(2,1)} async-done(((bf16[256,1664]{1,0:T(8,128)(2,1)}), bf16[1024,1664]{1,0:T(8,128)(2,1)}) %all-gather.3.cloned.1.call-update) | async-done | bytes 3407888 | tf_op jit(solution)/shard_map/all_gather | solution.py:599
  103.5 24.6 %collective-permute-done.8 = bf16[704,512]{1,0:T(8,128)(2,1)} collective-permute-done((bf16[704,512]{1,0:T(8,128)(2,1)}, bf16[704,512]{1,0:T(8,128)(2,1)}, u32[]{:S(2)}, u32[]{:S(2)}) %collective-permute-start.8) | collective-permute-done | bytes 720928 | tf_op jit(solution)/shard_map/ppermute | solution.py:514
  139.2 7.2 %collective-permute-done.6 = bf16[1,4,264,128]{3,2,1,0:T(8,128)(2,1)S(1)} collective-permute-done((bf16[1,4,264,128]{3,2,1,0:T(8,128)(2,1)S(1)}, bf16[1,4,264,128]{3,2,1,0:T(8,128)(2,1)S(1)}, u32[]{:S(2)}, u32[]{:S(2)}) %collective-permute-start.6) | collective-permute-done | bytes 270368 | tf_op jit(solution)/shard_map/ppermute | solution.py:426
  176.9 6.2 %fusion.90 = f32[512,2816]{1,0:T(8,128)S(1)} fusion(bf16[512,1024]{1,0:T(8,128)(2,1)S(1)} %copy-done.68, bf16[1024,2816]{1,0:T(8,128)(2,1)} %after.36), kind=kOutput, calls=%fused_computation.240 | convolution fusion | flops 2952790016 | bytes 12582912 | tf_op jit(solution)/shard_map/dot_general | solution.py:436
  189.4 5.8 %fusion.91 = f32[512,2816]{1,0:T(8,128)S(1)} fusion(bf16[512,1024]{1,0:T(8,128)(2,1)S(1)} %copy-done.68, bf16[1024,2816]{1,0:T(8,128)(2,1)} %collective-permute-done.11), kind=kOutput, calls=%fused_computation.241 | convolution fusion | flops 2952790016 | bytes 12582912 | tf_op jit(solution)/shard_map/dot_general | solution.py:436
  205.4 8.2 %fusion.28 = f32[512,1024]{1,0:T(8,128)} fusion(bf16[1024,2816]{1,0:T(8,128)(2,1)} %after.36, bf16[512,1408]{1,0:T(8,128)(2,1)} %get-tuple-element.78, bf16[512,1408]{1,0:T(8,128)(2,1)} %get-tuple-element.79), kind=kOutput, calls=%fused_computation.68 | convolution fusion | flops 2958557184 | bytes 10747904 | tf_op jit(solution)/shard_map/dot_general | solution.py:446
  215.0 6.9 %add_convert_fusion.other_ref = bf16[1024,2816]{1,0:T(8,128)(2,1)} fusion(bf16[1024,2816]{1,0:T(8,128)(2,1)} %collective-permute-done.13, bf16[512,1024]{1,0:T(8,128)(2,1)S(1)} %copy-done.69, bf16[512,1408]{1,0:T(8,128)(2,1)S(1)} %copy-done.96, bf16[512,1408]{1,0:T(8,128)(2,1)S(1)} %copy-done.97), kind=kOutput, calls=%fused_computation | convolution fusion | flops 2967207936 | bytes 15466496 | tf_op jit(solution)/shard_map/dot_general | solution.py:440
  221.9 8.2 %multiply_reduce_fusion = (bf16[1024]{0:T(1024)(128)(2,1)S(1)}, f32[512]{0:T(512)S(1)}, f32[512,1024]{1,0:T(8,128)S(1)}) fusion(f32[512,1024]{1,0:T(8,128)} %get-tuple-element.71, f32[512]{0:T(512)S(1)} %fusion.62, f32[1024]{0:T(1024)S(1)} %bitcast.137, f32[512,1024]{1,0:T(8,128)} %fusion.28, bf16[1024,2816]{1,0:T(8,128)(2,1)} %collective-permute-done.11, ...), kind=kOutput, calls=%fused_computation.60 | convolution fusion | flops 2962225664 | bytes 14952448 | tf_op jit(solution)/shard_map/dot_general | solution.py:446
  260.9 6.2 %convolution_convert_fusion.1 = bf16[2816,512]{1,0:T(8,128)(2,1)} fusion(bf16[512,512]{1,0:T(8,128)(2,1)} %after.47, bf16[512,1408]{1,0:T(8,128)(2,1)} %get-tuple-element.81, bf16[512,1408]{1,0:T(8,128)(2,1)} %get-tuple-element.80, pred[]{:T(512)S(6)} %eq.16), kind=kOutput, calls=%fused_computation.5 | convolution fusion | flops 1490812928 | bytes 6291457 | tf_op jit(solution)/shard_map/dot_general | solution.py:440
  267.1 8.4 %collective-permute-done.14 = bf16[1,4,264,128]{3,2,1,0:T(8,128)(2,1)S(1)} collective-permute-done((bf16[1,4,264,128]{3,2,1,0:T(8,128)(2,1)S(1)}, bf16[1,4,264,128]{3,2,1,0:T(8,128)(2,1)S(1)}, u32[]{:S(2)}, u32[]{:S(2)}) %collective-permute-start.14) | collective-permute-done | bytes 270368 | tf_op jit(solution)/shard_map/ppermute | solution.py:426
  280.7 12.0 %scan_backward.1 = (bf16[512,1536]{1,0:T(8,128)(2,1)S(1)}, bf16[512,1536]{1,0:T(8,128)(2,1)S(1)}, f32[512,512]{1,0:T(8,128)S(1)}) custom-call(f32[512,1536]{1,0:T(8,128)} %copy-done.2, f32[512,1536]{1,0:T(8,128)} %copy-done.2, f32[512,1536]{1,0:T(8,128)} %copy-done.2, f32[512,1536]{1,0:T(8,128)} %copy-done.3, f32[512,1536]{1,0:T(8,128)} %copy-done.3, ...), custom_call_target="tpu_custom_call" | custom-call | tf_op jit(solution)/shard_map/scan_backward/pallas_call | solution.py:353
  318.9 6.3 %add_convert_fusion.2.array_ref = bf16[2816,512]{1,0:T(8,128)(2,1)} fusion(bf16[2816,512]{1,0:T(8,128)(2,1)} %collective-permute-done.22, bf16[512,512]{1,0:T(8,128)(2,1)S(1)} %copy-done.58, bf16[512,1408]{1,0:T(8,128)(2,1)} %get-tuple-element.81, bf16[512,1408]{1,0:T(8,128)(2,1)S(1)} %copy-done.91, pred[]{:T(512)S(6)} %eq.16), kind=kOutput, calls=%fused_computation.2 | convolution fusion | flops 1493696512 | bytes 9175041 | tf_op jit(solution)/shard_map/dot_general | solution.py:440
  363.9 16.7 %collective-permute-done.26.array_ref = bf16[256,1536]{1,0:T(8,128)(2,1)} collective-permute-done((bf16[256,1536]{1,0:T(8,128)(2,1)}, bf16[256,1536]{1,0:T(8,128)(2,1)}, u32[]{:S(2)}, u32[]{:S(2)}) %collective-permute-start.26) | collective-permute-done | bytes 786464 | tf_op jit(solution)/shard_map/ppermute | solution.py:527
  393.0 20.7 %collective-permute-done.28.array_ref = bf16[704,512]{1,0:T(8,128)(2,1)} collective-permute-done((bf16[704,512]{1,0:T(8,128)(2,1)}, bf16[704,512]{1,0:T(8,128)(2,1)}, u32[]{:S(2)}, u32[]{:S(2)}) %collective-permute-start.28) | collective-permute-done | bytes 720928 | tf_op jit(solution)/shard_map/ppermute | solution.py:527
  427.5 6.9 %collective-permute-start.34 = (bf16[128,1536]{1,0:T(8,128)(2,1)}, bf16[128,1536]{1,0:T(8,128)(2,1)}, u32[]{:S(2)}, u32[]{:S(2)}) collective-permute-start(bf16[128,1536]{1,0:T(8,128)(2,1)} %get-tuple-element.117), channel_id=1, source_target_pairs={{0,8},{24,16},{1,9},{25,17},{2,10},{26,18},{3,11},{27,19},{4,12},{... | collective-permute-start | bytes 1179656 | tf_op jit(solution)/shard_map/ppermute | solution.py:541
  434.4 9.5 %collective-permute-start.31 = (bf16[128,1536]{1,0:T(8,128)(2,1)}, bf16[128,1536]{1,0:T(8,128)(2,1)}, u32[]{:S(2)}, u32[]{:S(2)}) collective-permute-start(bf16[128,1536]{1,0:T(8,128)(2,1)} %get-tuple-element.118), channel_id=1, source_target_pairs={{0,8},{24,16},{1,9},{25,17},{2,10},{26,18},{3,11},{27,19},{4,12},{... | collective-permute-start | bytes 1179656 | tf_op jit(solution)/shard_map/ppermute | solution.py:541
  455.0 10.0 %collective-permute-done.37 = bf16[128,2816]{1,0:T(8,128)(2,1)S(1)} collective-permute-done((bf16[128,2816]{1,0:T(8,128)(2,1)S(1)}, bf16[128,2816]{1,0:T(8,128)(2,1)S(1)}, u32[]{:S(2)}, u32[]{:S(2)}) %collective-permute-start.37) | collective-permute-done | bytes 720928 | tf_op jit(solution)/shard_map/ppermute | solution.py:541
  465.1 10.3 %collective-permute-done.38 = bf16[128,2816]{1,0:T(8,128)(2,1)S(1)} collective-permute-done((bf16[128,2816]{1,0:T(8,128)(2,1)S(1)}, bf16[128,2816]{1,0:T(8,128)(2,1)S(1)}, u32[]{:S(2)}, u32[]{:S(2)}) %collective-permute-start.38) | collective-permute-done | bytes 720928 | tf_op jit(solution)/shard_map/ppermute | solution.py:541
  486.1 5.9 %collective-permute-done.41 = bf16[128,1536]{1,0:T(8,128)(2,1)S(1)} collective-permute-done((bf16[128,1536]{1,0:T(8,128)(2,1)S(1)}, bf16[128,1536]{1,0:T(8,128)(2,1)S(1)}, u32[]{:S(2)}, u32[]{:S(2)}) %collective-permute-start.41) | collective-permute-done | bytes 393248 | tf_op jit(solution)/shard_map/ppermute | solution.py:541
  492.0 8.4 %collective-permute-done.40 = bf16[128,1536]{1,0:T(8,128)(2,1)S(1)} collective-permute-done((bf16[128,1536]{1,0:T(8,128)(2,1)S(1)}, bf16[128,1536]{1,0:T(8,128)(2,1)S(1)}, u32[]{:S(2)}, u32[]{:S(2)}) %collective-permute-start.40) | collective-permute-done | bytes 393248 | tf_op jit(solution)/shard_map/ppermute | solution.py:541
  508.7 19.2 %collective-permute-start.43 = (bf16[272,512]{1,0:T(8,128)(2,1)}, bf16[272,512]{1,0:T(8,128)(2,1)S(1)}, u32[]{:S(2)}, u32[]{:S(2)}) collective-permute-start(bf16[272,512]{1,0:T(8,128)(2,1)} %after.60), channel_id=1, source_target_pairs={{0,8},{24,16},{1,9},{25,17},{2,10},{26,18},{3,11},{27,19},{4,12},{... | collective-permute-start | bytes 835592 | tf_op jit(solution)/shard_map/ppermute | solution.py:541
  533.6 6.3 %collective-permute-done.44 = bf16[704,512]{1,0:T(8,128)(2,1)} collective-permute-done((bf16[704,512]{1,0:T(8,128)(2,1)S(1)}, bf16[704,512]{1,0:T(8,128)(2,1)}, u32[]{:S(2)}, u32[]{:S(2)}) %collective-permute-start.44) | collective-permute-done | bytes 720928 | tf_op jit(solution)/shard_map/ppermute | solution.py:541
  550.8 7.0 %collective-permute-done.46 = bf16[272,512]{1,0:T(8,128)(2,1)S(1)} collective-permute-done((bf16[272,512]{1,0:T(8,128)(2,1)S(1)}, bf16[272,512]{1,0:T(8,128)(2,1)S(1)}, u32[]{:S(2)}, u32[]{:S(2)}) %collective-permute-start.46) | collective-permute-done | bytes 278560 | tf_op jit(solution)/shard_map/ppermute | solution.py:541
  (525 shorter events, 299.6 us)
Async XLA Ops:
  7.2 65.7 %all-gather.3.cloned.1.call-start = ((), (), s32[]{:S(2)}) async-start(), calls=%async_computation.1 | async-start | bytes 4259840 | tf_op jit(solution)/shard_map/all_gather | solution.py:599
  16.5 153.8 %all-gather.5.cloned.1.call-start = ((), (), s32[]{:S(2)}) async-start(), calls=%async_computation.2 | async-start | bytes 7208960 | tf_op jit(solution)/shard_map/all_gather | solution.py:600
  19.0 331.1 %reduce-scatter.2.cloned.1.call-start = ((), (), s32[]{:S(2)}) async-start(), calls=%async_computation.3 | async-start | bytes 7208960 | tf_op jit(solution)/shard_map/reduce_scatter | solution.py:499
  77.0 57.3 %collective-permute-start.10 = (bf16[704,512]{1,0:T(8,128)(2,1)}, bf16[704,512]{1,0:T(8,128)(2,1)}, u32[]{:S(2)}, u32[]{:S(2)}) collective-permute-start(bf16[704,512]{1,0:T(8,128)(2,1)} %after.34), channel_id=1, source_target_pairs={{0,3},{1,2},{2,1},{3,0},{4,7},{5,6},{6,5},{7,4},{8,11},{9,10},{10,... | collective-permute-start | bytes 2162696 | tf_op jit(solution)/shard_map/ppermute | solution.py:514
  78.5 51.6 %collective-permute-start.9 = (bf16[704,512]{1,0:T(8,128)(2,1)}, bf16[704,512]{1,0:T(8,128)(2,1)}, u32[]{:S(2)}, u32[]{:S(2)}) collective-permute-start(bf16[704,512]{1,0:T(8,128)(2,1)} %after.34), channel_id=1, source_target_pairs={{0,2},{1,3},{2,0},{3,1},{4,6},{5,7},{6,4},{7,5},{8,10},{9,11},{10,... | collective-permute-start | bytes 2162696 | tf_op jit(solution)/shard_map/ppermute | solution.py:514
  80.0 48.2 %collective-permute-start.8 = (bf16[704,512]{1,0:T(8,128)(2,1)}, bf16[704,512]{1,0:T(8,128)(2,1)}, u32[]{:S(2)}, u32[]{:S(2)}) collective-permute-start(bf16[704,512]{1,0:T(8,128)(2,1)} %after.34), channel_id=1, source_target_pairs={{0,1},{1,0},{2,3},{3,2},{4,5},{5,4},{6,7},{7,6},{8,9},{9,8},{10,11... | collective-permute-start | bytes 2162696 | tf_op jit(solution)/shard_map/ppermute | solution.py:514
  100.2 39.0 %collective-permute-start.5 = (bf16[1,4,264,128]{3,2,1,0:T(8,128)(2,1)S(1)}, bf16[1,4,264,128]{3,2,1,0:T(8,128)(2,1)S(1)}, u32[]{:S(2)}, u32[]{:S(2)}) collective-permute-start(bf16[1,4,264,128]{3,2,1,0:T(8,128)(2,1)S(1)} %convert_element_type.391), channel_id=1, source_target_pairs={{0,1},{1,2},{2,3},{4,5},{5,6},{6,7},{8,9},{9,10},{10,11},{12,13},{... | collective-permute-start | bytes 811016 | tf_op jit(solution)/shard_map/ppermute | solution.py:426
  267.1 51.8 %collective-permute-start.22 = (bf16[2816,512]{1,0:T(8,128)(2,1)}, bf16[2816,512]{1,0:T(8,128)(2,1)}, u32[]{:S(2)}, u32[]{:S(2)}) collective-permute-start(bf16[2816,512]{1,0:T(8,128)(2,1)} %convolution_convert_fusion.1), channel_id=1, source_target_pairs={{0,4},{4,0},{1,5},{5,1},{2,6},{6,2},{3,7},{7,3},{8,12},{12,8},{9,1... | collective-permute-start | bytes 8650760 | tf_op jit(solution)/shard_map/ppermute | solution.py:455
  296.4 28.8 %collective-permute-start.17 = (bf16[1024,1536]{1,0:T(8,128)(2,1)}, bf16[1024,1536]{1,0:T(8,128)(2,1)}, u32[]{:S(2)}, u32[]{:S(2)}) collective-permute-start(bf16[1024,1536]{1,0:T(8,128)(2,1)} %convolution_convert_fusion.2), channel_id=1, source_target_pairs={{0,4},{4,0},{1,5},{5,1},{2,6},{6,2},{3,7},{7,3},{8,12},{12,8},{9,1... | collective-permute-start | bytes 9437192 | tf_op jit(solution)/shard_map/ppermute | solution.py:455
  344.5 36.1 %collective-permute-start.26 = (bf16[256,1536]{1,0:T(8,128)(2,1)}, bf16[256,1536]{1,0:T(8,128)(2,1)}, u32[]{:S(2)}, u32[]{:S(2)}) collective-permute-start(bf16[256,1536]{1,0:T(8,128)(2,1)} %get-tuple-element.83), channel_id=1, source_target_pairs={{0,3},{1,2},{2,1},{3,0},{4,7},{5,6},{6,5},{7,4},{8,11},{9,10},{10,... | collective-permute-start | bytes 2359304 | tf_op jit(solution)/shard_map/ppermute | solution.py:527
  346.0 35.9 %collective-permute-start.25 = (bf16[256,1536]{1,0:T(8,128)(2,1)}, bf16[256,1536]{1,0:T(8,128)(2,1)S(1)}, u32[]{:S(2)}, u32[]{:S(2)}) collective-permute-start(bf16[256,1536]{1,0:T(8,128)(2,1)} %get-tuple-element.84), channel_id=1, source_target_pairs={{0,2},{1,3},{2,0},{3,1},{4,6},{5,7},{6,4},{7,5},{8,10},{9,11},{10,... | collective-permute-start | bytes 2359304 | tf_op jit(solution)/shard_map/ppermute | solution.py:527
  352.8 30.5 %collective-permute-start.35 = (bf16[128,2816]{1,0:T(8,128)(2,1)}, bf16[128,2816]{1,0:T(8,128)(2,1)}, u32[]{:S(2)}, u32[]{:S(2)}) collective-permute-start(bf16[128,2816]{1,0:T(8,128)(2,1)} %get-tuple-element.96), channel_id=1, source_target_pairs={{0,8},{24,16},{1,9},{25,17},{2,10},{26,18},{3,11},{27,19},{4,12},{... | collective-permute-start | bytes 2162696 | tf_op jit(solution)/shard_map/ppermute | solution.py:541
  357.1 29.8 %collective-permute-start.29 = (bf16[128,2816]{1,0:T(8,128)(2,1)}, bf16[128,2816]{1,0:T(8,128)(2,1)}, u32[]{:S(2)}, u32[]{:S(2)}) collective-permute-start(bf16[128,2816]{1,0:T(8,128)(2,1)} %get-tuple-element.97), channel_id=1, source_target_pairs={{0,8},{24,16},{1,9},{25,17},{2,10},{26,18},{3,11},{27,19},{4,12},{... | collective-permute-start | bytes 2162696 | tf_op jit(solution)/shard_map/ppermute | solution.py:541
  363.9 51.2 %collective-permute-start.18 = (bf16[1024,512]{1,0:T(8,128)(2,1)}, bf16[1024,512]{1,0:T(8,128)(2,1)}, u32[]{:S(2)}, u32[]{:S(2)}) collective-permute-start(bf16[1024,512]{1,0:T(8,128)(2,1)} %convolution_convert_fusion.3), channel_id=1, source_target_pairs={{0,4},{4,0},{1,5},{5,1},{2,6},{6,2},{3,7},{7,3},{8,12},{12,8},{9,1... | collective-permute-start | bytes 3145736 | tf_op jit(solution)/shard_map/ppermute | solution.py:455
  380.6 34.5 %collective-permute-start.23 = (bf16[704,512]{1,0:T(8,128)(2,1)}, bf16[704,512]{1,0:T(8,128)(2,1)}, u32[]{:S(2)}, u32[]{:S(2)}) collective-permute-start(bf16[704,512]{1,0:T(8,128)(2,1)} %get-tuple-element.85), channel_id=1, source_target_pairs={{0,1},{1,0},{2,3},{3,2},{4,5},{5,4},{6,7},{7,6},{8,9},{9,8},{10,11... | collective-permute-start | bytes 2162696 | tf_op jit(solution)/shard_map/ppermute | solution.py:527
  381.9 31.7 %collective-permute-start.28 = (bf16[704,512]{1,0:T(8,128)(2,1)}, bf16[704,512]{1,0:T(8,128)(2,1)}, u32[]{:S(2)}, u32[]{:S(2)}) collective-permute-start(bf16[704,512]{1,0:T(8,128)(2,1)} %get-tuple-element.86), channel_id=1, source_target_pairs={{0,3},{1,2},{2,1},{3,0},{4,7},{5,6},{6,5},{7,4},{8,11},{9,10},{10,... | collective-permute-start | bytes 2162696 | tf_op jit(solution)/shard_map/ppermute | solution.py:527
  383.4 31.8 %collective-permute-start.27 = (bf16[704,512]{1,0:T(8,128)(2,1)}, bf16[704,512]{1,0:T(8,128)(2,1)}, u32[]{:S(2)}, u32[]{:S(2)}) collective-permute-start(bf16[704,512]{1,0:T(8,128)(2,1)} %get-tuple-element.87), channel_id=1, source_target_pairs={{0,2},{1,3},{2,0},{3,1},{4,6},{5,7},{6,4},{7,5},{8,10},{9,11},{10,... | collective-permute-start | bytes 2162696 | tf_op jit(solution)/shard_map/ppermute | solution.py:527
  388.5 34.8 %collective-permute-start.30 = (bf16[128,2816]{1,0:T(8,128)(2,1)S(1)}, bf16[128,2816]{1,0:T(8,128)(2,1)}, u32[]{:S(2)}, u32[]{:S(2)}) collective-permute-start(bf16[128,2816]{1,0:T(8,128)(2,1)S(1)} %get-tuple-element.95), channel_id=1, source_target_pairs={{8,16},{16,8},{9,17},{17,9},{10,18},{18,10},{11,19},{19,11},{12,20... | collective-permute-start | bytes 2162696 | tf_op jit(solution)/shard_map/ppermute | solution.py:541
  420.5 27.8 %collective-permute-start.21 = (bf16[272,512]{1,0:T(8,128)(2,1)}, bf16[272,512]{1,0:T(8,128)(2,1)S(1)}, u32[]{:S(2)}, u32[]{:S(2)}) collective-permute-start(bf16[272,512]{1,0:T(8,128)(2,1)} %get-tuple-element.99), channel_id=1, source_target_pairs={{0,3},{1,2},{2,1},{3,0},{4,7},{5,6},{6,5},{7,4},{8,11},{9,10},{10,... | collective-permute-start | bytes 835592 | tf_op jit(solution)/shard_map/ppermute | solution.py:527
  422.0 27.1 %collective-permute-start.20 = (bf16[272,512]{1,0:T(8,128)(2,1)S(1)}, bf16[272,512]{1,0:T(8,128)(2,1)S(1)}, u32[]{:S(2)}, u32[]{:S(2)}) collective-permute-start(bf16[272,512]{1,0:T(8,128)(2,1)S(1)} %get-tuple-element.100), channel_id=1, source_target_pairs={{0,2},{1,3},{2,0},{3,1},{4,6},{5,7},{6,4},{7,5},{8,10},{9,11},{10,... | collective-permute-start | bytes 835592 | tf_op jit(solution)/shard_map/ppermute | solution.py:527
  450.2 25.1 %collective-permute-start.38 = (bf16[128,2816]{1,0:T(8,128)(2,1)S(1)}, bf16[128,2816]{1,0:T(8,128)(2,1)S(1)}, u32[]{:S(2)}, u32[]{:S(2)}) collective-permute-start(bf16[128,2816]{1,0:T(8,128)(2,1)S(1)} %copy-done.54), channel_id=1, source_target_pairs={{8,0},{16,24},{9,1},{17,25},{10,2},{18,26},{11,3},{19,27},{12,4},{... | collective-permute-start | bytes 2162696 | tf_op jit(solution)/shard_map/ppermute | solution.py:541
  476.6 51.4 %collective-permute-start.49 = (bf16[256,2816]{1,0:T(8,128)(2,1)}, bf16[256,2816]{1,0:T(8,128)(2,1)}, u32[]{:S(2)}, u32[]{:S(2)}) collective-permute-start(bf16[256,2816]{1,0:T(8,128)(2,1)} %pad_maximum_fusion.9.other_ref), channel_id=1, source_target_pairs={{0,4},{4,0},{1,5},{5,1},{2,6},{6,2},{3,7},{7,3},{8,12},{12,8},{9,1... | collective-permute-start | bytes 4325384 | tf_op jit(solution)/shard_map/ppermute | solution.py:455
  506.4 39.2 %collective-permute-start.48 = (bf16[256,1536]{1,0:T(8,128)(2,1)}, bf16[256,1536]{1,0:T(8,128)(2,1)}, u32[]{:S(2)}, u32[]{:S(2)}) collective-permute-start(bf16[256,1536]{1,0:T(8,128)(2,1)} %pad_maximum_fusion.13.other_ref), channel_id=1, source_target_pairs={{0,4},{4,0},{1,5},{5,1},{2,6},{6,2},{3,7},{7,3},{8,12},{12,8},{9,1... | collective-permute-start | bytes 2359304 | tf_op jit(solution)/shard_map/ppermute | solution.py:455
  507.4 32.5 %collective-permute-start.44 = (bf16[704,512]{1,0:T(8,128)(2,1)S(1)}, bf16[704,512]{1,0:T(8,128)(2,1)}, u32[]{:S(2)}, u32[]{:S(2)}) collective-permute-start(bf16[704,512]{1,0:T(8,128)(2,1)S(1)} %add_convert_fusion.5.other_ref), channel_id=1, source_target_pairs={{8,0},{16,24},{9,1},{17,25},{10,2},{18,26},{11,3},{19,27},{12,4},{... | collective-permute-start | bytes 2162696 | tf_op jit(solution)/shard_map/ppermute | solution.py:541
  (151 other events, 1612.8 us)
Sparse Core Ops, SparseCore 0:
  16.6 56.2 all-gather.2
  75.3 94.9 all-gather.4
  222.0 84.5 reduce-scatter.1

commit v6 on v5

--- a/solution.py
+++ b/solution.py
@@ -529,35 +529,6 @@
     return low(total)
 
 
-def line_sum(array, parts, earlier=None):
-    count, me = lax.axis_size("z"), lax.axis_index("z")
-    if count % 2:
-        return (lax.psum(array, "z"),) * 2
-    middle = count // 2
-    rows = array.shape[0] // parts
-    totals = [array[i * rows : (i + 1) * rows] for i in range(parts)]
-
-    def send(pairs):
-        return [lax.ppermute(total, "z", pairs) for total in totals]
-
-    def add(came):
-        return [
-            low(total.astype(jnp.float32) + other.astype(jnp.float32)) for total, other in zip(totals, came)
-        ]
-
-    for step in range(middle - 1):
-        totals = add(send([(step, step + 1), (count - 1 - step, count - 2 - step)]))
-    if earlier is not None:
-        totals[0] = after(totals[0], earlier)
-    totals = add(send([(middle - 1, middle), (middle, middle - 1)]))
-    at_middle = totals[-1]
-    for step in reversed(range(middle - 1)):
-        came = send([(step + 1, step), (count - 2 - step, count - 1 - step)])
-        end = (me == step) | (me == count - 1 - step)
-        totals = [jnp.where(end, other, total) for total, other in zip(totals, came)]
-    return jnp.concatenate(totals, 0), at_middle
-
-
 def local(
     tokens,
     mixer_gain,
@@ -653,7 +624,7 @@
 
     both_mine, both_theirs = product(normed_two, ffn_mine), product(normed_two, ffn_theirs)
     hidden = joined(swiglu(both_mine), swiglu(both_theirs), 1)
-    down_theirs = swapped(after(down_mine, mixed))
+    down_theirs = swapped(down_mine)
     result = resid + joined(product(hidden, down_mine), product(hidden, down_theirs), 1)
     block_out = result.astype(jnp.bfloat16).reshape(tokens.shape)
 
@@ -704,7 +675,7 @@
     packed_came = swapped(low(product_left(normed_one, packed_theirs)))
     mixer_pair = low(product_left(normed_one, packed_mine) + packed_came.astype(jnp.float32))
     mixer_share = gathered_sum(mixer_pair, mixer_pair)
-    down_share = gathered_sum(after(down_pair, mixer_pair), mixer_share)
+    down_share = gathered_sum(after(down_pair, later_grad), mixer_pair)
     output_came = swapped(low(product_left(mixed, after(branch_theirs, mixer_pair))))
     output_pair = product_left(mixed, after(branch_mine, mixer_pair)) + output_came.astype(jnp.float32)
     gate_pulled = jax.vjp(gate_fn, low_rank, decay_up_f, decay_bias_f)[1](gates_grad)
@@ -746,14 +717,14 @@
     ).reshape(-1, width // 2)
     rest_share = gathered_sum(rest_pair, mixer_pair)
 
-    ffn_total, ffn_middle = line_sum(after(ffn_share, mixer_pair), 2)
+    ffn_total = lax.psum(ffn_share, "z")
     ffn_other = swapped(ffn_total)
-    mixer_total, mixer_middle = line_sum(after(mixer_share, ffn_middle), 2, ffn_total)
-    mixer_other = swapped(mixer_total)
-    down_total, down_middle = line_sum(after(down_share, mixer_middle), 1, mixer_total)
-    down_other = swapped(down_total)
-    rest_total, _ = line_sum(after(rest_share, down_middle), 1, down_total)
-    rest_other = swapped(rest_total)
+    mixer_total, down_total, rest_total = lax.psum(
+        tuple(after(share, ffn_total) for share in (mixer_share, down_share, rest_share)), "z"
+    )
+    mixer_other, down_other, rest_other = (
+        swapped(total) for total in (mixer_total, down_total, rest_total)
+    )
 
     def both_cores(total, other, begin, end):
         return joined(total[:, begin:end], other[:, begin:end], 1).astype(jnp.float32)

time: 583 us -> 547 us (0.938)
  starting transfers between devices: 91.1 us -> 41 us
  waiting for transfers between devices: 192 us -> 228 us
  other arithmetic: 65.2 us -> 48.6 us
    psum x0 -> x2, waiting for transfers between devices: none -> 75.5 us  [the longest x1 66.3 us: local(): lax.psum(tuple((after(share, ffn_total) for share in (mixer_share, down_s...]
    ppermute x18 -> x0, starting transfers between devices: 60.3 us -> none  [send(): return [lax.ppermute(total, 'z', pairs) for total in totals]]
    ppermute x18 -> x0, waiting for transfers between devices: 53 us -> none  [send(): return [lax.ppermute(total, 'z', pairs) for total in totals]]
    ppermute x12, waiting for transfers between devices: 2.43 us -> 20.9 us  [swapped(): return lax.ppermute(array, 'core', [(0, 1), (1, 0)])]
    convert_element_type x15 -> x5, other arithmetic: 21.7 us -> 12.5 us  [low(): return array.astype(jnp.bfloat16)]
    ppermute x9, starting transfers between devices: 9.8 us -> 19 us  [gathered_sum(): came = lax.ppermute(piece, 'seq', [(i, i ^ distance) for i in range(count)])]
    unnamed x254 -> x193, local copies, waits for them, and re-layouts: 34.5 us -> 34.4 us
  transfers between devices with their start and end apart: 54 -> 38, of which waited for: 24 -> 17; matrix products, arithmetic and copies ran while one was open for 33% -> 31% of each run, Pallas kernels for 4% -> 4%
where the time goes in v6:
time: 547 us; the launch traced here: 537 us
  waiting for transfers between devices  228 us (42%)
  matrix products  110 us (20%)
  local copies, waits for them, and re-layouts  69.9 us (13%)
  other arithmetic  48.6 us (9%)
  starting transfers between devices  41 us (7%)
  Pallas kernels  23.9 us (4%)
  between operations  15.4 us (3%)
    psum x1, waiting for transfers between devices, local(): lax.psum(tuple((after(share, ffn_total) for share in (mixer_share, down_s...  66.3 us
    ppermute x6, waiting for transfers between devices, spread(): came = lax.ppermute(array, 'seq', [(i, i ^ distance) for i in range(count)])  41.6 us
    dot_general x9, matrix products, product_left(): lax.dot_general(left, right, (((0,), (0,)), ((), ())), preferred_element_...  41.4 us
    dot_general x9, matrix products, product_right(): lax.dot_general(left, right, (((1,), (1,)), ((), ())), preferred_element_...  37.8 us
    ppermute x9, waiting for transfers between devices, gathered_sum(): came = lax.ppermute(piece, 'seq', [(i, i ^ distance) for i in range(count)])  35.7 us
    unnamed x193, local copies, waits for them, and re-layouts  34.4 us
    all_gather x1, waiting for transfers between devices, local(): mixer_mine = lax.all_gather(mixer_packed, 'seq', tiled=True)  27.8 us
    dot_general x9, matrix products, product(): return jnp.dot(left, right, preferred_element_type=jnp.float32)  25.5 us
  transfers between devices with their start and end apart: 38, of which 17 were waited for; matrix products, arithmetic and copies ran while one was open for 31% of the time, Pallas kernels for 4%

profile of v6, /device:TPU:0, one launch (start us, length us, event | category | flops | bytes accessed | tf_op | source)
XLA Modules:
  0.0 537.2 jit_solution(6737252710590199540)
XLA Ops:
  25.3 8.1 %collective-permute-done = bf16[256,512]{1,0:T(8,128)(2,1)S(1)} collective-permute-done((bf16[256,512]{1,0:T(8,128)(2,1)S(1)}, bf16[256,512]{1,0:T(8,128)(2,1)S(1)}, u32[]{:S(2)}, u32[]{:S(2)}) %collective-permute-start) | collective-permute-done | bytes 262176 | tf_op jit(solution)/shard_map/ppermute | solution.py:514
  45.0 27.8 %all-gather.3.cloned.1.call-done.array_ref = bf16[1024,1664]{1,0:T(8,128)(2,1)} async-done(((bf16[256,1664]{1,0:T(8,128)(2,1)}), bf16[1024,1664]{1,0:T(8,128)(2,1)}) %all-gather.3.cloned.1.call-update) | async-done | bytes 3407888 | tf_op jit(solution)/shard_map/all_gather | solution.py:570
  94.1 5.7 %scan_forward.1 = (f32[512,1024]{1,0:T(8,128)S(1)}, bf16[512,512]{1,0:T(8,128)(2,1)S(1)}, bf16[4,4,128,128]{3,2,1,0:T(8,128)(2,1)S(1)}, f32[4,4,256,128]{3,2,1,0...) custom-call(f32[512,1536]{1,0:T(8,128)S(1)} %fusion.11.q0.k0.v0.og0, ...), custom_call_target="tpu_custom_call" | custom-call | tf_op jit(solution)/shard_map/scan_forward/pallas_call | solution.py:317
  104.1 24.1 %collective-permute-done.8 = bf16[704,512]{1,0:T(8,128)(2,1)} collective-permute-done((bf16[704,512]{1,0:T(8,128)(2,1)}, bf16[704,512]{1,0:T(8,128)(2,1)}, u32[]{:S(2)}, u32[]{:S(2)}) %collective-permute-start.8) | collective-permute-done | bytes 720928 | tf_op jit(solution)/shard_map/ppermute | solution.py:514
  139.4 6.9 %collective-permute-done.6 = bf16[1,4,264,128]{3,2,1,0:T(8,128)(2,1)S(1)} collective-permute-done((bf16[1,4,264,128]{3,2,1,0:T(8,128)(2,1)S(1)}, bf16[1,4,264,128]{3,2,1,0:T(8,128)(2,1)S(1)}, u32[]{:S(2)}, u32[]{:S(2)}) %collective-permute-start.6) | collective-permute-done | bytes 270368 | tf_op jit(solution)/shard_map/ppermute | solution.py:426
  172.1 11.9 %collective-permute-done.12 = bf16[2816,512]{1,0:T(8,128)(2,1)S(1)} collective-permute-done((bf16[2816,512]{1,0:T(8,128)(2,1)}, bf16[2816,512]{1,0:T(8,128)(2,1)S(1)}, u32[]{:S(2)}, u32[]{:S(2)}) %collective-permute-start.12) | collective-permute-done | bytes 2883616 | tf_op jit(solution)/shard_map/ppermute | solution.py:455
  203.4 5.2 convolution_convert_fusion
  209.5 8.9 %collective-permute-done.13 = bf16[1024,2816]{1,0:T(8,128)(2,1)} collective-permute-done((bf16[1024,2816]{1,0:T(8,128)(2,1)}, bf16[1024,2816]{1,0:T(8,128)(2,1)}, u32[]{:S(2)}, u32[]{:S(2)}) %collective-permute-start.13) | collective-permute-done | bytes 5767200 | tf_op jit(solution)/shard_map/ppermute | solution.py:455
  218.4 9.5 %add_convert_fusion.other_ref = bf16[1024,2816]{1,0:T(8,128)(2,1)} fusion(bf16[1024,2816]{1,0:T(8,128)(2,1)} %collective-permute-done.13, bf16[512,1024]{1,0:T(8,128)(2,1)} %multiply_convert_fusion.6.other_ref, bf16[512,1408]{1,0:T(8,128)(2,1)} %get-tuple-element.81, bf16[512,1408]{1,0:T(8,128)(2,1)} %get-tuple-element.82), kind=kOutput, calls=%fused_computation | convolution fusion | flops 2967207936 | bytes 15466496 | tf_op jit(solution)/shard_map/dot_general | solution.py:440
  228.0 6.2 %fusion.28 = f32[512,1024]{1,0:T(8,128)S(1)} fusion(bf16[1024,2816]{1,0:T(8,128)(2,1)} %after.31, bf16[512,1408]{1,0:T(8,128)(2,1)} %get-tuple-element.81, bf16[512,1408]{1,0:T(8,128)(2,1)} %get-tuple-element.82), kind=kOutput, calls=%fused_computation.68 | convolution fusion | flops 2958557184 | bytes 10747904 | tf_op jit(solution)/shard_map/dot_general | solution.py:446
  234.2 7.6 %multiply_reduce_fusion = (bf16[1024]{0:T(1024)(128)(2,1)S(1)}, f32[512]{0:T(512)S(1)}, f32[512,1024]{1,0:T(8,128)}) fusion(f32[512,1024]{1,0:T(8,128)} %get-tuple-element.74, f32[512]{0:T(512)S(1)} %fusion.56, f32[1024]{0:T(1024)S(1)} %bitcast.139, f32[512,1024]{1,0:T(8,128)S(1)} %fusion.28, bf16[1024,2816]{1,0:T(8,128)(2,1)} %copy-done.88, ...), kind=kOutput, calls=%fused_computation.60 | convolution fusion | flops 2962225664 | bytes 14952448 | tf_op jit(solution)/shard_map/dot_general | solution.py:446
  276.1 6.3 %convolution_convert_fusion.1 = bf16[2816,512]{1,0:T(8,128)(2,1)} fusion(bf16[512,512]{1,0:T(8,128)(2,1)} %after.46, bf16[512,1408]{1,0:T(8,128)(2,1)} %get-tuple-element.84, bf16[512,1408]{1,0:T(8,128)(2,1)} %get-tuple-element.83, pred[]{:T(512)S(6)} %eq.10), kind=kOutput, calls=%fused_computation.5 | convolution fusion | flops 1490812928 | bytes 6291457 | tf_op jit(solution)/shard_map/dot_general | solution.py:440
  282.7 13.3 %collective-permute-done.14 = bf16[1,4,264,128]{3,2,1,0:T(8,128)(2,1)S(1)} collective-permute-done((bf16[1,4,264,128]{3,2,1,0:T(8,128)(2,1)S(1)}, bf16[1,4,264,128]{3,2,1,0:T(8,128)(2,1)S(1)}, u32[]{:S(2)}, u32[]{:S(2)}) %collective-permute-start.14) | collective-permute-done | bytes 270368 | tf_op jit(solution)/shard_map/ppermute | solution.py:426
  298.0 12.4 %scan_backward.1 = (bf16[512,1536]{1,0:T(8,128)(2,1)S(1)}, bf16[512,1536]{1,0:T(8,128)(2,1)S(1)}, f32[512,512]{1,0:T(8,128)S(1)}) custom-call(f32[512,1536]{1,0:T(8,128)} %copy-done.2, f32[512,1536]{1,0:T(8,128)} %copy-done.2, f32[512,1536]{1,0:T(8,128)} %copy-done.2, f32[512,1536]{1,0:T(8,128)} %copy-done.3, f32[512,1536]{1,0:T(8,128)} %copy-done.3, ...), custom_call_target="tpu_custom_call" | custom-call | tf_op jit(solution)/shard_map/scan_backward/pallas_call | solution.py:353
  327.4 7.0 %add_convert_fusion.2.array_ref = bf16[2816,512]{1,0:T(8,128)(2,1)} fusion(bf16[2816,512]{1,0:T(8,128)(2,1)} %collective-permute-done.28, bf16[512,512]{1,0:T(8,128)(2,1)S(1)} %copy-done.47, bf16[512,1408]{1,0:T(8,128)(2,1)} %get-tuple-element.84, bf16[512,1408]{1,0:T(8,128)(2,1)} %get-tuple-element.83, pred[]{:T(512)S(6)} %eq.10), kind=kOutput, calls=%fused_computation.2 | convolution fusion | flops 1493696512 | bytes 9175041 | tf_op jit(solution)/shard_map/dot_general | solution.py:440
  337.5 8.0 %collective-permute-start.29 = (bf16[704,512]{1,0:T(8,128)(2,1)}, bf16[704,512]{1,0:T(8,128)(2,1)}, u32[]{:S(2)}, u32[]{:S(2)}) collective-permute-start(bf16[704,512]{1,0:T(8,128)(2,1)} %get-tuple-element.88), channel_id=1, source_target_pairs={{0,1},{1,0},{2,3},{3,2},{4,5},{5,4},{6,7},{7,6},{8,9},{9,8},{10,11... | collective-permute-start | bytes 2162696 | tf_op jit(solution)/shard_map/ppermute | solution.py:527
  349.5 5.6 %add_convert_fusion.1.other_ref = bf16[1024,1536]{1,0:T(8,128)(2,1)} fusion(bf16[1024,1536]{1,0:T(8,128)(2,1)} %collective-permute-done.17, bf16[512,1536]{1,0:T(8,128)(2,1)S(1)} %copy-done.23, bf16[1,512,1024]{2,1,0:T(8,128)(2,1)S(1)} %copy-done.42, f32[1024]{0:T(1024)S(1)} %bitcast.151, f32[512]{0:T(512)S(1)} %fusion.55), kind=kOutput, calls=%fused_computation.1 | convolution fusion | flops 1617428480 | bytes 8919040 | tf_op jit(solution)/shard_map/dot_general | solution.py:440
  360.7 5.2 fusion.5
  369.0 13.3 %collective-permute-done.31.array_ref = bf16[704,512]{1,0:T(8,128)(2,1)} collective-permute-done((bf16[704,512]{1,0:T(8,128)(2,1)}, bf16[704,512]{1,0:T(8,128)(2,1)}, u32[]{:S(2)}, u32[]{:S(2)}) %collective-permute-start.31) | collective-permute-done | bytes 720928 | tf_op jit(solution)/shard_map/ppermute | solution.py:527
  382.3 6.7 %fusion.16 = (bf16[1024]{0:T(1024)(128)(2,1)S(1)}, f32[512]{0:T(512)S(1)}, f32[512,1024]{1,0:T(8,128)}) fusion(bf16[1,512,1024]{2,1,0:T(8,128)(2,1)S(1)} %copy-done.42, f32[512]{0:T(512)S(1)} %fusion.55, f32[1024]{0:T(1024)S(1)} %bitcast.152, f32[512,1024]{1,0:T(8,128)} %fusion.89, f32[512,1024]{1,0:T(8,128)} %fusion.5, ...), kind=kOutput, calls=%fused_computation.46 | convolution fusion | flops 1615329792 | bytes 12068864 | tf_op jit(solution)/shard_map/dot_general | solution.py:446
  395.9 18.7 %collective-permute-done.25.array_ref = bf16[256,1536]{1,0:T(8,128)(2,1)} collective-permute-done((bf16[256,1536]{1,0:T(8,128)(2,1)}, bf16[256,1536]{1,0:T(8,128)(2,1)}, u32[]{:S(2)}, u32[]{:S(2)}) %collective-permute-start.25) | collective-permute-done | bytes 786464 | tf_op jit(solution)/shard_map/ppermute | solution.py:527
  422.5 9.2 %all-reduce.6.cloned.1.call-done.other_ref = bf16[256,2816]{1,0:T(8,128)(2,1)} async-done(((bf16[256,2816]{1,0:T(8,128)(2,1)}), bf16[256,2816]{1,0:T(8,128)(2,1)}) %all-reduce.6.cloned.1.call-update) | async-done | bytes 1441808 | tf_op jit(solution)/shard_map/psum | solution.py:720
  438.6 5.3 fusion.25
  448.3 66.3 %all-reduce.8.cloned.1.call-done = (bf16[272,512]{1,0:T(8,128)(2,1)}, bf16[256,1536]{1,0:T(8,128)(2,1)}, bf16[704,512]{1,0:T(8,128)(2,1)}) async-done(((bf16[272,512]{1,0:T(8,128)(2,1)}, bf16[256,1536]{1,0:T(8,128)(2,1)}, bf16[704,512]{1,0:T(8,128)(2,1)}), (bf16[272,512]{1,0:T(8,128)(2,1)}, bf16[256,1536]{1,0:T(8,128)(2,1)}, bf16[704,512]{1,0:T(8,128)(2,1)})) %all-reduce.8.cloned.1.call-update) | async-done | bytes 1785872 | tf_op jit(solution)/shard_map/psum | solution.py:722
  (409 shorter events, 222.6 us)
Async XLA Ops:
  7.2 65.7 %all-gather.3.cloned.1.call-start = ((), (), s32[]{:S(2)}) async-start(), calls=%async_computation.1 | async-start | bytes 4259840 | tf_op jit(solution)/shard_map/all_gather | solution.py:570
  16.5 153.8 %all-gather.5.cloned.1.call-start = ((), (), s32[]{:S(2)}) async-start(), calls=%async_computation.2 | async-start | bytes 7208960 | tf_op jit(solution)/shard_map/all_gather | solution.py:571
  19.0 346.9 %reduce-scatter.2.cloned.1.call-start = ((), (), s32[]{:S(2)}) async-start(), calls=%async_computation.3 | async-start | bytes 7208960 | tf_op jit(solution)/shard_map/reduce_scatter | solution.py:499
  25.3 19.0 %collective-permute-start.2 = (bf16[256,512]{1,0:T(8,128)(2,1)S(1)}, bf16[256,512]{1,0:T(8,128)(2,1)S(1)}, u32[]{:S(2)}, u32[]{:S(2)}) collective-permute-start(bf16[256,512]{1,0:T(8,128)(2,1)S(1)} %get-tuple-element.76), channel_id=1, source_target_pairs={{0,3},{1,2},{2,1},{3,0},{4,7},{5,6},{6,5},{7,4},{8,11},{9,10},{10,... | collective-permute-start | bytes 786440 | tf_op jit(solution)/shard_map/ppermute | solution.py:514
  72.9 17.0 %collective-permute-start.3 = (bf16[1024,1664]{1,0:T(8,128)(2,1)}, bf16[1024,1664]{1,0:T(8,128)(2,1)}, u32[]{:S(2)}, u32[]{:S(2)}) collective-permute-start(bf16[1024,1664]{1,0:T(8,128)(2,1)} %after.27.other_ref), channel_id=1, source_target_pairs={{0,4},{4,0},{1,5},{5,1},{2,6},{6,2},{3,7},{7,3},{8,12},{12,8},{9,1... | collective-permute-start | bytes 10223624 | tf_op jit(solution)/shard_map/ppermute | solution.py:455
  77.0 57.3 %collective-permute-start.10 = (bf16[704,512]{1,0:T(8,128)(2,1)}, bf16[704,512]{1,0:T(8,128)(2,1)}, u32[]{:S(2)}, u32[]{:S(2)}) collective-permute-start(bf16[704,512]{1,0:T(8,128)(2,1)} %after.29), channel_id=1, source_target_pairs={{0,3},{1,2},{2,1},{3,0},{4,7},{5,6},{6,5},{7,4},{8,11},{9,10},{10,... | collective-permute-start | bytes 2162696 | tf_op jit(solution)/shard_map/ppermute | solution.py:514
  78.5 51.6 %collective-permute-start.9 = (bf16[704,512]{1,0:T(8,128)(2,1)}, bf16[704,512]{1,0:T(8,128)(2,1)}, u32[]{:S(2)}, u32[]{:S(2)}) collective-permute-start(bf16[704,512]{1,0:T(8,128)(2,1)} %after.29), channel_id=1, source_target_pairs={{0,2},{1,3},{2,0},{3,1},{4,6},{5,7},{6,4},{7,5},{8,10},{9,11},{10,... | collective-permute-start | bytes 2162696 | tf_op jit(solution)/shard_map/ppermute | solution.py:514
  80.0 48.2 %collective-permute-start.8 = (bf16[704,512]{1,0:T(8,128)(2,1)}, bf16[704,512]{1,0:T(8,128)(2,1)}, u32[]{:S(2)}, u32[]{:S(2)}) collective-permute-start(bf16[704,512]{1,0:T(8,128)(2,1)} %after.29), channel_id=1, source_target_pairs={{0,1},{1,0},{2,3},{3,2},{4,5},{5,4},{6,7},{7,6},{8,9},{9,8},{10,11... | collective-permute-start | bytes 2162696 | tf_op jit(solution)/shard_map/ppermute | solution.py:514
  100.7 38.7 %collective-permute-start.5 = (bf16[1,4,264,128]{3,2,1,0:T(8,128)(2,1)S(1)}, bf16[1,4,264,128]{3,2,1,0:T(8,128)(2,1)S(1)}, u32[]{:S(2)}, u32[]{:S(2)}) collective-permute-start(bf16[1,4,264,128]{3,2,1,0:T(8,128)(2,1)S(1)} %convert_element_type.283), channel_id=1, source_target_pairs={{0,1},{1,2},{2,3},{4,5},{5,6},{6,7},{8,9},{9,10},{10,11},{12,13},{... | collective-permute-start | bytes 811016 | tf_op jit(solution)/shard_map/ppermute | solution.py:426
  170.2 22.9 %collective-permute-start.11 = (bf16[1024,2816]{1,0:T(8,128)(2,1)}, bf16[1024,2816]{1,0:T(8,128)(2,1)S(1)}, u32[]{:S(2)}, u32[]{:S(2)}) collective-permute-start(bf16[1024,2816]{1,0:T(8,128)(2,1)} %after.31), channel_id=1, source_target_pairs={{0,4},{4,0},{1,5},{5,1},{2,6},{6,2},{3,7},{7,3},{8,12},{12,8},{9,1... | collective-permute-start | bytes 17301512 | tf_op jit(solution)/shard_map/ppermute | solution.py:455
  227.9 203.8 %all-reduce.6.cloned.1.call-start = ((), (), s32[]{:S(2)}) async-start(), calls=%async_computation.4 | async-start | bytes 2883584 | tf_op jit(solution)/shard_map/psum | solution.py:720
  272.1 24.6 %collective-permute-start.16 = (bf16[1,4,264,128]{3,2,1,0:T(8,128)(2,1)S(1)}, bf16[1,4,264,128]{3,2,1,0:T(8,128)(2,1)}, u32[]{:S(2)}, u32[]{:S(2)}) collective-permute-start(bf16[1,4,264,128]{3,2,1,0:T(8,128)(2,1)S(1)} %pad_maximum_fusion.14), channel_id=1, source_target_pairs={{3,0},{7,4},{11,8},{15,12},{19,16},{23,20},{27,24},{31,28}} | collective-permute-start | bytes 811016 | tf_op jit(solution)/shard_map/ppermute | solution.py:426
  273.4 22.6 %collective-permute-start.15 = (bf16[1,4,264,128]{3,2,1,0:T(8,128)(2,1)S(1)}, bf16[1,4,264,128]{3,2,1,0:T(8,128)(2,1)}, u32[]{:S(2)}, u32[]{:S(2)}) collective-permute-start(bf16[1,4,264,128]{3,2,1,0:T(8,128)(2,1)S(1)} %pad_maximum_fusion.14), channel_id=1, source_target_pairs={{2,0},{3,1},{6,4},{7,5},{10,8},{11,9},{14,12},{15,13},{18,16},{19,... | collective-permute-start | bytes 811016 | tf_op jit(solution)/shard_map/ppermute | solution.py:426
  274.7 21.3 %collective-permute-start.14 = (bf16[1,4,264,128]{3,2,1,0:T(8,128)(2,1)S(1)}, bf16[1,4,264,128]{3,2,1,0:T(8,128)(2,1)S(1)}, u32[]{:S(2)}, u32[]{:S(2)}) collective-permute-start(bf16[1,4,264,128]{3,2,1,0:T(8,128)(2,1)S(1)} %pad_maximum_fusion.14), channel_id=1, source_target_pairs={{1,0},{2,1},{3,2},{5,4},{6,5},{7,6},{9,8},{10,9},{11,10},{13,12},{... | collective-permute-start | bytes 811016 | tf_op jit(solution)/shard_map/ppermute | solution.py:426
  282.5 45.0 %collective-permute-start.28 = (bf16[2816,512]{1,0:T(8,128)(2,1)}, bf16[2816,512]{1,0:T(8,128)(2,1)}, u32[]{:S(2)}, u32[]{:S(2)}) collective-permute-start(bf16[2816,512]{1,0:T(8,128)(2,1)} %convolution_convert_fusion.1), channel_id=1, source_target_pairs={{0,4},{4,0},{1,5},{5,1},{2,6},{6,2},{3,7},{7,3},{8,12},{12,8},{9,1... | collective-permute-start | bytes 8650760 | tf_op jit(solution)/shard_map/ppermute | solution.py:455
  314.1 35.3 %collective-permute-start.17 = (bf16[1024,1536]{1,0:T(8,128)(2,1)}, bf16[1024,1536]{1,0:T(8,128)(2,1)}, u32[]{:S(2)}, u32[]{:S(2)}) collective-permute-start(bf16[1024,1536]{1,0:T(8,128)(2,1)} %convolution_convert_fusion.2), channel_id=1, source_target_pairs={{0,4},{4,0},{1,5},{5,1},{2,6},{6,2},{3,7},{7,3},{8,12},{12,8},{9,1... | collective-permute-start | bytes 9437192 | tf_op jit(solution)/shard_map/ppermute | solution.py:455
  337.5 28.5 %collective-permute-start.29 = (bf16[704,512]{1,0:T(8,128)(2,1)}, bf16[704,512]{1,0:T(8,128)(2,1)}, u32[]{:S(2)}, u32[]{:S(2)}) collective-permute-start(bf16[704,512]{1,0:T(8,128)(2,1)} %get-tuple-element.88), channel_id=1, source_target_pairs={{0,1},{1,0},{2,3},{3,2},{4,5},{5,4},{6,7},{7,6},{8,9},{9,8},{10,11... | collective-permute-start | bytes 2162696 | tf_op jit(solution)/shard_map/ppermute | solution.py:527
  345.5 36.8 %collective-permute-start.31 = (bf16[704,512]{1,0:T(8,128)(2,1)}, bf16[704,512]{1,0:T(8,128)(2,1)}, u32[]{:S(2)}, u32[]{:S(2)}) collective-permute-start(bf16[704,512]{1,0:T(8,128)(2,1)} %get-tuple-element.89), channel_id=1, source_target_pairs={{0,3},{1,2},{2,1},{3,0},{4,7},{5,6},{6,5},{7,4},{8,11},{9,10},{10,... | collective-permute-start | bytes 2162696 | tf_op jit(solution)/shard_map/ppermute | solution.py:527
  349.4 40.2 %collective-permute-start.30 = (bf16[704,512]{1,0:T(8,128)(2,1)}, bf16[704,512]{1,0:T(8,128)(2,1)}, u32[]{:S(2)}, u32[]{:S(2)}) collective-permute-start(bf16[704,512]{1,0:T(8,128)(2,1)} %get-tuple-element.90), channel_id=1, source_target_pairs={{0,2},{1,3},{2,0},{3,1},{4,6},{5,7},{6,4},{7,5},{8,10},{9,11},{10,... | collective-permute-start | bytes 2162696 | tf_op jit(solution)/shard_map/ppermute | solution.py:527
  358.1 57.9 %collective-permute-start.18 = (bf16[1024,512]{1,0:T(8,128)(2,1)}, bf16[1024,512]{1,0:T(8,128)(2,1)}, u32[]{:S(2)}, u32[]{:S(2)}) collective-permute-start(bf16[1024,512]{1,0:T(8,128)(2,1)} %convolution_convert_fusion.3), channel_id=1, source_target_pairs={{0,4},{4,0},{1,5},{5,1},{2,6},{6,2},{3,7},{7,3},{8,12},{12,8},{9,1... | collective-permute-start | bytes 3145736 | tf_op jit(solution)/shard_map/ppermute | solution.py:455
  360.1 34.9 %collective-permute-start.23 = (bf16[256,1536]{1,0:T(8,128)(2,1)}, bf16[256,1536]{1,0:T(8,128)(2,1)S(1)}, u32[]{:S(2)}, u32[]{:S(2)}) collective-permute-start(bf16[256,1536]{1,0:T(8,128)(2,1)} %get-tuple-element.85), channel_id=1, source_target_pairs={{0,1},{1,0},{2,3},{3,2},{4,5},{5,4},{6,7},{7,6},{8,9},{9,8},{10,11... | collective-permute-start | bytes 2359304 | tf_op jit(solution)/shard_map/ppermute | solution.py:527
  365.9 148.6 %all-reduce.8.cloned.1.call-start = ((), (), s32[]{:S(2)}) async-start(), calls=%async_computation.5 | async-start | bytes 3571712 | tf_op jit(solution)/shard_map/psum | solution.py:722
  366.0 48.6 %collective-permute-start.25 = (bf16[256,1536]{1,0:T(8,128)(2,1)}, bf16[256,1536]{1,0:T(8,128)(2,1)}, u32[]{:S(2)}, u32[]{:S(2)}) collective-permute-start(bf16[256,1536]{1,0:T(8,128)(2,1)} %get-tuple-element.86), channel_id=1, source_target_pairs={{0,3},{1,2},{2,1},{3,0},{4,7},{5,6},{6,5},{7,4},{8,11},{9,10},{10,... | collective-permute-start | bytes 2359304 | tf_op jit(solution)/shard_map/ppermute | solution.py:527
  382.3 33.8 %collective-permute-start.24 = (bf16[256,1536]{1,0:T(8,128)(2,1)}, bf16[256,1536]{1,0:T(8,128)(2,1)}, u32[]{:S(2)}, u32[]{:S(2)}) collective-permute-start(bf16[256,1536]{1,0:T(8,128)(2,1)} %get-tuple-element.87), channel_id=1, source_target_pairs={{0,2},{1,3},{2,0},{3,1},{4,6},{5,7},{6,4},{7,5},{8,10},{9,11},{10,... | collective-permute-start | bytes 2359304 | tf_op jit(solution)/shard_map/ppermute | solution.py:527
  (105 other events, 956.5 us)
Sparse Core Ops, SparseCore 0:
  16.6 56.2 all-gather.2
  75.3 94.9 all-gather.4
  228.0 79.2 reduce-scatter.1
  366.1 65.6 all-reduce.5
  437.5 77.0 all-reduce.7

commit v7 on v6

--- a/solution.py
+++ b/solution.py
@@ -519,14 +519,16 @@
 def gathered_sum(array, late):
     count, me = lax.axis_size("seq"), lax.axis_index("seq")
     if not direct(count):
-        return scattered(array)
+        return scattered(array), late
     rows = array.shape[0] // count
+    pieces = []
     total = lax.dynamic_slice_in_dim(array, me * rows, rows, 0).astype(jnp.float32)
     for distance in range(1, count):
         piece = lax.dynamic_slice_in_dim(array, (me ^ distance) * rows, rows, 0)
         came = lax.ppermute(piece, "seq", [(i, i ^ distance) for i in range(count)])
-        total = total + after(came, late).astype(jnp.float32)
-    return low(total)
+        pieces.append(after(came, late))
+        total = total + pieces[-1].astype(jnp.float32)
+    return low(total), pieces[0]
 
 
 def local(
@@ -612,7 +614,8 @@
     attended, mixed = mix_forward(
         local_out, forget, incoming_state, mine, theirs, head_gain_f[None, :], seqs_here, chunk
     )
-    mixed = jnp.concatenate(halves_of(mixed), 1)
+    down_theirs = swapped(down_mine)
+    mixed = jnp.concatenate(halves_of(after(mixed, down_theirs)), 1)
     resid = inputs + joined(product(mixed, output_mine), product(mixed, output_theirs), 1)
     normed_two = first_norm(resid, gain_two).astype(jnp.bfloat16)
     ffn_mine = after(ffn_mine, normed_two)
@@ -624,7 +627,6 @@
 
     both_mine, both_theirs = product(normed_two, ffn_mine), product(normed_two, ffn_theirs)
     hidden = joined(swiglu(both_mine), swiglu(both_theirs), 1)
-    down_theirs = swapped(down_mine)
     result = resid + joined(product(hidden, down_mine), product(hidden, down_theirs), 1)
     block_out = result.astype(jnp.bfloat16).reshape(tokens.shape)
 
@@ -647,7 +649,10 @@
     grad_mine, grad_theirs = halves_of(hidden_grad)
     back_mine, back_theirs = swiglu_back(both_mine, grad_mine), swiglu_back(both_theirs, grad_theirs)
 
+    down_came = swapped(low(product_left(hidden, low_theirs)))
     ffn_came = swapped(low(product_left(normed_two, back_theirs)))
+    down_pair = low(product_left(hidden, low_mine) + down_came.astype(jnp.float32))
+    back_mine = after(back_mine, down_pair)
     normed_two_grad = product_right(back_mine, ffn_mine) + product_right(back_theirs, ffn_theirs)
     norm_pulled = jax.vjp(first_norm, resid, gain_two)[1](normed_two_grad)
     resid_grad = grad_out + norm_pulled[0]
@@ -666,26 +671,28 @@
     later_grad = from_neighbours(
         jnp.concatenate([state_grad, summary[:, :, DV:]], axis=2).astype(jnp.bfloat16), -1
     )
-    down_came = swapped(low(product_left(hidden, after(low_theirs, attended_grad))))
-    down_pair = low(product_left(hidden, after(low_mine, attended_grad)) + down_came.astype(jnp.float32))
+    output_came = swapped(low(product_left(mixed, after(branch_theirs, attended_grad))))
+    output_pair = product_left(mixed, after(branch_mine, attended_grad)) + output_came.astype(jnp.float32)
+    output_pair = low(output_pair)
+    down_share, _ = gathered_sum(down_pair, attended_grad)
+    attended_grad = after(after(attended_grad, output_pair), down_share)
     packed_mine, packed_theirs, gates_grad = scan_backward(
         mine, theirs, gates, scores, states, starts, incoming_state,
         attended_grad, later_grad, outgate_grads, seqs_here, chunk,
     )
+    packed_theirs = after(packed_theirs, ffn_share)
     packed_came = swapped(low(product_left(normed_one, packed_theirs)))
     mixer_pair = low(product_left(normed_one, packed_mine) + packed_came.astype(jnp.float32))
-    mixer_share = gathered_sum(mixer_pair, mixer_pair)
-    down_share = gathered_sum(after(down_pair, later_grad), mixer_pair)
-    output_came = swapped(low(product_left(mixed, after(branch_theirs, mixer_pair))))
-    output_pair = product_left(mixed, after(branch_mine, mixer_pair)) + output_came.astype(jnp.float32)
+    mixer_share, mixer_first = gathered_sum(mixer_pair, mixer_pair)
+    gates_grad = after(gates_grad, mixer_first)
     gate_pulled = jax.vjp(gate_fn, low_rank, decay_up_f, decay_bias_f)[1](gates_grad)
     low_rank_grad = gate_pulled[0].astype(jnp.bfloat16)
     decay_up_grad = jnp.concatenate(halves_of(gate_pulled[1]), 1)
     decay_bias_grad = jnp.concatenate(halves_of(gate_pulled[2]), 1)[0]
     decay_down_grad = product_left(normed_one, low_rank_grad)
     normed_one_grad = (
-        product_right(after(packed_mine, mixer_pair), projection_mine)
-        + product_right(after(packed_theirs, mixer_pair), projection_theirs)
+        product_right(after(packed_mine, mixer_first), projection_mine)
+        + product_right(after(packed_theirs, mixer_first), projection_theirs)
         + product_right(low_rank_grad, decay_down_all)
     )
     first_pulled = jax.vjp(first_norm, inputs, gain_one)[1](normed_one_grad)
@@ -710,14 +717,14 @@
     small_grads = jnp.pad(low(small_grads), ((0, 0), (0, small_rows * width // 2 - flat_size)))
     rest_pair = jnp.concatenate(
         [
-            low(output_pair).reshape(count, shard_rows, width // 2),
+            output_pair.reshape(count, shard_rows, width // 2),
             small_grads.reshape(count, small_rows, width // 2),
         ],
         axis=1,
     ).reshape(-1, width // 2)
-    rest_share = gathered_sum(rest_pair, mixer_pair)
-
-    ffn_total = lax.psum(ffn_share, "z")
+    rest_share, _ = gathered_sum(rest_pair, mixer_pair)
+
+    ffn_total = after(lax.psum(ffn_share, "z"), rest_share)
     ffn_other = swapped(ffn_total)
     mixer_total, down_total, rest_total = lax.psum(
         tuple(after(share, ffn_total) for share in (mixer_share, down_share, rest_share)), "z"

time: 547 us -> 574 us (1.049)
  waiting for transfers between devices: 228 us -> 254 us
  local copies, waits for them, and re-layouts: 69.9 us -> 84.3 us
  starting transfers between devices: 41 us -> 31.9 us
    ppermute x6, waiting for transfers between devices: 41.6 us -> 60.5 us  [spread(): came = lax.ppermute(array, 'seq', [(i, i ^ distance) for i in range(count)])]
    unnamed x193 -> x203, local copies, waits for them, and re-layouts: 34.4 us -> 53 us
    ppermute x9, waiting for transfers between devices: 35.7 us -> 48.9 us  [gathered_sum(): came = lax.ppermute(piece, 'seq', [(i, i ^ distance) for i in range(count)])]
    ppermute x9, starting transfers between devices: 19 us -> 10 us  [gathered_sum(): came = lax.ppermute(piece, 'seq', [(i, i ^ distance) for i in range(count)])]
    ppermute x12, waiting for transfers between devices: 20.9 us -> 13.8 us  [swapped(): return lax.ppermute(array, 'core', [(0, 1), (1, 0)])]
  transfers between devices with their start and end apart: 38 -> 38, of which waited for: 17 -> 17; matrix products, arithmetic and copies ran while one was open for 31% -> 25% of each run, Pallas kernels for 4% -> 4%
where the time goes in v7:
time: 574 us; the launch traced here: 563 us
  waiting for transfers between devices  254 us (44%)
  matrix products  108 us (19%)
  local copies, waits for them, and re-layouts  84.3 us (15%)
  other arithmetic  47.3 us (8%)
  starting transfers between devices  31.9 us (6%)
  Pallas kernels  23.4 us (4%)
  between operations  15.5 us (3%)
    psum x1, waiting for transfers between devices, local(): lax.psum(tuple((after(share, ffn_total) for share in (mixer_share, down_s...  66.7 us
    ppermute x6, waiting for transfers between devices, spread(): came = lax.ppermute(array, 'seq', [(i, i ^ distance) for i in range(count)])  60.5 us
    unnamed x203, local copies, waits for them, and re-layouts  53 us
    ppermute x9, waiting for transfers between devices, gathered_sum(): came = lax.ppermute(piece, 'seq', [(i, i ^ distance) for i in range(count)])  48.9 us
    dot_general x9, matrix products, product_left(): lax.dot_general(left, right, (((0,), (0,)), ((), ())), preferred_element_...  40.9 us
    dot_general x9, matrix products, product_right(): lax.dot_general(left, right, (((1,), (1,)), ((), ())), preferred_element_...  32.2 us
    dot_general x9, matrix products, product(): return jnp.dot(left, right, preferred_element_type=jnp.float32)  30.1 us
    all_gather x1, waiting for transfers between devices, local(): mixer_mine = lax.all_gather(mixer_packed, 'seq', tiled=True)  27.8 us
  transfers between devices with their start and end apart: 38, of which 17 were waited for; matrix products, arithmetic and copies ran while one was open for 25% of the time, Pallas kernels for 4%

profile of v7, /device:TPU:0, one launch (start us, length us, event | category | flops | bytes accessed | tf_op | source)
XLA Modules:
  0.0 563.5 jit_solution(18009789258484712512)
XLA Ops:
  25.3 8.1 %collective-permute-done = bf16[256,512]{1,0:T(8,128)(2,1)S(1)} collective-permute-done((bf16[256,512]{1,0:T(8,128)(2,1)S(1)}, bf16[256,512]{1,0:T(8,128)(2,1)S(1)}, u32[]{:S(2)}, u32[]{:S(2)}) %collective-permute-start) | collective-permute-done | bytes 262176 | tf_op jit(solution)/shard_map/ppermute | solution.py:514
  45.0 27.8 %all-gather.3.cloned.1.call-done.array_ref = bf16[1024,1664]{1,0:T(8,128)(2,1)} async-done(((bf16[256,1664]{1,0:T(8,128)(2,1)}), bf16[1024,1664]{1,0:T(8,128)(2,1)}) %all-gather.3.cloned.1.call-update) | async-done | bytes 3407888 | tf_op jit(solution)/shard_map/all_gather | solution.py:572
  84.8 43.0 %collective-permute-done.8 = bf16[704,512]{1,0:T(8,128)(2,1)} collective-permute-done((bf16[704,512]{1,0:T(8,128)(2,1)}, bf16[704,512]{1,0:T(8,128)(2,1)}, u32[]{:S(2)}, u32[]{:S(2)}) %collective-permute-start.8) | collective-permute-done | bytes 720928 | tf_op jit(solution)/shard_map/ppermute | solution.py:514
  137.9 5.2 fusion.7.q1.k1.v1.og1
  143.2 5.7 %scan_forward.1 = (f32[512,1024]{1,0:T(8,128)S(1)}, bf16[512,512]{1,0:T(8,128)(2,1)S(1)}, bf16[4,4,128,128]{3,2,1,0:T(8,128)(2,1)S(1)}, f32[4,4,256,128]{3,2,1,0...) custom-call(f32[512,1536]{1,0:T(8,128)S(1)} %fusion.11.q0.k0.v0.og0, ...), custom_call_target="tpu_custom_call" | custom-call | tf_op jit(solution)/shard_map/scan_forward/pallas_call | solution.py:317
  161.3 6.9 %collective-permute-done.5 = bf16[1,4,264,128]{3,2,1,0:T(8,128)(2,1)} collective-permute-done((bf16[1,4,264,128]{3,2,1,0:T(8,128)(2,1)S(1)}, bf16[1,4,264,128]{3,2,1,0:T(8,128)(2,1)}, u32[]{:S(2)}, u32[]{:S(2)}) %collective-permute-start.5) | collective-permute-done | bytes 270368 | tf_op jit(solution)/shard_map/ppermute | solution.py:426
  168.9 6.7 %collective-permute-done.6 = bf16[1,4,264,128]{3,2,1,0:T(8,128)(2,1)} collective-permute-done((bf16[1,4,264,128]{3,2,1,0:T(8,128)(2,1)S(1)}, bf16[1,4,264,128]{3,2,1,0:T(8,128)(2,1)}, u32[]{:S(2)}, u32[]{:S(2)}) %collective-permute-start.6) | collective-permute-done | bytes 270368 | tf_op jit(solution)/shard_map/ppermute | solution.py:426
  208.3 5.8 %fusion.83 = f32[512,2816]{1,0:T(8,128)S(1)} fusion(bf16[512,1024]{1,0:T(8,128)(2,1)S(1)} %copy-done.61, bf16[1024,2816]{1,0:T(8,128)(2,1)} %collective-permute-done.12), kind=kOutput, calls=%fused_computation.202 | convolution fusion | flops 2952790016 | bytes 12582912 | tf_op jit(solution)/shard_map/dot_general | solution.py:436
  218.6 7.8 %convolution_convert_fusion = bf16[1024,2816]{1,0:T(8,128)(2,1)} fusion(bf16[512,1024]{1,0:T(8,128)(2,1)S(1)} %copy-done.61, bf16[512,1408]{1,0:T(8,128)(2,1)} %get-tuple-element.81, bf16[512,1408]{1,0:T(8,128)(2,1)} %get-tuple-element.82), kind=kOutput, calls=%fused_computation.3 | convolution fusion | flops 2961440768 | bytes 9699328 | tf_op jit(solution)/shard_map/dot_general | solution.py:440
  232.3 7.7 %collective-permute-done.13 = bf16[2816,512]{1,0:T(8,128)(2,1)S(1)} collective-permute-done((bf16[2816,512]{1,0:T(8,128)(2,1)S(1)}, bf16[2816,512]{1,0:T(8,128)(2,1)S(1)}, u32[]{:S(2)}, u32[]{:S(2)}) %collective-permute-start.13) | collective-permute-done | bytes 2883616 | tf_op jit(solution)/shard_map/ppermute | solution.py:455
  240.0 4.9 add_convert_fusion.2.other_ref
  244.9 9.5 %add_convert_fusion.other_ref = bf16[1024,2816]{1,0:T(8,128)(2,1)} fusion(bf16[1024,2816]{1,0:T(8,128)(2,1)} %collective-permute-done.14, bf16[512,1024]{1,0:T(8,128)(2,1)} %multiply_convert_fusion.6.other_ref, bf16[512,2816]{1,0:T(8,128)(2,1)} %after.37), kind=kOutput, calls=%fused_computation | convolution fusion | flops 2961440768 | bytes 15466496 | tf_op jit(solution)/shard_map/dot_general | solution.py:440
  254.5 6.2 %fusion.26 = f32[512,1024]{1,0:T(8,128)S(1)} fusion(bf16[1024,2816]{1,0:T(8,128)(2,1)} %collective-permute-done.12, bf16[512,1408]{1,0:T(8,128)(2,1)} %get-tuple-element.81, bf16[512,1408]{1,0:T(8,128)(2,1)} %get-tuple-element.82), kind=kOutput, calls=%fused_computation.66 | convolution fusion | flops 2958557184 | bytes 10747904 | tf_op jit(solution)/shard_map/dot_general | solution.py:446
  266.2 5.9 %multiply_reduce_fusion = (bf16[1024]{0:T(1024)(128)(2,1)S(1)}, f32[512]{0:T(512)S(1)}, f32[512,1024]{1,0:T(8,128)S(1)}) fusion(f32[512,1024]{1,0:T(8,128)S(1)} %copy-done.39, f32[512]{0:T(512)S(1)} %fusion.55, f32[1024]{0:T(1024)S(1)} %bitcast.140, f32[512,1024]{1,0:T(8,128)S(1)} %fusion.26, bf16[512,2816]{1,0:T(8,128)(2,1)S(1)} %copy-done.50, ...), kind=kOutput, calls=%fused_computation.60 | convolution fusion | flops 2956458496 | bytes 14952448 | tf_op jit(solution)/shard_map/dot_general | solution.py:446
  297.4 30.1 %collective-permute-done.18.array_ref = bf16[704,512]{1,0:T(8,128)(2,1)} collective-permute-done((bf16[704,512]{1,0:T(8,128)(2,1)}, bf16[704,512]{1,0:T(8,128)(2,1)}, u32[]{:S(2)}, u32[]{:S(2)}) %collective-permute-start.18) | collective-permute-done | bytes 720928 | tf_op jit(solution)/shard_map/ppermute | solution.py:528
  337.6 5.8 %collective-permute-done.21 = bf16[1,4,264,128]{3,2,1,0:T(8,128)(2,1)S(1)} collective-permute-done((bf16[1,4,264,128]{3,2,1,0:T(8,128)(2,1)S(1)}, bf16[1,4,264,128]{3,2,1,0:T(8,128)(2,1)S(1)}, u32[]{:S(2)}, u32[]{:S(2)}) %collective-permute-start.21) | collective-permute-done | bytes 270368 | tf_op jit(solution)/shard_map/ppermute | solution.py:426
  352.6 11.9 %scan_backward.1 = (bf16[512,1536]{1,0:T(8,128)(2,1)S(1)}, bf16[512,1536]{1,0:T(8,128)(2,1)S(1)}, f32[512,512]{1,0:T(8,128)S(1)}) custom-call(f32[512,1536]{1,0:T(8,128)} %copy-done.2, f32[512,1536]{1,0:T(8,128)} %copy-done.2, f32[512,1536]{1,0:T(8,128)} %copy-done.2, f32[512,1536]{1,0:T(8,128)} %copy-done.3, f32[512,1536]{1,0:T(8,128)} %copy-done.3, ...), custom_call_target="tpu_custom_call" | custom-call | tf_op jit(solution)/shard_map/scan_backward/pallas_call | solution.py:353
  368.9 5.0 convolution_convert_fusion.2
  374.0 6.0 %collective-permute-done.22 = bf16[1024,1536]{1,0:T(8,128)(2,1)} collective-permute-done((bf16[1024,1536]{1,0:T(8,128)(2,1)}, bf16[1024,1536]{1,0:T(8,128)(2,1)}, u32[]{:S(2)}, u32[]{:S(2)}) %collective-permute-start.22) | collective-permute-done | bytes 3145760 | tf_op jit(solution)/shard_map/ppermute | solution.py:455
  399.1 7.5 %collective-permute-done.23.array_ref = bf16[256,1536]{1,0:T(8,128)(2,1)S(1)} collective-permute-done((bf16[256,1536]{1,0:T(8,128)(2,1)S(1)}, bf16[256,1536]{1,0:T(8,128)(2,1)S(1)}, u32[]{:S(2)}, u32[]{:S(2)}) %collective-permute-start.23) | collective-permute-done | bytes 786464 | tf_op jit(solution)/shard_map/ppermute | solution.py:528
  431.9 8.3 %collective-permute-done.28.array_ref = bf16[256,1536]{1,0:T(8,128)(2,1)} collective-permute-done((bf16[256,1536]{1,0:T(8,128)(2,1)}, bf16[256,1536]{1,0:T(8,128)(2,1)}, u32[]{:S(2)}, u32[]{:S(2)}) %collective-permute-start.28) | collective-permute-done | bytes 786464 | tf_op jit(solution)/shard_map/ppermute | solution.py:528
  448.0 12.0 %all-reduce.6.cloned.1.call-done.array_ref = bf16[256,2816]{1,0:T(8,128)(2,1)} async-done(((bf16[256,2816]{1,0:T(8,128)(2,1)}), bf16[256,2816]{1,0:T(8,128)(2,1)}) %all-reduce.6.cloned.1.call-update) | async-done | bytes 1441808 | tf_op jit(solution)/shard_map/psum | solution.py:727
  464.5 4.9 fusion.25
  473.9 66.7 %all-reduce.8.cloned.1.call-done = (bf16[272,512]{1,0:T(8,128)(2,1)}, bf16[256,1536]{1,0:T(8,128)(2,1)}, bf16[704,512]{1,0:T(8,128)(2,1)}) async-done(((bf16[272,512]{1,0:T(8,128)(2,1)}, bf16[256,1536]{1,0:T(8,128)(2,1)}, bf16[704,512]{1,0:T(8,128)(2,1)}), (bf16[272,512]{1,0:T(8,128)(2,1)}, bf16[256,1536]{1,0:T(8,128)(2,1)}, bf16[704,512]{1,0:T(8,128)(2,1)})) %all-reduce.8.cloned.1.call-update) | async-done | bytes 1785872 | tf_op jit(solution)/shard_map/psum | solution.py:729
  (424 shorter events, 238.5 us)
Async XLA Ops:
  7.2 65.7 %all-gather.3.cloned.1.call-start = ((), (), s32[]{:S(2)}) async-start(), calls=%async_computation.1 | async-start | bytes 4259840 | tf_op jit(solution)/shard_map/all_gather | solution.py:572
  16.5 180.8 %all-gather.5.cloned.1.call-start = ((), (), s32[]{:S(2)}) async-start(), calls=%async_computation.2 | async-start | bytes 7208960 | tf_op jit(solution)/shard_map/all_gather | solution.py:573
  19.0 348.7 %reduce-scatter.2.cloned.1.call-start = ((), (), s32[]{:S(2)}) async-start(), calls=%async_computation.3 | async-start | bytes 7208960 | tf_op jit(solution)/shard_map/reduce_scatter | solution.py:499
  25.3 19.0 %collective-permute-start.2 = (bf16[256,512]{1,0:T(8,128)(2,1)S(1)}, bf16[256,512]{1,0:T(8,128)(2,1)S(1)}, u32[]{:S(2)}, u32[]{:S(2)}) collective-permute-start(bf16[256,512]{1,0:T(8,128)(2,1)S(1)} %get-tuple-element.76), channel_id=1, source_target_pairs={{0,3},{1,2},{2,1},{3,0},{4,7},{5,6},{6,5},{7,4},{8,11},{9,10},{10,... | collective-permute-start | bytes 786440 | tf_op jit(solution)/shard_map/ppermute | solution.py:514
  72.9 65.0 %collective-permute-start.3 = (bf16[1024,1664]{1,0:T(8,128)(2,1)}, bf16[1024,1664]{1,0:T(8,128)(2,1)}, u32[]{:S(2)}, u32[]{:S(2)}) collective-permute-start(bf16[1024,1664]{1,0:T(8,128)(2,1)} %after.31.other_ref), channel_id=1, source_target_pairs={{0,4},{4,0},{1,5},{5,1},{2,6},{6,2},{3,7},{7,3},{8,12},{12,8},{9,1... | collective-permute-start | bytes 10223624 | tf_op jit(solution)/shard_map/ppermute | solution.py:455
  76.0 61.9 %collective-permute-start.4 = (bf16[1024,512]{1,0:T(8,128)(2,1)}, bf16[1024,512]{1,0:T(8,128)(2,1)}, u32[]{:S(2)}, u32[]{:S(2)}) collective-permute-start(bf16[1024,512]{1,0:T(8,128)(2,1)} %constant_dynamic-update-slice_fusion.4.other_ref), channel_id=1, source_target_pairs={{0,4},{4,0},{1,5},{5,1},{2,6},{6,2},{3,7},{7,3},{8,12},{12,8},{9,1... | collective-permute-start | bytes 3145736 | tf_op jit(solution)/shard_map/ppermute | solution.py:455
  77.0 53.7 %collective-permute-start.10 = (bf16[704,512]{1,0:T(8,128)(2,1)}, bf16[704,512]{1,0:T(8,128)(2,1)S(1)}, u32[]{:S(2)}, u32[]{:S(2)}) collective-permute-start(bf16[704,512]{1,0:T(8,128)(2,1)} %after.33), channel_id=1, source_target_pairs={{0,3},{1,2},{2,1},{3,0},{4,7},{5,6},{6,5},{7,4},{8,11},{9,10},{10,... | collective-permute-start | bytes 2162696 | tf_op jit(solution)/shard_map/ppermute | solution.py:514
  78.5 51.3 %collective-permute-start.9 = (bf16[704,512]{1,0:T(8,128)(2,1)}, bf16[704,512]{1,0:T(8,128)(2,1)S(1)}, u32[]{:S(2)}, u32[]{:S(2)}) collective-permute-start(bf16[704,512]{1,0:T(8,128)(2,1)} %after.33), channel_id=1, source_target_pairs={{0,2},{1,3},{2,0},{3,1},{4,6},{5,7},{6,4},{7,5},{8,10},{9,11},{10,... | collective-permute-start | bytes 2162696 | tf_op jit(solution)/shard_map/ppermute | solution.py:514
  80.0 47.8 %collective-permute-start.8 = (bf16[704,512]{1,0:T(8,128)(2,1)}, bf16[704,512]{1,0:T(8,128)(2,1)}, u32[]{:S(2)}, u32[]{:S(2)}) collective-permute-start(bf16[704,512]{1,0:T(8,128)(2,1)} %after.33), channel_id=1, source_target_pairs={{0,1},{1,0},{2,3},{3,2},{4,5},{5,4},{6,7},{7,6},{8,9},{9,8},{10,11... | collective-permute-start | bytes 2162696 | tf_op jit(solution)/shard_map/ppermute | solution.py:514
  131.6 56.1 %collective-permute-start.11 = (bf16[2816,512]{1,0:T(8,128)(2,1)}, bf16[2816,512]{1,0:T(8,128)(2,1)}, u32[]{:S(2)}, u32[]{:S(2)}) collective-permute-start(bf16[2816,512]{1,0:T(8,128)(2,1)} %constant_dynamic-update-slice_fusion.other_ref), channel_id=1, source_target_pairs={{0,4},{4,0},{1,5},{5,1},{2,6},{6,2},{3,7},{7,3},{8,12},{12,8},{9,1... | collective-permute-start | bytes 8650760 | tf_op jit(solution)/shard_map/ppermute | solution.py:455
  156.3 19.3 %collective-permute-start.6 = (bf16[1,4,264,128]{3,2,1,0:T(8,128)(2,1)S(1)}, bf16[1,4,264,128]{3,2,1,0:T(8,128)(2,1)}, u32[]{:S(2)}, u32[]{:S(2)}) collective-permute-start(bf16[1,4,264,128]{3,2,1,0:T(8,128)(2,1)S(1)} %convert_element_type.283), channel_id=1, source_target_pairs={{0,2},{1,3},{4,6},{5,7},{8,10},{9,11},{12,14},{13,15},{16,18},{17,... | collective-permute-start | bytes 811016 | tf_op jit(solution)/shard_map/ppermute | solution.py:426
  226.4 18.6 %collective-permute-start.14 = (bf16[1024,2816]{1,0:T(8,128)(2,1)}, bf16[1024,2816]{1,0:T(8,128)(2,1)}, u32[]{:S(2)}, u32[]{:S(2)}) collective-permute-start(bf16[1024,2816]{1,0:T(8,128)(2,1)} %convolution_convert_fusion), channel_id=1, source_target_pairs={{0,4},{4,0},{1,5},{5,1},{2,6},{6,2},{3,7},{7,3},{8,12},{12,8},{9,1... | collective-permute-start | bytes 17301512 | tf_op jit(solution)/shard_map/ppermute | solution.py:455
  262.1 66.7 %collective-permute-start.16 = (bf16[704,512]{1,0:T(8,128)(2,1)}, bf16[704,512]{1,0:T(8,128)(2,1)}, u32[]{:S(2)}, u32[]{:S(2)}) collective-permute-start(bf16[704,512]{1,0:T(8,128)(2,1)} %get-tuple-element.88), channel_id=1, source_target_pairs={{0,1},{1,0},{2,3},{3,2},{4,5},{5,4},{6,7},{7,6},{8,9},{9,8},{10,11... | collective-permute-start | bytes 2162696 | tf_op jit(solution)/shard_map/ppermute | solution.py:528
  262.1 65.4 %collective-permute-start.18 = (bf16[704,512]{1,0:T(8,128)(2,1)}, bf16[704,512]{1,0:T(8,128)(2,1)}, u32[]{:S(2)}, u32[]{:S(2)}) collective-permute-start(bf16[704,512]{1,0:T(8,128)(2,1)} %get-tuple-element.89), channel_id=1, source_target_pairs={{0,3},{1,2},{2,1},{3,0},{4,7},{5,6},{6,5},{7,4},{8,11},{9,10},{10,... | collective-permute-start | bytes 2162696 | tf_op jit(solution)/shard_map/ppermute | solution.py:528
  266.2 62.6 %collective-permute-start.17 = (bf16[704,512]{1,0:T(8,128)(2,1)}, bf16[704,512]{1,0:T(8,128)(2,1)}, u32[]{:S(2)}, u32[]{:S(2)}) collective-permute-start(bf16[704,512]{1,0:T(8,128)(2,1)} %get-tuple-element.90), channel_id=1, source_target_pairs={{0,2},{1,3},{2,0},{3,1},{4,6},{5,7},{6,4},{7,5},{8,10},{9,11},{10,... | collective-permute-start | bytes 2162696 | tf_op jit(solution)/shard_map/ppermute | solution.py:528
  296.1 47.5 %collective-permute-start.15 = (bf16[1024,512]{1,0:T(8,128)(2,1)}, bf16[1024,512]{1,0:T(8,128)(2,1)}, u32[]{:S(2)}, u32[]{:S(2)}) collective-permute-start(bf16[1024,512]{1,0:T(8,128)(2,1)} %convolution_convert_fusion.3), channel_id=1, source_target_pairs={{0,4},{4,0},{1,5},{5,1},{2,6},{6,2},{3,7},{7,3},{8,12},{12,8},{9,1... | collective-permute-start | bytes 3145736 | tf_op jit(solution)/shard_map/ppermute | solution.py:455
  296.1 41.5 %collective-permute-start.20 = (bf16[1,4,264,128]{3,2,1,0:T(8,128)(2,1)S(1)}, bf16[1,4,264,128]{3,2,1,0:T(8,128)(2,1)S(1)}, u32[]{:S(2)}, u32[]{:S(2)}) collective-permute-start(bf16[1,4,264,128]{3,2,1,0:T(8,128)(2,1)S(1)} %pad_maximum_fusion.8), channel_id=1, source_target_pairs={{2,0},{3,1},{6,4},{7,5},{10,8},{11,9},{14,12},{15,13},{18,16},{19,... | collective-permute-start | bytes 811016 | tf_op jit(solution)/shard_map/ppermute | solution.py:426
  367.7 92.3 %all-reduce.6.cloned.1.call-start = ((), (), s32[]{:S(2)}) async-start(), calls=%async_computation.4 | async-start | bytes 2883584 | tf_op jit(solution)/shard_map/psum | solution.py:727
  386.2 20.4 %collective-permute-start.23 = (bf16[256,1536]{1,0:T(8,128)(2,1)S(1)}, bf16[256,1536]{1,0:T(8,128)(2,1)S(1)}, u32[]{:S(2)}, u32[]{:S(2)}) collective-permute-start(bf16[256,1536]{1,0:T(8,128)(2,1)S(1)} %get-tuple-element.87), channel_id=1, source_target_pairs={{0,1},{1,0},{2,3},{3,2},{4,5},{5,4},{6,7},{7,6},{8,9},{9,8},{10,11... | collective-permute-start | bytes 2359304 | tf_op jit(solution)/shard_map/ppermute | solution.py:528
  396.3 144.2 %all-reduce.8.cloned.1.call-start = ((), (), s32[]{:S(2)}) async-start(), calls=%async_computation.5 | async-start | bytes 3571712 | tf_op jit(solution)/shard_map/psum | solution.py:729
  396.6 43.6 %collective-permute-start.28 = (bf16[256,1536]{1,0:T(8,128)(2,1)}, bf16[256,1536]{1,0:T(8,128)(2,1)}, u32[]{:S(2)}, u32[]{:S(2)}) collective-permute-start(bf16[256,1536]{1,0:T(8,128)(2,1)} %get-tuple-element.85), channel_id=1, source_target_pairs={{0,2},{1,3},{2,0},{3,1},{4,6},{5,7},{6,4},{7,5},{8,10},{9,11},{10,... | collective-permute-start | bytes 2359304 | tf_op jit(solution)/shard_map/ppermute | solution.py:528
  396.7 43.5 %collective-permute-start.29 = (bf16[256,1536]{1,0:T(8,128)(2,1)}, bf16[256,1536]{1,0:T(8,128)(2,1)}, u32[]{:S(2)}, u32[]{:S(2)}) collective-permute-start(bf16[256,1536]{1,0:T(8,128)(2,1)} %get-tuple-element.86), channel_id=1, source_target_pairs={{0,3},{1,2},{2,1},{3,0},{4,7},{5,6},{6,5},{7,4},{8,11},{9,10},{10,... | collective-permute-start | bytes 2359304 | tf_op jit(solution)/shard_map/ppermute | solution.py:528
  424.7 16.9 %collective-permute-start.26 = (bf16[272,512]{1,0:T(8,128)(2,1)}, bf16[272,512]{1,0:T(8,128)(2,1)S(1)}, u32[]{:S(2)}, u32[]{:S(2)}) collective-permute-start(bf16[272,512]{1,0:T(8,128)(2,1)} %get-tuple-element.98), channel_id=1, source_target_pairs={{0,3},{1,2},{2,1},{3,0},{4,7},{5,6},{6,5},{7,4},{8,11},{9,10},{10,... | collective-permute-start | bytes 835592 | tf_op jit(solution)/shard_map/ppermute | solution.py:528
  424.7 20.5 %collective-permute-start.25 = (bf16[272,512]{1,0:T(8,128)(2,1)}, bf16[272,512]{1,0:T(8,128)(2,1)S(1)}, u32[]{:S(2)}, u32[]{:S(2)}) collective-permute-start(bf16[272,512]{1,0:T(8,128)(2,1)} %get-tuple-element.99), channel_id=1, source_target_pairs={{0,2},{1,3},{2,0},{3,1},{4,6},{5,7},{6,4},{7,5},{8,10},{9,11},{10,... | collective-permute-start | bytes 835592 | tf_op jit(solution)/shard_map/ppermute | solution.py:528
  (111 other events, 664.0 us)
Sparse Core Ops, SparseCore 0:
  16.6 56.2 all-gather.2
  75.3 100.2 all-gather.4
  254.5 109.7 reduce-scatter.1
  396.4 63.5 all-reduce.5
  463.6 76.8 all-reduce.7

commit v8 on v7

--- a/solution.py
+++ b/solution.py
@@ -614,11 +614,11 @@
     attended, mixed = mix_forward(
         local_out, forget, incoming_state, mine, theirs, head_gain_f[None, :], seqs_here, chunk
     )
-    down_theirs = swapped(down_mine)
-    mixed = jnp.concatenate(halves_of(after(mixed, down_theirs)), 1)
+    mixed = jnp.concatenate(halves_of(mixed), 1)
     resid = inputs + joined(product(mixed, output_mine), product(mixed, output_theirs), 1)
     normed_two = first_norm(resid, gain_two).astype(jnp.bfloat16)
     ffn_mine = after(ffn_mine, normed_two)
+    down_theirs = swapped(down_mine)
     ffn_theirs = swapped(ffn_mine)
 
     def swiglu(both):
@@ -649,10 +649,7 @@
     grad_mine, grad_theirs = halves_of(hidden_grad)
     back_mine, back_theirs = swiglu_back(both_mine, grad_mine), swiglu_back(both_theirs, grad_theirs)
 
-    down_came = swapped(low(product_left(hidden, low_theirs)))
     ffn_came = swapped(low(product_left(normed_two, back_theirs)))
-    down_pair = low(product_left(hidden, low_mine) + down_came.astype(jnp.float32))
-    back_mine = after(back_mine, down_pair)
     normed_two_grad = product_right(back_mine, ffn_mine) + product_right(back_theirs, ffn_theirs)
     norm_pulled = jax.vjp(first_norm, resid, gain_two)[1](normed_two_grad)
     resid_grad = grad_out + norm_pulled[0]
@@ -674,8 +671,9 @@
     output_came = swapped(low(product_left(mixed, after(branch_theirs, attended_grad))))
     output_pair = product_left(mixed, after(branch_mine, attended_grad)) + output_came.astype(jnp.float32)
     output_pair = low(output_pair)
-    down_share, _ = gathered_sum(down_pair, attended_grad)
-    attended_grad = after(after(attended_grad, output_pair), down_share)
+    down_came = swapped(low(product_left(hidden, after(low_theirs, attended_grad))))
+    down_pair = low(product_left(hidden, after(low_mine, attended_grad)) + down_came.astype(jnp.float32))
+    attended_grad = after(after(attended_grad, output_pair), down_pair)
     packed_mine, packed_theirs, gates_grad = scan_backward(
         mine, theirs, gates, scores, states, starts, incoming_state,
         attended_grad, later_grad, outgate_grads, seqs_here, chunk,
@@ -723,6 +721,7 @@
         axis=1,
     ).reshape(-1, width // 2)
     rest_share, _ = gathered_sum(rest_pair, mixer_pair)
+    down_share, _ = gathered_sum(after(down_pair, later_grad), tokens_grad)
 
     ffn_total = after(lax.psum(ffn_share, "z"), rest_share)
     ffn_other = swapped(ffn_total)

time: 574 us -> 565 us (0.984)
  matrix products: 108 us -> 98.5 us
    ppermute x6, waiting for transfers between devices: 60.5 us -> 41.7 us  [spread(): came = lax.ppermute(array, 'seq', [(i, i ^ distance) for i in range(count)])]
    ppermute x6, waiting for transfers between devices: 23.7 us -> 42.4 us  [from_neighbours(): came = lax.ppermute(summary, 'seq', pairs)]
    psum x1, waiting for transfers between devices: 12 us -> 0.01 us  [local(): ffn_total = after(lax.psum(ffn_share, 'z'), rest_share)]
    ppermute x12, waiting for transfers between devices: 13.8 us -> 21.3 us  [swapped(): return lax.ppermute(array, 'core', [(0, 1), (1, 0)])]
    unnamed x203 -> x221, local copies, waits for them, and re-layouts: 53 us -> 53.9 us
  transfers between devices with their start and end apart: 38 -> 38, of which waited for: 17 -> 18; matrix products, arithmetic and copies ran while one was open for 25% -> 26% of each run, Pallas kernels for 4% -> 4%
where the time goes in v8:
time: 565 us; the launch traced here: 555 us
  waiting for transfers between devices  257 us (45%)
  matrix products  98.5 us (17%)
  local copies, waits for them, and re-layouts  88.6 us (16%)
  other arithmetic  43.1 us (8%)
  starting transfers between devices  29.5 us (5%)
  Pallas kernels  23.4 us (4%)
  between operations  15.6 us (3%)
    psum x1, waiting for transfers between devices, local(): lax.psum(tuple((after(share, ffn_total) for share in (mixer_share, down_s...  67.1 us
    unnamed x221, local copies, waits for them, and re-layouts  53.9 us
    ppermute x9, waiting for transfers between devices, gathered_sum(): came = lax.ppermute(piece, 'seq', [(i, i ^ distance) for i in range(count)])  53.8 us
    ppermute x6, waiting for transfers between devices, from_neighbours(): came = lax.ppermute(summary, 'seq', pairs)  42.4 us
    ppermute x6, waiting for transfers between devices, spread(): came = lax.ppermute(array, 'seq', [(i, i ^ distance) for i in range(count)])  41.7 us
    dot_general x9, matrix products, product_left(): lax.dot_general(left, right, (((0,), (0,)), ((), ())), preferred_element_...  36.2 us
    dot_general x9, matrix products, product_right(): lax.dot_general(left, right, (((1,), (1,)), ((), ())), preferred_element_...  30.8 us
    all_gather x1, waiting for transfers between devices, local(): mixer_mine = lax.all_gather(mixer_packed, 'seq', tiled=True)  27.8 us
  transfers between devices with their start and end apart: 38, of which 18 were waited for; matrix products, arithmetic and copies ran while one was open for 26% of the time, Pallas kernels for 4%

profile of v8, /device:TPU:0, one launch (start us, length us, event | category | flops | bytes accessed | tf_op | source)
XLA Modules:
  0.0 555.3 jit_solution(8124024015829920294)
XLA Ops:
  25.3 8.1 %collective-permute-done = bf16[256,512]{1,0:T(8,128)(2,1)S(1)} collective-permute-done((bf16[256,512]{1,0:T(8,128)(2,1)S(1)}, bf16[256,512]{1,0:T(8,128)(2,1)S(1)}, u32[]{:S(2)}, u32[]{:S(2)}) %collective-permute-start) | collective-permute-done | bytes 262176 | tf_op jit(solution)/shard_map/ppermute | solution.py:514
  34.1 4.8 collective-permute-done.1
  45.0 27.8 %all-gather.3.cloned.1.call-done.array_ref = bf16[1024,1664]{1,0:T(8,128)(2,1)} async-done(((bf16[256,1664]{1,0:T(8,128)(2,1)}), bf16[1024,1664]{1,0:T(8,128)(2,1)}) %all-gather.3.cloned.1.call-update) | async-done | bytes 3407888 | tf_op jit(solution)/shard_map/all_gather | solution.py:572
  94.1 5.7 %scan_forward.1 = (f32[512,1024]{1,0:T(8,128)S(1)}, bf16[512,512]{1,0:T(8,128)(2,1)S(1)}, bf16[4,4,128,128]{3,2,1,0:T(8,128)(2,1)S(1)}, f32[4,4,256,128]{3,2,1,0...) custom-call(f32[512,1536]{1,0:T(8,128)S(1)} %fusion.11.q0.k0.v0.og0, ...), custom_call_target="tpu_custom_call" | custom-call | tf_op jit(solution)/shard_map/scan_forward/pallas_call | solution.py:317
  104.0 24.1 %collective-permute-done.8 = bf16[704,512]{1,0:T(8,128)(2,1)} collective-permute-done((bf16[704,512]{1,0:T(8,128)(2,1)}, bf16[704,512]{1,0:T(8,128)(2,1)}, u32[]{:S(2)}, u32[]{:S(2)}) %collective-permute-start.8) | collective-permute-done | bytes 720928 | tf_op jit(solution)/shard_map/ppermute | solution.py:514
  139.1 7.2 %collective-permute-done.6 = bf16[1,4,264,128]{3,2,1,0:T(8,128)(2,1)S(1)} collective-permute-done((bf16[1,4,264,128]{3,2,1,0:T(8,128)(2,1)S(1)}, bf16[1,4,264,128]{3,2,1,0:T(8,128)(2,1)S(1)}, u32[]{:S(2)}, u32[]{:S(2)}) %collective-permute-start.6) | collective-permute-done | bytes 270368 | tf_op jit(solution)/shard_map/ppermute | solution.py:426
  172.1 11.9 %collective-permute-done.12 = bf16[2816,512]{1,0:T(8,128)(2,1)S(1)} collective-permute-done((bf16[2816,512]{1,0:T(8,128)(2,1)}, bf16[2816,512]{1,0:T(8,128)(2,1)S(1)}, u32[]{:S(2)}, u32[]{:S(2)}) %collective-permute-start.12) | collective-permute-done | bytes 2883616 | tf_op jit(solution)/shard_map/ppermute | solution.py:455
  207.4 9.3 %collective-permute-done.13 = bf16[1024,2816]{1,0:T(8,128)(2,1)S(1)} collective-permute-done((bf16[1024,2816]{1,0:T(8,128)(2,1)S(1)}, bf16[1024,2816]{1,0:T(8,128)(2,1)S(1)}, u32[]{:S(2)}, u32[]{:S(2)}) %collective-permute-start.13) | collective-permute-done | bytes 5767200 | tf_op jit(solution)/shard_map/ppermute | solution.py:455
  216.7 5.1 add_convert_fusion.other_ref
  221.8 6.2 %fusion.28 = f32[512,1024]{1,0:T(8,128)S(1)} fusion(bf16[1024,2816]{1,0:T(8,128)(2,1)} %after.36, bf16[512,1408]{1,0:T(8,128)(2,1)} %copy-done.74, bf16[512,1408]{1,0:T(8,128)(2,1)} %copy-done.75), kind=kOutput, calls=%fused_computation.68 | convolution fusion | flops 2958557184 | bytes 10747904 | tf_op jit(solution)/shard_map/dot_general | solution.py:446
  228.1 6.2 %multiply_reduce_fusion = (bf16[1024]{0:T(1024)(128)(2,1)S(1)}, f32[512]{0:T(512)S(1)}, f32[512,1024]{1,0:T(8,128)S(1)}) fusion(f32[512,1024]{1,0:T(8,128)S(1)} %copy-done.39, f32[512]{0:T(512)S(1)} %fusion.56, f32[1024]{0:T(1024)S(1)} %bitcast.139, f32[512,1024]{1,0:T(8,128)S(1)} %fusion.28, bf16[1024,2816]{1,0:T(8,128)(2,1)} %copy-done.102, ...), kind=kOutput, calls=%fused_computation.60 | convolution fusion | flops 2962225664 | bytes 14952448 | tf_op jit(solution)/shard_map/dot_general | solution.py:446
  255.7 5.4 convolution_convert_fusion.1
  269.5 15.3 %collective-permute-done.16 = bf16[1,4,264,128]{3,2,1,0:T(8,128)(2,1)S(1)} collective-permute-done((bf16[1,4,264,128]{3,2,1,0:T(8,128)(2,1)S(1)}, bf16[1,4,264,128]{3,2,1,0:T(8,128)(2,1)S(1)}, u32[]{:S(2)}, u32[]{:S(2)}) %collective-permute-start.16) | collective-permute-done | bytes 270368 | tf_op jit(solution)/shard_map/ppermute | solution.py:426
  284.8 6.6 %collective-permute-done.17 = bf16[1,4,264,128]{3,2,1,0:T(8,128)(2,1)} collective-permute-done((bf16[1,4,264,128]{3,2,1,0:T(8,128)(2,1)S(1)}, bf16[1,4,264,128]{3,2,1,0:T(8,128)(2,1)}, u32[]{:S(2)}, u32[]{:S(2)}) %collective-permute-start.17) | collective-permute-done | bytes 270368 | tf_op jit(solution)/shard_map/ppermute | solution.py:426
  292.1 8.7 %collective-permute-done.18 = bf16[1,4,264,128]{3,2,1,0:T(8,128)(2,1)S(1)} collective-permute-done((bf16[1,4,264,128]{3,2,1,0:T(8,128)(2,1)S(1)}, bf16[1,4,264,128]{3,2,1,0:T(8,128)(2,1)S(1)}, u32[]{:S(2)}, u32[]{:S(2)}) %collective-permute-start.18) | collective-permute-done | bytes 270368 | tf_op jit(solution)/shard_map/ppermute | solution.py:426
  306.4 6.2 %add_convert_fusion.2.other_ref.array_ref = bf16[2816,512]{1,0:T(8,128)(2,1)} fusion(bf16[2816,512]{1,0:T(8,128)(2,1)} %collective-permute-done.15, bf16[512,512]{1,0:T(8,128)(2,1)S(1)} %copy-done.54, bf16[512,1408]{1,0:T(8,128)(2,1)} %get-tuple-element.84, bf16[512,1408]{1,0:T(8,128)(2,1)S(1)} %copy-done.67, pred[]{:T(512)S(6)} %eq.10), kind=kOutput, calls=%fused_computation.2 | convolution fusion | flops 1493696512 | bytes 9175041 | tf_op jit(solution)/shard_map/dot_general | solution.py:440
  318.5 11.9 %scan_backward.1 = (bf16[512,1536]{1,0:T(8,128)(2,1)S(1)}, bf16[512,1536]{1,0:T(8,128)(2,1)S(1)}, f32[512,512]{1,0:T(8,128)S(1)}) custom-call(f32[512,1536]{1,0:T(8,128)} %copy-done.2, f32[512,1536]{1,0:T(8,128)} %copy-done.2, f32[512,1536]{1,0:T(8,128)} %copy-done.2, f32[512,1536]{1,0:T(8,128)} %copy-done.3, f32[512,1536]{1,0:T(8,128)} %copy-done.3, ...), custom_call_target="tpu_custom_call" | custom-call | tf_op jit(solution)/shard_map/scan_backward/pallas_call | solution.py:353
  335.0 5.0 convolution_convert_fusion.2
  340.1 6.3 %convolution_bitcast_fusion.1 = f32[1,512,512]{2,1,0:T(8,128)} fusion(bf16[2816,512]{1,0:T(8,128)(2,1)} %constant_dynamic-update-slice_fusion.other_ref, bf16[512,1408]{1,0:T(8,128)(2,1)} %get-tuple-element.84, bf16[512,1408]{1,0:T(8,128)(2,1)} %get-tuple-element.83, pred[]{:T(512)S(6)} %eq.10), kind=kOutput, calls=%fused_computation.82 | convolution fusion | flops 1489371136 | bytes 6815745 | tf_op jit(solution)/shard_map/dot_general | solution.py:436
  363.8 9.2 %collective-permute-done.20.array_ref = bf16[256,1536]{1,0:T(8,128)(2,1)S(1)} collective-permute-done((bf16[256,1536]{1,0:T(8,128)(2,1)S(1)}, bf16[256,1536]{1,0:T(8,128)(2,1)S(1)}, u32[]{:S(2)}, u32[]{:S(2)}) %collective-permute-start.20) | collective-permute-done | bytes 786464 | tf_op jit(solution)/shard_map/ppermute | solution.py:528
  392.5 36.7 %collective-permute-done.25.array_ref = bf16[256,1536]{1,0:T(8,128)(2,1)} collective-permute-done((bf16[256,1536]{1,0:T(8,128)(2,1)}, bf16[256,1536]{1,0:T(8,128)(2,1)}, u32[]{:S(2)}, u32[]{:S(2)}) %collective-permute-start.25) | collective-permute-done | bytes 786464 | tf_op jit(solution)/shard_map/ppermute | solution.py:528
  432.4 4.8 fusion.25.other_ref
  444.3 5.0 collective-permute-done.22.array_ref
  465.3 67.1 %all-reduce.8.cloned.1.call-done = (bf16[272,512]{1,0:T(8,128)(2,1)}, bf16[256,1536]{1,0:T(8,128)(2,1)}, bf16[704,512]{1,0:T(8,128)(2,1)}) async-done(((bf16[272,512]{1,0:T(8,128)(2,1)}, bf16[256,1536]{1,0:T(8,128)(2,1)}, bf16[704,512]{1,0:T(8,128)(2,1)}), (bf16[272,512]{1,0:T(8,128)(2,1)}, bf16[256,1536]{1,0:T(8,128)(2,1)}, bf16[704,512]{1,0:T(8,128)(2,1)})) %all-reduce.8.cloned.1.call-update) | async-done | bytes 1785872 | tf_op jit(solution)/shard_map/psum | solution.py:728
  (442 shorter events, 235.0 us)
Async XLA Ops:
  7.2 65.7 %all-gather.3.cloned.1.call-start = ((), (), s32[]{:S(2)}) async-start(), calls=%async_computation.1 | async-start | bytes 4259840 | tf_op jit(solution)/shard_map/all_gather | solution.py:572
  16.5 153.8 %all-gather.5.cloned.1.call-start = ((), (), s32[]{:S(2)}) async-start(), calls=%async_computation.2 | async-start | bytes 7208960 | tf_op jit(solution)/shard_map/all_gather | solution.py:573
  19.0 314.7 %reduce-scatter.2.cloned.1.call-start = ((), (), s32[]{:S(2)}) async-start(), calls=%async_computation.3 | async-start | bytes 7208960 | tf_op jit(solution)/shard_map/reduce_scatter | solution.py:499
  23.8 15.1 %collective-permute-start.1 = (bf16[256,512]{1,0:T(8,128)(2,1)S(1)}, bf16[256,512]{1,0:T(8,128)(2,1)S(1)}, u32[]{:S(2)}, u32[]{:S(2)}) collective-permute-start(bf16[256,512]{1,0:T(8,128)(2,1)S(1)} %get-tuple-element.76), channel_id=1, source_target_pairs={{0,2},{1,3},{2,0},{3,1},{4,6},{5,7},{6,4},{7,5},{8,10},{9,11},{10,... | collective-permute-start | bytes 786440 | tf_op jit(solution)/shard_map/ppermute | solution.py:514
  25.3 19.0 %collective-permute-start.2 = (bf16[256,512]{1,0:T(8,128)(2,1)S(1)}, bf16[256,512]{1,0:T(8,128)(2,1)S(1)}, u32[]{:S(2)}, u32[]{:S(2)}) collective-permute-start(bf16[256,512]{1,0:T(8,128)(2,1)S(1)} %get-tuple-element.76), channel_id=1, source_target_pairs={{0,3},{1,2},{2,1},{3,0},{4,7},{5,6},{6,5},{7,4},{8,11},{9,10},{10,... | collective-permute-start | bytes 786440 | tf_op jit(solution)/shard_map/ppermute | solution.py:514
  72.9 17.0 %collective-permute-start.3 = (bf16[1024,1664]{1,0:T(8,128)(2,1)}, bf16[1024,1664]{1,0:T(8,128)(2,1)}, u32[]{:S(2)}, u32[]{:S(2)}) collective-permute-start(bf16[1024,1664]{1,0:T(8,128)(2,1)} %after.32.other_ref), channel_id=1, source_target_pairs={{0,4},{4,0},{1,5},{5,1},{2,6},{6,2},{3,7},{7,3},{8,12},{12,8},{9,1... | collective-permute-start | bytes 10223624 | tf_op jit(solution)/shard_map/ppermute | solution.py:455
  77.0 57.3 %collective-permute-start.10 = (bf16[704,512]{1,0:T(8,128)(2,1)}, bf16[704,512]{1,0:T(8,128)(2,1)}, u32[]{:S(2)}, u32[]{:S(2)}) collective-permute-start(bf16[704,512]{1,0:T(8,128)(2,1)} %after.34), channel_id=1, source_target_pairs={{0,3},{1,2},{2,1},{3,0},{4,7},{5,6},{6,5},{7,4},{8,11},{9,10},{10,... | collective-permute-start | bytes 2162696 | tf_op jit(solution)/shard_map/ppermute | solution.py:514
  78.5 51.6 %collective-permute-start.9 = (bf16[704,512]{1,0:T(8,128)(2,1)}, bf16[704,512]{1,0:T(8,128)(2,1)}, u32[]{:S(2)}, u32[]{:S(2)}) collective-permute-start(bf16[704,512]{1,0:T(8,128)(2,1)} %after.34), channel_id=1, source_target_pairs={{0,2},{1,3},{2,0},{3,1},{4,6},{5,7},{6,4},{7,5},{8,10},{9,11},{10,... | collective-permute-start | bytes 2162696 | tf_op jit(solution)/shard_map/ppermute | solution.py:514
  80.0 48.2 %collective-permute-start.8 = (bf16[704,512]{1,0:T(8,128)(2,1)}, bf16[704,512]{1,0:T(8,128)(2,1)}, u32[]{:S(2)}, u32[]{:S(2)}) collective-permute-start(bf16[704,512]{1,0:T(8,128)(2,1)} %after.34), channel_id=1, source_target_pairs={{0,1},{1,0},{2,3},{3,2},{4,5},{5,4},{6,7},{7,6},{8,9},{9,8},{10,11... | collective-permute-start | bytes 2162696 | tf_op jit(solution)/shard_map/ppermute | solution.py:514
  100.6 38.5 %collective-permute-start.5 = (bf16[1,4,264,128]{3,2,1,0:T(8,128)(2,1)S(1)}, bf16[1,4,264,128]{3,2,1,0:T(8,128)(2,1)S(1)}, u32[]{:S(2)}, u32[]{:S(2)}) collective-permute-start(bf16[1,4,264,128]{3,2,1,0:T(8,128)(2,1)S(1)} %convert_element_type.283), channel_id=1, source_target_pairs={{0,1},{1,2},{2,3},{4,5},{5,6},{6,7},{8,9},{9,10},{10,11},{12,13},{... | collective-permute-start | bytes 811016 | tf_op jit(solution)/shard_map/ppermute | solution.py:426
  170.2 23.0 %collective-permute-start.11 = (bf16[1024,2816]{1,0:T(8,128)(2,1)}, bf16[1024,2816]{1,0:T(8,128)(2,1)S(1)}, u32[]{:S(2)}, u32[]{:S(2)}) collective-permute-start(bf16[1024,2816]{1,0:T(8,128)(2,1)} %after.36), channel_id=1, source_target_pairs={{0,4},{4,0},{1,5},{5,1},{2,6},{6,2},{3,7},{7,3},{8,12},{12,8},{9,1... | collective-permute-start | bytes 17301512 | tf_op jit(solution)/shard_map/ppermute | solution.py:455
  261.0 44.3 %collective-permute-start.15 = (bf16[2816,512]{1,0:T(8,128)(2,1)}, bf16[2816,512]{1,0:T(8,128)(2,1)}, u32[]{:S(2)}, u32[]{:S(2)}) collective-permute-start(bf16[2816,512]{1,0:T(8,128)(2,1)} %convolution_convert_fusion.1), channel_id=1, source_target_pairs={{0,4},{4,0},{1,5},{5,1},{2,6},{6,2},{3,7},{7,3},{8,12},{12,8},{9,1... | collective-permute-start | bytes 8650760 | tf_op jit(solution)/shard_map/ppermute | solution.py:455
  265.1 36.9 %collective-permute-start.14 = (bf16[1024,512]{1,0:T(8,128)(2,1)}, bf16[1024,512]{1,0:T(8,128)(2,1)}, u32[]{:S(2)}, u32[]{:S(2)}) collective-permute-start(bf16[1024,512]{1,0:T(8,128)(2,1)} %convolution_convert_fusion.3), channel_id=1, source_target_pairs={{0,4},{4,0},{1,5},{5,1},{2,6},{6,2},{3,7},{7,3},{8,12},{12,8},{9,1... | collective-permute-start | bytes 3145736 | tf_op jit(solution)/shard_map/ppermute | solution.py:455
  265.3 19.6 %collective-permute-start.16 = (bf16[1,4,264,128]{3,2,1,0:T(8,128)(2,1)S(1)}, bf16[1,4,264,128]{3,2,1,0:T(8,128)(2,1)S(1)}, u32[]{:S(2)}, u32[]{:S(2)}) collective-permute-start(bf16[1,4,264,128]{3,2,1,0:T(8,128)(2,1)S(1)} %pad_maximum_fusion.14), channel_id=1, source_target_pairs={{1,0},{2,1},{3,2},{5,4},{6,5},{7,6},{9,8},{10,9},{11,10},{13,12},{... | collective-permute-start | bytes 811016 | tf_op jit(solution)/shard_map/ppermute | solution.py:426
  266.7 24.7 %collective-permute-start.17 = (bf16[1,4,264,128]{3,2,1,0:T(8,128)(2,1)S(1)}, bf16[1,4,264,128]{3,2,1,0:T(8,128)(2,1)}, u32[]{:S(2)}, u32[]{:S(2)}) collective-permute-start(bf16[1,4,264,128]{3,2,1,0:T(8,128)(2,1)S(1)} %pad_maximum_fusion.14), channel_id=1, source_target_pairs={{2,0},{3,1},{6,4},{7,5},{10,8},{11,9},{14,12},{15,13},{18,16},{19,... | collective-permute-start | bytes 811016 | tf_op jit(solution)/shard_map/ppermute | solution.py:426
  268.1 32.8 %collective-permute-start.18 = (bf16[1,4,264,128]{3,2,1,0:T(8,128)(2,1)S(1)}, bf16[1,4,264,128]{3,2,1,0:T(8,128)(2,1)S(1)}, u32[]{:S(2)}, u32[]{:S(2)}) collective-permute-start(bf16[1,4,264,128]{3,2,1,0:T(8,128)(2,1)S(1)} %pad_maximum_fusion.14), channel_id=1, source_target_pairs={{3,0},{7,4},{11,8},{15,12},{19,16},{23,20},{27,24},{31,28}} | collective-permute-start | bytes 811016 | tf_op jit(solution)/shard_map/ppermute | solution.py:426
  333.8 118.3 %all-reduce.6.cloned.1.call-start = ((), (), s32[]{:S(2)}) async-start(), calls=%async_computation.4 | async-start | bytes 2883584 | tf_op jit(solution)/shard_map/psum | solution.py:726
  352.7 20.3 %collective-permute-start.20 = (bf16[256,1536]{1,0:T(8,128)(2,1)S(1)}, bf16[256,1536]{1,0:T(8,128)(2,1)S(1)}, u32[]{:S(2)}, u32[]{:S(2)}) collective-permute-start(bf16[256,1536]{1,0:T(8,128)(2,1)S(1)} %get-tuple-element.87), channel_id=1, source_target_pairs={{0,1},{1,0},{2,3},{3,2},{4,5},{5,4},{6,7},{7,6},{8,9},{9,8},{10,11... | collective-permute-start | bytes 2359304 | tf_op jit(solution)/shard_map/ppermute | solution.py:528
  360.0 77.7 %collective-permute-start.29 = (bf16[704,512]{1,0:T(8,128)(2,1)}, bf16[704,512]{1,0:T(8,128)(2,1)}, u32[]{:S(2)}, u32[]{:S(2)}) collective-permute-start(bf16[704,512]{1,0:T(8,128)(2,1)} %get-tuple-element.88), channel_id=1, source_target_pairs={{0,1},{1,0},{2,3},{3,2},{4,5},{5,4},{6,7},{7,6},{8,9},{9,8},{10,11... | collective-permute-start | bytes 2162696 | tf_op jit(solution)/shard_map/ppermute | solution.py:528
  360.5 76.8 %collective-permute-start.31 = (bf16[704,512]{1,0:T(8,128)(2,1)}, bf16[704,512]{1,0:T(8,128)(2,1)}, u32[]{:S(2)}, u32[]{:S(2)}) collective-permute-start(bf16[704,512]{1,0:T(8,128)(2,1)} %get-tuple-element.89), channel_id=1, source_target_pairs={{0,3},{1,2},{2,1},{3,0},{4,7},{5,6},{6,5},{7,4},{8,11},{9,10},{10,... | collective-permute-start | bytes 2162696 | tf_op jit(solution)/shard_map/ppermute | solution.py:528
  360.5 77.2 %collective-permute-start.30 = (bf16[704,512]{1,0:T(8,128)(2,1)}, bf16[704,512]{1,0:T(8,128)(2,1)}, u32[]{:S(2)}, u32[]{:S(2)}) collective-permute-start(bf16[704,512]{1,0:T(8,128)(2,1)} %get-tuple-element.90), channel_id=1, source_target_pairs={{0,2},{1,3},{2,0},{3,1},{4,6},{5,7},{6,4},{7,5},{8,10},{9,11},{10,... | collective-permute-start | bytes 2162696 | tf_op jit(solution)/shard_map/ppermute | solution.py:528
  363.5 168.9 %all-reduce.8.cloned.1.call-start = ((), (), s32[]{:S(2)}) async-start(), calls=%async_computation.5 | async-start | bytes 3571712 | tf_op jit(solution)/shard_map/psum | solution.py:728
  363.8 65.4 %collective-permute-start.25 = (bf16[256,1536]{1,0:T(8,128)(2,1)}, bf16[256,1536]{1,0:T(8,128)(2,1)}, u32[]{:S(2)}, u32[]{:S(2)}) collective-permute-start(bf16[256,1536]{1,0:T(8,128)(2,1)} %get-tuple-element.85), channel_id=1, source_target_pairs={{0,2},{1,3},{2,0},{3,1},{4,6},{5,7},{6,4},{7,5},{8,10},{9,11},{10,... | collective-permute-start | bytes 2359304 | tf_op jit(solution)/shard_map/ppermute | solution.py:528
  373.0 56.7 %collective-permute-start.26 = (bf16[256,1536]{1,0:T(8,128)(2,1)}, bf16[256,1536]{1,0:T(8,128)(2,1)}, u32[]{:S(2)}, u32[]{:S(2)}) collective-permute-start(bf16[256,1536]{1,0:T(8,128)(2,1)} %get-tuple-element.86), channel_id=1, source_target_pairs={{0,3},{1,2},{2,1},{3,0},{4,7},{5,6},{6,5},{7,4},{8,11},{9,10},{10,... | collective-permute-start | bytes 2359304 | tf_op jit(solution)/shard_map/ppermute | solution.py:528
  (119 other events, 779.5 us)
Sparse Core Ops, SparseCore 0:
  16.6 56.2 all-gather.2
  75.3 94.9 all-gather.4
  221.9 85.2 reduce-scatter.1
  363.6 63.2 all-reduce.5
  455.1 77.1 all-reduce.7
